TPU v7x, 256 devices: a whole 4x4x8 slice. The times are simulated.
256 devices in a mesh: seq: 32 (over x, y, core), head: 8 (over z).
Axes of the slice: x: 4, y: 4, z: 8, core: 2. Of those that a mesh axis runs over, the one named last changes fastest.
Arguments:
- key_rows: bfloat16 [8192, 2048], P('seq', 'head'), may hold values from -1 to 1, as said below
- values: bfloat16 [8192, 2048], P('seq', 'head'), may hold values from -6 to 6
- d_layer: bfloat16 [8192, 2048], P('seq', 'head'), may hold values from -6 to 6
- out_weight: bfloat16 [2048, 2048], P('head'), may hold values from -0.125 to 0.125
- saved_solutions: float32 [8192, 2048], P('seq', 'head'), may hold values from -0.3125 to 0.3125
- ridge_scale: float32 [16], P('head'), may hold values from 0.5 to 4
Outputs:
- grad_queries: float32 [8192, 2048], P('seq', 'head')
- grad_keys: float32 [8192, 2048], P('seq', 'head')
- grad_values: float32 [8192, 2048], P('seq', 'head')
Inputs may be any that keep to these rules, and one draw needn't show every extreme that they name: `key_rows`: within each head the 128 entries of a key have Euclidean norm 1 up to bfloat16 rounding.
All inputs are finite; a program needn't handle non-finite values.
Results may differ from a plain program's by a relative error of at most 0.0029.
Values may be sent and summed in bfloat16 or wider, within the bound.
No kernel may reach another device: no remote copies, remote signals or barrier semaphores. Data moves between devices by JAX's collectives and lax.ppermute only.
A program may use at most 64 MiB of HBM per device.

v0:
```python
import jax
import jax.numpy as jnp
from jax import lax
from jax.sharding import PartitionSpec as P

DH = 128
ITERS = 8


HIGHEST_PRECISION = lax.Precision.HIGHEST
EPSILON = 1e-06


def joined_along(blocks, dim):
    dims = list(blocks.shape[1:])
    dims[dim] *= blocks.shape[0]
    return jnp.moveaxis(blocks, 0, dim).reshape(dims)


def sent_to_all(value, axis):
    copies = jnp.broadcast_to(value, (lax.axis_size(axis), *value.shape))
    return lax.all_to_all(copies, axis, split_axis=0, concat_axis=0, tiled=True)


def gather_directly(value, axis, dim):
    return joined_along(sent_to_all(value, axis), dim)


def from_behind(block, axis, distance):
    devices = range(lax.axis_size(axis))
    route = [(i - distance, i) for i in devices if i - distance in devices]
    return lax.ppermute(block, axis, route)


def to_blocks(flat, block_len):
    tok_rows = flat.shape[0]
    head_count = flat.shape[1] // DH
    return flat.reshape(tok_rows // block_len, block_len, head_count, DH).transpose(2, 0, 1, 3)


def to_flat(blocked):
    head_count, block_count, block_len, width = blocked.shape
    return blocked.transpose(1, 2, 0, 3).reshape(block_count * block_len, head_count * width)


def make_lower(block_len):
    row_ids = lax.broadcasted_iota(jnp.int32, (block_len, block_len), 0)
    col_ids = lax.broadcasted_iota(jnp.int32, (block_len, block_len), 1)
    return (row_ids >= col_ids).astype(jnp.float32)


def masked_apply(left, right, carried, mask_table):
    scores = jnp.einsum("hbid,hbjd->hbij", left, right, precision=HIGHEST_PRECISION) * mask_table
    return jnp.einsum("hbij,hbjd->hbid", scores, carried, precision=HIGHEST_PRECISION)


def outer_sums(left, right):
    return jnp.einsum("hbid,hbie->hbde", left, right, precision=HIGHEST_PRECISION)


def exclusive_prefix(per_block):
    return jnp.cumsum(per_block, axis=1) - per_block


def exclusive_suffix(per_block):
    return jnp.flip(jnp.cumsum(jnp.flip(per_block, 1), axis=1), 1) - per_block


def add_pair(earlier, later):
    return (earlier[0] + later[0], earlier[1] + later[1])


def apply_states(key_blk, val_blk, pair_state, cross_state):
    sym_state = pair_state + jnp.swapaxes(pair_state, 1, 2)
    grad_k = -jnp.einsum("hbid,hde->hbie", key_blk, sym_state, precision=HIGHEST_PRECISION)
    grad_k = grad_k + jnp.einsum(
        "hbif,hef->hbie", val_blk, cross_state, precision=HIGHEST_PRECISION
    )
    grad_v = jnp.einsum("hbid,hdf->hbif", key_blk, cross_state, precision=HIGHEST_PRECISION)
    return (grad_k, grad_v)


def within_later(key_blk, val_blk, sol_blk, sav_blk, out_blk, upper_table):
    pair_after = exclusive_suffix(outer_sums(sol_blk, sav_blk))
    sym_after = pair_after + jnp.swapaxes(pair_after, 2, 3)
    cross_after = exclusive_suffix(outer_sums(sav_blk, out_blk))
    grad_k = -jnp.einsum("hbid,hbde->hbie", key_blk, sym_after, precision=HIGHEST_PRECISION)
    grad_k = grad_k + jnp.einsum(
        "hbif,hbef->hbie", val_blk, cross_after, precision=HIGHEST_PRECISION
    )
    grad_k = grad_k - masked_apply(key_blk, sav_blk, sol_blk, upper_table)
    grad_k = grad_k - masked_apply(key_blk, sol_blk, sav_blk, upper_table)
    grad_k = grad_k + masked_apply(val_blk, out_blk, sav_blk, upper_table)
    grad_v = jnp.einsum("hbid,hbdf->hbif", key_blk, cross_after, precision=HIGHEST_PRECISION)
    grad_v = grad_v + masked_apply(key_blk, sav_blk, out_blk, upper_table)
    return (grad_k, grad_v)


def body(key_rows, values, d_layer, out_weight, saved_solutions, ridge_scale):
    tok_rows = key_rows.shape[0]
    block_len = min(512, tok_rows)
    span_devs = lax.axis_size("seq") // 4
    lower_table = make_lower(block_len)
    upper_table = lower_table.T
    d_heads = jnp.einsum(
        "tf,cf->tc",
        gather_directly(d_layer, "head", 1),
        out_weight,
        preferred_element_type=jnp.float32,
    ).astype(jnp.bfloat16)
    keys_back, values_back = from_behind((key_rows, values), "seq", span_devs)
    key_blk = to_blocks(key_rows.astype(jnp.float32), block_len)
    val_blk = to_blocks(values.astype(jnp.float32), block_len)
    key_lag = to_blocks(keys_back.astype(jnp.float32), block_len)
    val_lag = to_blocks(values_back.astype(jnp.float32), block_len)
    out_flat = d_heads.astype(jnp.float32)
    out_blk = to_blocks(out_flat, block_len)
    sav_blk = to_blocks(saved_solutions, block_len)
    gram_own = outer_sums(key_blk, key_blk)
    state_own = outer_sums(val_blk, key_blk)
    gram_lag = outer_sums(key_lag, key_lag)
    state_lag = outer_sums(val_lag, key_lag)
    totals = (jnp.sum(gram_own, axis=1), jnp.sum(state_own, axis=1))
    distances = [1] + [1 << level_idx for level_idx in range(span_devs.bit_length() - 1)]
    source = totals
    for number, distance in enumerate(distances):
        arrived = from_behind((source[0], source[1]), "seq", distance)
        source = arrived if number == 0 else add_pair(source, arrived)
    window_base = source
    gram_base = window_base[0][:, None] + exclusive_prefix(gram_own) - exclusive_prefix(gram_lag)
    state_base = window_base[1][:, None] + exclusive_prefix(state_own) - exclusive_prefix(state_lag)
    ridge_term = ridge_scale[:, None, None, None]
    adjoint_rhs = jnp.einsum("hbif,hbfe->hbie", out_blk, state_base, precision=HIGHEST_PRECISION)
    adjoint_rhs = adjoint_rhs + masked_apply(out_blk, val_blk, key_blk, lower_table)
    adjoint_rhs = adjoint_rhs - masked_apply(out_blk, val_lag, key_lag, lower_table)
    solution = jnp.zeros_like(adjoint_rhs)
    residual_now = adjoint_rhs
    direction = adjoint_rhs
    norm_now = jnp.sum(residual_now * residual_now, axis=-1, keepdims=True)
    for iteration in range(ITERS):
        result = jnp.einsum("hbid,hbde->hbie", direction, gram_base, precision=HIGHEST_PRECISION)
        result = result + masked_apply(direction, key_blk, key_blk, lower_table)
        result = result - masked_apply(direction, key_lag, key_lag, lower_table)
        image = result + ridge_term * direction
        alpha = norm_now / (jnp.sum(direction * image, axis=-1, keepdims=True) + EPSILON)
        solution = solution + alpha * direction
        residual_now = residual_now - alpha * image
        norm_next = jnp.sum(residual_now * residual_now, axis=-1, keepdims=True)
        direction = residual_now + norm_next / (norm_now + EPSILON) * direction
        norm_now = norm_next
    later_totals = (
        jnp.sum(outer_sums(solution, sav_blk), axis=1),
        jnp.sum(outer_sums(sav_blk, out_blk), axis=1),
    )
    distances = [1] + [1 << level_idx for level_idx in range(span_devs.bit_length() - 1)]
    source = later_totals
    for number, distance in enumerate(distances):
        arrived = from_behind((source[0], source[1]), "seq", -distance)
        source = arrived if number == 0 else add_pair(source, arrived)
    grad_k, grad_v = apply_states(key_blk, val_blk, source[0], source[1])
    own_k, own_v = within_later(key_blk, val_blk, solution, sav_blk, out_blk, upper_table)
    grad_k = grad_k + own_k
    grad_v = grad_v + own_v
    early_k, early_v = within_later(key_lag, val_lag, solution, sav_blk, out_blk, upper_table)
    early_k = -early_k
    early_v = -early_v
    flat_k, flat_v = from_behind((to_flat(early_k), to_flat(early_v)), "seq", -span_devs)
    extra_k = to_blocks(flat_k, block_len)
    extra_v = to_blocks(flat_v, block_len)
    grad_k = grad_k + extra_k
    grad_v = grad_v + extra_v
    return (to_flat(solution), to_flat(grad_k), to_flat(grad_v))


def solution(mesh):
    return jax.shard_map(
        body,
        mesh=mesh,
        in_specs=(
            P("seq", "head"),
            P("seq", "head"),
            P("seq", "head"),
            P("head", None),
            P("seq", "head"),
            P("head"),
        ),
        out_specs=(P("seq", "head"), P("seq", "head"), P("seq", "head")),
        check_vma=False,
    )
```

profile of v0, /device:TPU:59, one launch (start us, length us, event | category | flops | bytes accessed | tf_op | source)
XLA Modules:
  0.0 140.4 jit_solution(9731894360038953585)
XLA Ops:
  2.8 8.1 %all-to-all-start = ((bf16[8,256,256]{1,2,0:T(8,128)(2,1)}), bf16[8,256,256]{1,2,0:T(8,128)(2,1)}, u32[]{:S(2)}, u32[]{:S(2)}) async-start(bf16[8,256,256]{1,2,0:T(8,128)(2,1)} %broadcast_in_dim.2), calls=%async_computation | async-start | bytes 2097152 | tf_op jit(solution)/shard_map/all_to_all | solution.py:22
  11.0 3.1 %collective-permute-start.5 = (bf16[256,256]{1,0:T(8,128)(2,1)S(1)}, bf16[256,256]{1,0:T(8,128)(2,1)S(1)}, u32[]{:S(2)}, u32[]{:S(2)}) collective-permute-start(bf16[256,256]{1,0:T(8,128)(2,1)S(1)} %copy-done.16), channel_id=1, source_target_pairs={{0,64},{8,72},{16,80},{24,88},{32,96},{40,104},{48,112},{56,120},{... | collective-permute-start | bytes 393224 | tf_op jit(solution)/shard_map/ppermute | solution.py:32
  14.4 3.9 %collective-permute-start.6 = (f32[2,128,128]{2,1,0:T(8,128)S(1)}, f32[2,128,128]{2,1,0:T(8,128)S(1)}, u32[]{:S(2)}, u32[]{:S(2)}) collective-permute-start(f32[2,128,128]{2,1,0:T(8,128)S(1)} %fusion.82), channel_id=1, source_target_pairs={{0,8},{8,16},{16,24},{24,32},{32,40},{40,48},{48,56},{56,64},{64,7... | collective-permute-start | bytes 393224 | tf_op jit(solution)/shard_map/ppermute | solution.py:32
  18.6 1.9 %collective-permute-start = (f32[2,128,128]{2,1,0:T(8,128)S(1)}, f32[2,128,128]{2,1,0:T(8,128)S(1)}, u32[]{:S(2)}, u32[]{:S(2)}) collective-permute-start(f32[2,128,128]{2,1,0:T(8,128)S(1)} %fusion.85), channel_id=1, source_target_pairs={{0,8},{8,16},{16,24},{24,32},{32,40},{40,48},{48,56},{56,64},{64,7... | collective-permute-start | bytes 393224 | tf_op jit(solution)/shard_map/ppermute | solution.py:32
  20.6 1.9 %collective-permute-start.4 = (bf16[256,256]{0,1:T(8,128)(2,1)S(1)}, bf16[256,256]{0,1:T(8,128)(2,1)S(1)}, u32[]{:S(2)}, u32[]{:S(2)}) collective-permute-start(bf16[256,256]{0,1:T(8,128)(2,1)S(1)} %copy.77), channel_id=1, source_target_pairs={{0,64},{8,72},{16,80},{24,88},{32,96},{40,104},{48,112},{56,120},{... | collective-permute-start | bytes 393224 | tf_op jit(solution)/shard_map/ppermute | solution.py:32
  22.7 3.9 %collective-permute-start.7 = (f32[2,128,128]{2,1,0:T(8,128)S(1)}, f32[2,128,128]{2,1,0:T(8,128)S(1)}, u32[]{:S(2)}, u32[]{:S(2)}) collective-permute-start(f32[2,128,128]{2,1,0:T(8,128)S(1)} %collective-permute-done.6), channel_id=1, source_target_pairs={{0,8},{8,16},{16,24},{24,32},{32,40},{40,48},{48,56},{56,64},{64,7... | collective-permute-start | bytes 393224 | tf_op jit(solution)/shard_map/ppermute | solution.py:32
  28.0 3.6 %collective-permute-start.1 = (f32[2,128,128]{2,1,0:T(8,128)S(1)}, f32[2,128,128]{2,1,0:T(8,128)}, u32[]{:S(2)}, u32[]{:S(2)}) collective-permute-start(f32[2,128,128]{2,1,0:T(8,128)S(1)} %collective-permute-done), channel_id=1, source_target_pairs={{0,8},{8,16},{16,24},{24,32},{32,40},{40,48},{48,56},{56,64},{64,7... | collective-permute-start | bytes 393224 | tf_op jit(solution)/shard_map/ppermute | solution.py:32
  31.8 3.2 %collective-permute-start.8 = (f32[2,128,128]{2,1,0:T(8,128)S(1)}, f32[2,128,128]{2,1,0:T(8,128)S(1)}, u32[]{:S(2)}, u32[]{:S(2)}) collective-permute-start(f32[2,128,128]{2,1,0:T(8,128)S(1)} %add.369), channel_id=1, source_target_pairs={{0,16},{8,24},{16,32},{24,40},{32,48},{40,56},{48,64},{56,72},{64,... | collective-permute-start | bytes 393224 | tf_op jit(solution)/shard_map/ppermute | solution.py:32
  36.4 2.9 %collective-permute-start.2 = (f32[2,128,128]{2,1,0:T(8,128)S(1)}, f32[2,128,128]{2,1,0:T(8,128)S(1)}, u32[]{:S(2)}, u32[]{:S(2)}) collective-permute-start(f32[2,128,128]{2,1,0:T(8,128)S(1)} %add.364), channel_id=1, source_target_pairs={{0,16},{8,24},{16,32},{24,40},{32,48},{40,56},{48,64},{56,72},{64,... | collective-permute-start | bytes 393224 | tf_op jit(solution)/shard_map/ppermute | solution.py:32
  39.3 3.5 %collective-permute-start.9 = (f32[2,128,128]{2,1,0:T(8,128)S(1)}, f32[2,128,128]{2,1,0:T(8,128)S(1)}, u32[]{:S(2)}, u32[]{:S(2)}) collective-permute-start(f32[2,128,128]{2,1,0:T(8,128)S(1)} %add.370), channel_id=1, source_target_pairs={{0,32},{8,40},{16,48},{24,56},{32,64},{40,72},{48,80},{56,88},{64,... | collective-permute-start | bytes 393224 | tf_op jit(solution)/shard_map/ppermute | solution.py:32
  44.4 3.2 %collective-permute-start.3 = (f32[2,128,128]{2,1,0:T(8,128)}, f32[2,128,128]{2,1,0:T(8,128)}, u32[]{:S(2)}, u32[]{:S(2)}) collective-permute-start(f32[2,128,128]{2,1,0:T(8,128)} %add.365), channel_id=1, source_target_pairs={{0,32},{8,40},{16,48},{24,56},{32,64},{40,72},{48,80},{56,88},{64,... | collective-permute-start | bytes 393224 | tf_op jit(solution)/shard_map/ppermute | solution.py:32
  47.8 1.7 %convolution_convert_fusion = bf16[256,256]{0,1:T(8,128)(2,1)S(1)} fusion(bf16[256,2048]{1,0:T(8,128)(2,1)S(1)} %copy-done, bf16[256,2048]{0,1:T(8,128)(2,1)} %bitcast.1), kind=kOutput, calls=%fused_computation.79 | convolution fusion | flops 268500992 | bytes 2228224 | tf_op jit(solution)/shard_map/tf,cf->tc/dot_general | solution.py:105
  52.4 1.3 fusion.12
  74.2 4.4 %collective-permute-start.10 = (f32[2,128,128]{2,1,0:T(8,128)}, f32[2,128,128]{2,1,0:T(8,128)}, u32[]{:S(2)}, u32[]{:S(2)}) collective-permute-start(f32[2,128,128]{2,1,0:T(8,128)} %fusion.140), channel_id=1, source_target_pairs={{8,0},{16,8},{24,16},{32,24},{40,32},{48,40},{56,48},{64,56},{72,6... | collective-permute-start | bytes 393224 | tf_op jit(solution)/shard_map/ppermute | solution.py:32
  78.6 1.6 %subtract_bitcast_fusion = f32[2,1,128,128]{3,2,0,1:T(8,128)} fusion(f32[2,128,128]{2,1,0:T(8,128)} %fusion.140), kind=kLoop, calls=%fused_computation.176 | loop fusion | flops 32768 | bytes 262144 | tf_op jit(solution)/shard_map/sub | solution.py:66
  80.5 1.2 fusion
  84.0 1.9 %collective-permute-start.14 = (f32[2,128,128]{1,2,0:T(8,128)S(1)}, f32[2,128,128]{1,2,0:T(8,128)}, u32[]{:S(2)}, u32[]{:S(2)}) collective-permute-start(f32[2,128,128]{1,2,0:T(8,128)S(1)} %convolution_bitcast_fusion.5), channel_id=1, source_target_pairs={{8,0},{16,8},{24,16},{32,24},{40,32},{48,40},{56,48},{64,56},{72,6... | collective-permute-start | bytes 393224 | tf_op jit(solution)/shard_map/ppermute | solution.py:32
  85.9 1.7 %copy.117 = f32[2,1,128,128]{2,3,0,1:T(8,128)} copy(f32[2,1,128,128]{3,2,0,1:T(8,128)} %subtract_bitcast_fusion) | data formatting | bytes 262144 | tf_op jit(solution)/shard_map/sub | solution.py:66
  87.6 1.3 convolution_negate_fusion.1
  93.2 1.2 fusion.27
  97.1 3.4 %collective-permute-start.18 = (f32[256,256]{0,1:T(8,128)}, f32[256,256]{0,1:T(8,128)}, u32[]{:S(2)}, u32[]{:S(2)}) collective-permute-start(f32[256,256]{0,1:T(8,128)} %bitcast.67), channel_id=1, source_target_pairs={{64,0},{72,8},{80,16},{88,24},{96,32},{104,40},{112,48},{120,56},{... | collective-permute-start | bytes 786440 | tf_op jit(solution)/shard_map/ppermute | solution.py:32
  100.8 3.2 %collective-permute-start.15 = (f32[2,128,128]{1,2,0:T(8,128)}, f32[2,128,128]{1,2,0:T(8,128)S(1)}, u32[]{:S(2)}, u32[]{:S(2)}) collective-permute-start(f32[2,128,128]{1,2,0:T(8,128)} %collective-permute-done.14), channel_id=1, source_target_pairs={{8,0},{16,8},{24,16},{32,24},{40,32},{48,40},{56,48},{64,56},{72,6... | collective-permute-start | bytes 393224 | tf_op jit(solution)/shard_map/ppermute | solution.py:32
  104.4 1.9 %collective-permute-start.11 = (f32[2,128,128]{2,1,0:T(8,128)}, f32[2,128,128]{2,1,0:T(8,128)S(1)}, u32[]{:S(2)}, u32[]{:S(2)}) collective-permute-start(f32[2,128,128]{2,1,0:T(8,128)} %collective-permute-done.10), channel_id=1, source_target_pairs={{8,0},{16,8},{24,16},{32,24},{40,32},{48,40},{56,48},{64,56},{72,6... | collective-permute-start | bytes 393224 | tf_op jit(solution)/shard_map/ppermute | solution.py:32
  106.3 5.1 %collective-permute-done.15 = f32[2,128,128]{1,2,0:T(8,128)S(1)} collective-permute-done((f32[2,128,128]{1,2,0:T(8,128)}, f32[2,128,128]{1,2,0:T(8,128)S(1)}, u32[]{:S(2)}, u32[]{:S(2)}) %collective-permute-start.15) | collective-permute-done | bytes 131104 | tf_op jit(solution)/shard_map/ppermute | solution.py:32
  112.3 1.9 %collective-permute-start.16 = (f32[2,128,128]{1,2,0:T(8,128)S(1)}, f32[2,128,128]{1,2,0:T(8,128)S(1)}, u32[]{:S(2)}, u32[]{:S(2)}) collective-permute-start(f32[2,128,128]{1,2,0:T(8,128)S(1)} %add.423), channel_id=1, source_target_pairs={{16,0},{24,8},{32,16},{40,24},{48,32},{56,40},{64,48},{72,56},{80,... | collective-permute-start | bytes 393224 | tf_op jit(solution)/shard_map/ppermute | solution.py:32
  115.5 1.9 %collective-permute-start.12 = (f32[2,128,128]{2,1,0:T(8,128)S(1)}, f32[2,128,128]{2,1,0:T(8,128)S(1)}, u32[]{:S(2)}, u32[]{:S(2)}) collective-permute-start(f32[2,128,128]{2,1,0:T(8,128)S(1)} %add.419), channel_id=1, source_target_pairs={{16,0},{24,8},{32,16},{40,24},{48,32},{56,40},{64,48},{72,56},{80,... | collective-permute-start | bytes 393224 | tf_op jit(solution)/shard_map/ppermute | solution.py:32
  117.4 3.5 %collective-permute-done.16 = f32[2,128,128]{1,2,0:T(8,128)S(1)} collective-permute-done((f32[2,128,128]{1,2,0:T(8,128)S(1)}, f32[2,128,128]{1,2,0:T(8,128)S(1)}, u32[]{:S(2)}, u32[]{:S(2)}) %collective-permute-start.16) | collective-permute-done | bytes 131104 | tf_op jit(solution)/shard_map/ppermute | solution.py:32
  121.0 2.0 %collective-permute-start.17 = (f32[2,128,128]{1,2,0:T(8,128)S(1)}, f32[2,128,128]{1,2,0:T(8,128)S(1)}, u32[]{:S(2)}, u32[]{:S(2)}) collective-permute-start(f32[2,128,128]{1,2,0:T(8,128)S(1)} %add.424), channel_id=1, source_target_pairs={{32,0},{40,8},{48,16},{56,24},{64,32},{72,40},{80,48},{88,56},{96,... | collective-permute-start | bytes 393224 | tf_op jit(solution)/shard_map/ppermute | solution.py:32
  123.2 2.7 %collective-permute-start.19 = (f32[256,256]{0,1:T(8,128)S(1)}, f32[256,256]{0,1:T(8,128)S(1)}, u32[]{:S(2)}, u32[]{:S(2)}) collective-permute-start(f32[256,256]{0,1:T(8,128)S(1)} %bitcast.356), channel_id=1, source_target_pairs={{64,0},{72,8},{80,16},{88,24},{96,32},{104,40},{112,48},{120,56},{... | collective-permute-start | bytes 786440 | tf_op jit(solution)/shard_map/ppermute | solution.py:32
  126.7 4.6 %collective-permute-start.13 = (f32[2,128,128]{2,1,0:T(8,128)S(1)}, f32[2,128,128]{2,1,0:T(8,128)S(1)}, u32[]{:S(2)}, u32[]{:S(2)}) collective-permute-start(f32[2,128,128]{2,1,0:T(8,128)S(1)} %add.420), channel_id=1, source_target_pairs={{32,0},{40,8},{48,16},{56,24},{64,32},{72,40},{80,48},{88,56},{96,... | collective-permute-start | bytes 393224 | tf_op jit(solution)/shard_map/ppermute | solution.py:32
  131.7 5.3 %collective-permute-done.13 = f32[2,128,128]{2,1,0:T(8,128)S(1)} collective-permute-done((f32[2,128,128]{2,1,0:T(8,128)S(1)}, f32[2,128,128]{2,1,0:T(8,128)S(1)}, u32[]{:S(2)}, u32[]{:S(2)}) %collective-permute-start.13) | collective-permute-done | bytes 131104 | tf_op jit(solution)/shard_map/ppermute | solution.py:32
  137.1 1.3 fusion.32
  (174 shorter events, 46.4 us)
Async XLA Ops:
  0.6 47.2 %copy-start = (bf16[256,2048]{1,0:T(8,128)(2,1)S(1)}, bf16[256,2048]{1,0:T(8,128)(2,1)}, u32[]{:S(2)}) copy-start(bf16[256,2048]{1,0:T(8,128)(2,1)} %param.9) | copy-start | bytes 3145732
  2.8 8.1 %copy-start.16 = (bf16[256,256]{1,0:T(8,128)(2,1)S(1)}, bf16[256,256]{1,0:T(8,128)(2,1)}, u32[]{:S(2)}) copy-start(bf16[256,256]{1,0:T(8,128)(2,1)} %param.6) | copy-start | bytes 393220
  2.8 45.0 %all-to-all-start = ((bf16[8,256,256]{1,2,0:T(8,128)(2,1)}), bf16[8,256,256]{1,2,0:T(8,128)(2,1)}, u32[]{:S(2)}, u32[]{:S(2)}) async-start(bf16[8,256,256]{1,2,0:T(8,128)(2,1)} %broadcast_in_dim.2), calls=%async_computation | async-start | bytes 2097152 | tf_op jit(solution)/shard_map/all_to_all | solution.py:22
  11.0 20.7 %collective-permute-start.5 = (bf16[256,256]{1,0:T(8,128)(2,1)S(1)}, bf16[256,256]{1,0:T(8,128)(2,1)S(1)}, u32[]{:S(2)}, u32[]{:S(2)}) collective-permute-start(bf16[256,256]{1,0:T(8,128)(2,1)S(1)} %copy-done.16), channel_id=1, source_target_pairs={{0,64},{8,72},{16,80},{24,88},{32,96},{40,104},{48,112},{56,120},{... | collective-permute-start | bytes 393224 | tf_op jit(solution)/shard_map/ppermute | solution.py:32
  14.1 4.1 %copy-start.11 = (bf16[256,256]{1,0:T(8,128)(2,1)S(1)}, bf16[256,256]{1,0:T(8,128)(2,1)}, u32[]{:S(2)}) copy-start(bf16[256,256]{1,0:T(8,128)(2,1)} %param.7) | copy-start | bytes 393220
  14.4 8.3 %collective-permute-start.6 = (f32[2,128,128]{2,1,0:T(8,128)S(1)}, f32[2,128,128]{2,1,0:T(8,128)S(1)}, u32[]{:S(2)}, u32[]{:S(2)}) collective-permute-start(f32[2,128,128]{2,1,0:T(8,128)S(1)} %fusion.82), channel_id=1, source_target_pairs={{0,8},{8,16},{16,24},{24,32},{32,40},{40,48},{48,56},{56,64},{64,7... | collective-permute-start | bytes 393224 | tf_op jit(solution)/shard_map/ppermute | solution.py:32
  18.3 4.2 %copy-start.15 = (f32[256,256]{1,0:T(8,128)S(1)}, f32[256,256]{1,0:T(8,128)}, u32[]{:S(2)}) copy-start(f32[256,256]{1,0:T(8,128)} %param.10) | copy-start | bytes 786436
  18.5 2.0 %copy-start.12 = (f32[2,128,128]{2,1,0:T(8,128)}, f32[2,128,128]{2,1,0:T(8,128)S(1)}, u32[]{:S(2)}) copy-start(f32[2,128,128]{2,1,0:T(8,128)S(1)} %fusion.85) | copy-start | bytes 393220
  18.6 9.5 %collective-permute-start = (f32[2,128,128]{2,1,0:T(8,128)S(1)}, f32[2,128,128]{2,1,0:T(8,128)S(1)}, u32[]{:S(2)}, u32[]{:S(2)}) collective-permute-start(f32[2,128,128]{2,1,0:T(8,128)S(1)} %fusion.85), channel_id=1, source_target_pairs={{0,8},{8,16},{16,24},{24,32},{32,40},{40,48},{48,56},{56,64},{64,7... | collective-permute-start | bytes 393224 | tf_op jit(solution)/shard_map/ppermute | solution.py:32
  20.6 7.3 %collective-permute-start.4 = (bf16[256,256]{0,1:T(8,128)(2,1)S(1)}, bf16[256,256]{0,1:T(8,128)(2,1)S(1)}, u32[]{:S(2)}, u32[]{:S(2)}) collective-permute-start(bf16[256,256]{0,1:T(8,128)(2,1)S(1)} %copy.77), channel_id=1, source_target_pairs={{0,64},{8,72},{16,80},{24,88},{32,96},{40,104},{48,112},{56,120},{... | collective-permute-start | bytes 393224 | tf_op jit(solution)/shard_map/ppermute | solution.py:32
  22.7 9.1 %collective-permute-start.7 = (f32[2,128,128]{2,1,0:T(8,128)S(1)}, f32[2,128,128]{2,1,0:T(8,128)S(1)}, u32[]{:S(2)}, u32[]{:S(2)}) collective-permute-start(f32[2,128,128]{2,1,0:T(8,128)S(1)} %collective-permute-done.6), channel_id=1, source_target_pairs={{0,8},{8,16},{16,24},{24,32},{32,40},{40,48},{48,56},{56,64},{64,7... | collective-permute-start | bytes 393224 | tf_op jit(solution)/shard_map/ppermute | solution.py:32
  28.0 14.9 %copy-start.6 = (bf16[1,256,2,128]{3,1,2,0:T(8,128)(2,1)}, bf16[1,256,2,128]{3,1,2,0:T(8,128)(2,1)S(1)}, u32[]{:S(2)}) copy-start(bf16[1,256,2,128]{3,1,2,0:T(8,128)(2,1)S(1)} %copy.78) | copy-start | bytes 393220
  28.0 7.4 %collective-permute-start.1 = (f32[2,128,128]{2,1,0:T(8,128)S(1)}, f32[2,128,128]{2,1,0:T(8,128)}, u32[]{:S(2)}, u32[]{:S(2)}) collective-permute-start(f32[2,128,128]{2,1,0:T(8,128)S(1)} %collective-permute-done), channel_id=1, source_target_pairs={{0,8},{8,16},{16,24},{24,32},{32,40},{40,48},{48,56},{56,64},{64,7... | collective-permute-start | bytes 393224 | tf_op jit(solution)/shard_map/ppermute | solution.py:32
  31.8 7.5 %collective-permute-start.8 = (f32[2,128,128]{2,1,0:T(8,128)S(1)}, f32[2,128,128]{2,1,0:T(8,128)S(1)}, u32[]{:S(2)}, u32[]{:S(2)}) collective-permute-start(f32[2,128,128]{2,1,0:T(8,128)S(1)} %add.369), channel_id=1, source_target_pairs={{0,16},{8,24},{16,32},{24,40},{32,48},{40,56},{48,64},{56,72},{64,... | collective-permute-start | bytes 393224 | tf_op jit(solution)/shard_map/ppermute | solution.py:32
  36.4 7.4 %collective-permute-start.2 = (f32[2,128,128]{2,1,0:T(8,128)S(1)}, f32[2,128,128]{2,1,0:T(8,128)S(1)}, u32[]{:S(2)}, u32[]{:S(2)}) collective-permute-start(f32[2,128,128]{2,1,0:T(8,128)S(1)} %add.364), channel_id=1, source_target_pairs={{0,16},{8,24},{16,32},{24,40},{32,48},{40,56},{48,64},{56,72},{64,... | collective-permute-start | bytes 393224 | tf_op jit(solution)/shard_map/ppermute | solution.py:32
  39.3 8.3 %collective-permute-start.9 = (f32[2,128,128]{2,1,0:T(8,128)S(1)}, f32[2,128,128]{2,1,0:T(8,128)S(1)}, u32[]{:S(2)}, u32[]{:S(2)}) collective-permute-start(f32[2,128,128]{2,1,0:T(8,128)S(1)} %add.370), channel_id=1, source_target_pairs={{0,32},{8,40},{16,48},{24,56},{32,64},{40,72},{48,80},{56,88},{64,... | collective-permute-start | bytes 393224 | tf_op jit(solution)/shard_map/ppermute | solution.py:32
  44.4 8.0 %collective-permute-start.3 = (f32[2,128,128]{2,1,0:T(8,128)}, f32[2,128,128]{2,1,0:T(8,128)}, u32[]{:S(2)}, u32[]{:S(2)}) collective-permute-start(f32[2,128,128]{2,1,0:T(8,128)} %add.365), channel_id=1, source_target_pairs={{0,32},{8,40},{16,48},{24,56},{32,64},{40,72},{48,80},{56,88},{64,... | collective-permute-start | bytes 393224 | tf_op jit(solution)/shard_map/ppermute | solution.py:32
  51.2 1.2 copy-start.13
  51.2 1.2 copy-start.14
  74.2 30.1 %collective-permute-start.10 = (f32[2,128,128]{2,1,0:T(8,128)}, f32[2,128,128]{2,1,0:T(8,128)}, u32[]{:S(2)}, u32[]{:S(2)}) collective-permute-start(f32[2,128,128]{2,1,0:T(8,128)} %fusion.140), channel_id=1, source_target_pairs={{8,0},{16,8},{24,16},{32,24},{40,32},{48,40},{56,48},{64,56},{72,6... | collective-permute-start | bytes 393224 | tf_op jit(solution)/shard_map/ppermute | solution.py:32
  84.0 16.8 %collective-permute-start.14 = (f32[2,128,128]{1,2,0:T(8,128)S(1)}, f32[2,128,128]{1,2,0:T(8,128)}, u32[]{:S(2)}, u32[]{:S(2)}) collective-permute-start(f32[2,128,128]{1,2,0:T(8,128)S(1)} %convolution_bitcast_fusion.5), channel_id=1, source_target_pairs={{8,0},{16,8},{24,16},{32,24},{40,32},{48,40},{56,48},{64,56},{72,6... | collective-permute-start | bytes 393224 | tf_op jit(solution)/shard_map/ppermute | solution.py:32
  92.0 1.2 copy-start.8
  92.0 1.2 copy-start.9
  97.1 40.0 %collective-permute-start.18 = (f32[256,256]{0,1:T(8,128)}, f32[256,256]{0,1:T(8,128)}, u32[]{:S(2)}, u32[]{:S(2)}) collective-permute-start(f32[256,256]{0,1:T(8,128)} %bitcast.67), channel_id=1, source_target_pairs={{64,0},{72,8},{80,16},{88,24},{96,32},{104,40},{112,48},{120,56},{... | collective-permute-start | bytes 786440 | tf_op jit(solution)/shard_map/ppermute | solution.py:32
  100.8 10.6 %collective-permute-start.15 = (f32[2,128,128]{1,2,0:T(8,128)}, f32[2,128,128]{1,2,0:T(8,128)S(1)}, u32[]{:S(2)}, u32[]{:S(2)}) collective-permute-start(f32[2,128,128]{1,2,0:T(8,128)} %collective-permute-done.14), channel_id=1, source_target_pairs={{8,0},{16,8},{24,16},{32,24},{40,32},{48,40},{56,48},{64,56},{72,6... | collective-permute-start | bytes 393224 | tf_op jit(solution)/shard_map/ppermute | solution.py:32
  104.4 10.2 %collective-permute-start.11 = (f32[2,128,128]{2,1,0:T(8,128)}, f32[2,128,128]{2,1,0:T(8,128)S(1)}, u32[]{:S(2)}, u32[]{:S(2)}) collective-permute-start(f32[2,128,128]{2,1,0:T(8,128)} %collective-permute-done.10), channel_id=1, source_target_pairs={{8,0},{16,8},{24,16},{32,24},{40,32},{48,40},{56,48},{64,56},{72,6... | collective-permute-start | bytes 393224 | tf_op jit(solution)/shard_map/ppermute | solution.py:32
  112.3 8.7 %collective-permute-start.16 = (f32[2,128,128]{1,2,0:T(8,128)S(1)}, f32[2,128,128]{1,2,0:T(8,128)S(1)}, u32[]{:S(2)}, u32[]{:S(2)}) collective-permute-start(f32[2,128,128]{1,2,0:T(8,128)S(1)} %add.423), channel_id=1, source_target_pairs={{16,0},{24,8},{32,16},{40,24},{48,32},{56,40},{64,48},{72,56},{80,... | collective-permute-start | bytes 393224 | tf_op jit(solution)/shard_map/ppermute | solution.py:32
  115.5 11.2 %collective-permute-start.12 = (f32[2,128,128]{2,1,0:T(8,128)S(1)}, f32[2,128,128]{2,1,0:T(8,128)S(1)}, u32[]{:S(2)}, u32[]{:S(2)}) collective-permute-start(f32[2,128,128]{2,1,0:T(8,128)S(1)} %add.419), channel_id=1, source_target_pairs={{16,0},{24,8},{32,16},{40,24},{48,32},{56,40},{64,48},{72,56},{80,... | collective-permute-start | bytes 393224 | tf_op jit(solution)/shard_map/ppermute | solution.py:32
  121.0 10.4 %collective-permute-start.17 = (f32[2,128,128]{1,2,0:T(8,128)S(1)}, f32[2,128,128]{1,2,0:T(8,128)S(1)}, u32[]{:S(2)}, u32[]{:S(2)}) collective-permute-start(f32[2,128,128]{1,2,0:T(8,128)S(1)} %add.424), channel_id=1, source_target_pairs={{32,0},{40,8},{48,16},{56,24},{64,32},{72,40},{80,48},{88,56},{96,... | collective-permute-start | bytes 393224 | tf_op jit(solution)/shard_map/ppermute | solution.py:32
  123.2 16.0 %collective-permute-start.19 = (f32[256,256]{0,1:T(8,128)S(1)}, f32[256,256]{0,1:T(8,128)S(1)}, u32[]{:S(2)}, u32[]{:S(2)}) collective-permute-start(f32[256,256]{0,1:T(8,128)S(1)} %bitcast.356), channel_id=1, source_target_pairs={{64,0},{72,8},{80,16},{88,24},{96,32},{104,40},{112,48},{120,56},{... | collective-permute-start | bytes 786440 | tf_op jit(solution)/shard_map/ppermute | solution.py:32
  126.7 10.2 %collective-permute-start.13 = (f32[2,128,128]{2,1,0:T(8,128)S(1)}, f32[2,128,128]{2,1,0:T(8,128)S(1)}, u32[]{:S(2)}, u32[]{:S(2)}) collective-permute-start(f32[2,128,128]{2,1,0:T(8,128)S(1)} %add.420), channel_id=1, source_target_pairs={{32,0},{40,8},{48,16},{56,24},{64,32},{72,40},{80,48},{88,56},{96,... | collective-permute-start | bytes 393224 | tf_op jit(solution)/shard_map/ppermute | solution.py:32
  131.7 5.4 %copy-start.10 = (f32[2,256,128]{1,2,0:T(8,128)S(1)}, f32[2,256,128]{1,2,0:T(8,128)}, u32[]{:S(2)}) copy-start(f32[2,256,128]{1,2,0:T(8,128)} %convolution_add_fusion.2) | copy-start | bytes 786436
  (7 other events, 6.5 us)
where the time goes:
time: 142 us; the launch traced here: 140 us
  starting transfers between devices  67.2 us (47%)
  matrix products  40.3 us (28%)
  waiting for transfers between devices  14.7 us (10%)
  local copies, waits for them, and re-layouts  10.3 us (7%)
  other arithmetic  6.12 us (4%)
  between operations  1.77 us (1%)
    ppermute x20, starting transfers between devices, from_behind(): return lax.ppermute(block, axis, route)  59 us
    ppermute x20, waiting for transfers between devices, from_behind(): return lax.ppermute(block, axis, route)  14.7 us
    dot_general x26, matrix products, masked_apply(): jnp.einsum('hbij,hbjd->hbid', scores, carried, precision=HIGHEST_PRECISION)  12.8 us
    dot_general x22, matrix products, masked_apply(): jnp.einsum('hbid,hbjd->hbij', left, right, precision=HIGHEST_PRECISION)  11.6 us
    all_to_all x1, starting transfers between devices, sent_to_all(): return lax.all_to_all(copies, axis, split_axis=0, concat_axis=0, tiled=True)  8.14 us
    unnamed x41, local copies, waits for them, and re-layouts  7.08 us
    dot_general x8, matrix products, body(): jnp.einsum('hbid,hbde->hbie', direction, gram_base, precision=HIGHEST_PRE...  3.8 us
    add x9, other arithmetic, add_pair(): return (earlier[0] + later[0], earlier[1] + later[1])  3.52 us
  transfers between devices with their start and end apart: 21, of which 4 were waited for; matrix products, arithmetic and copies ran while one was open for 21% of the time, Pallas kernels for 0%

commit v1 on v0

v1 whole, which is shorter than its diff:
```python
import jax
import jax.numpy as jnp
from jax import lax
from jax.experimental import pallas as pl
from jax.experimental.pallas import tpu as pltpu
from jax.sharding import PartitionSpec as P

DH = 128
TOK = 256
NH = 2
ITERS = 8
EPSILON = 1e-06
F32 = jnp.float32
BF16 = jnp.bfloat16
VM = pl.BlockSpec(memory_space=pltpu.VMEM)
SM = pl.BlockSpec(memory_space=pltpu.SMEM)
PARAMS = pltpu.CompilerParams(vmem_limit_bytes=24 * 1024 * 1024)


def mm(a, b):
    return lax.dot_general(a, b, (((1,), (0,)), ((), ())), preferred_element_type=F32)


def mm_nt(a, b):
    return lax.dot_general(a, b, (((1,), (1,)), ((), ())), preferred_element_type=F32)


def mm_tn(a, b):
    return lax.dot_general(a, b, (((0,), (0,)), ((), ())), preferred_element_type=F32)


def split(a):
    hi = a.astype(BF16)
    return hi, (a - hi.astype(F32)).astype(BF16)


def head(ref, h, base=0):
    return ref[:, base + h * DH : base + (h + 1) * DH]


def tri(rows, cols):
    r = lax.broadcasted_iota(jnp.int32, (rows, cols), 0)
    c = lax.broadcasted_iota(jnp.int32, (rows, cols), 1)
    return r, c


def call(kernel, outs, *args, flops=0, smem=()):
    return pl.pallas_call(
        kernel,
        out_shape=[jax.ShapeDtypeStruct(s, d) for s, d in outs],
        in_specs=[SM if i in smem else VM for i in range(len(args))],
        out_specs=[VM] * len(outs),
        compiler_params=PARAMS,
        cost_estimate=pl.CostEstimate(flops=flops, bytes_accessed=1 << 19, transcendentals=0),
    )(*args)


def own_states(k_ref, v_ref, x_ref, t_ref, kv_ref, xb_ref):
    for h in range(NH):
        k = head(k_ref, h)
        t_ref[h] = mm_tn(k, k)
        t_ref[NH + h] = mm_tn(head(v_ref, h), k)
    kv_ref[:, : NH * DH] = k_ref[...]
    kv_ref[:, NH * DH :] = v_ref[...]
    xb_ref[...] = x_ref[...].astype(BF16)


def states_to_send(t_ref, lag_ref, p1_ref, p2_ref, part_ref, send_ref):
    core = lax.rem(lax.axis_index("seq"), 2)
    for h in range(NH):
        k = head(lag_ref, h)
        lag_g = mm_tn(k, k)
        lag_s = mm_tn(head(lag_ref, h, NH * DH), k)
        for at, lag in ((h, lag_g), (NH + h, lag_s)):
            part = p1_ref[at] + p2_ref[at]
            part_ref[at] = part
            send_ref[at] = part + jnp.where(core == 0, t_ref[at], lag)


def adjoints(d_ref, w_ref, kv_ref, lag_ref, x_ref, part_ref, recv_ref, ridge_ref, y_ref, yo_ref, t_ref):
    B = 128
    out = mm_nt(d_ref[0], w_ref[:, :256])
    for z in range(1, 8):
        out = out + mm_nt(d_ref[z], w_ref[:, z * 256 : (z + 1) * 256])
    out = out.astype(BF16)
    yo_ref[:, 256:] = out
    rows, cols = tri(B, B)
    low, up = rows >= cols, rows < cols

    rhs, keys, ps, ridges = [], [], [], []
    for h in range(NH):
        k, v = head(kv_ref, h), head(kv_ref, h, 256)
        kl, vl = head(lag_ref, h), head(lag_ref, h, 256)
        gram = part_ref[h] + recv_ref[h]
        state = part_ref[NH + h] + recv_ref[NH + h]
        o = out[:, h * DH : (h + 1) * DH]
        for b in range(2):
            kb, vb = k[b * B : (b + 1) * B], v[b * B : (b + 1) * B]
            klb, vlb = kl[b * B : (b + 1) * B], vl[b * B : (b + 1) * B]
            ob = o[b * B : (b + 1) * B]
            kf, vf = (kl[B:], vl[B:]) if b == 0 else (k[:B], v[:B])
            g = gram + mm_tn(kf, kf)
            s = state + mm_tn(vf, kf)
            g_hi, g_lo = split(g)
            kbt = kb.astype(F32).T.astype(BF16)
            klbt = klb.astype(F32).T.astype(BF16)
            half = jnp.concatenate([g_hi, kbt, klbt, g_lo], axis=1)
            rhs.append(jnp.concatenate([half, half], axis=0))
            both = jnp.concatenate([kb, klb], axis=0)
            keys.append(jnp.concatenate([both, both], axis=0))
            sc = jnp.concatenate(
                [jnp.where(low, mm_nt(ob, vb), 0.0), jnp.where(up, mm_nt(ob, vlb), 0.0)], axis=1
            )
            sc_hi, sc_lo = split(sc)
            s_hi, s_lo = split(s)
            p = mm(ob, s_hi) + mm(ob, s_lo)
            p = p + mm(jnp.concatenate([sc_hi, sc_lo], axis=1), keys[-1])
            ps.append(p)
            ridges.append(ridge_ref[h])

    n = len(ps)

    def apply_gram(p, i):
        p_hi, p_lo = split(p)
        r = mm(jnp.concatenate([p_hi, p_lo], axis=1), rhs[i])
        sc = jnp.concatenate(
            [jnp.where(low, r[:, B : 2 * B], 0.0), jnp.where(up, r[:, 2 * B : 3 * B], 0.0)], axis=1
        )
        sc_hi, sc_lo = split(sc)
        t = mm(jnp.concatenate([sc_hi, sc_lo], axis=1), keys[i])
        return t + r[:, :B] + r[:, 3 * B :] + ridges[i] * p

    ys = [jnp.zeros((B, DH), F32)] * n
    rs = list(ps)
    rrs = [jnp.sum(r * r, axis=-1, keepdims=True) for r in rs]
    for it in range(ITERS):
        for i in range(n):
            a = apply_gram(ps[i], i)
            alpha = rrs[i] / (jnp.sum(ps[i] * a, axis=-1, keepdims=True) + EPSILON)
            ys[i] = ys[i] + alpha * ps[i]
            if it < ITERS - 1:
                rs[i] = rs[i] - alpha * a
                nr = jnp.sum(rs[i] * rs[i], axis=-1, keepdims=True)
                ps[i] = rs[i] + nr / (rrs[i] + EPSILON) * ps[i]
                rrs[i] = nr

    for h in range(NH):
        y = jnp.concatenate([ys[2 * h], ys[2 * h + 1]], axis=0)
        y_ref[:, h * DH : (h + 1) * DH] = y
        yo_ref[:, h * DH : (h + 1) * DH] = y.astype(BF16)
        y_hi, y_lo = split(y)
        x_hi, x_lo = split(head(x_ref, h))
        o = out[:, h * DH : (h + 1) * DH]
        pair = mm_tn(y_hi, x_hi) + mm_tn(y_lo, x_hi) + mm_tn(y_hi, x_lo)
        t_ref[h] = pair + pair.T
        t_ref[NH + h] = mm_tn(x_hi, o) + mm_tn(x_lo, o)


def near_terms(kv_ref, xb_ref, yo_ref, xl_ref, yol_ref, t_ref, gk_ref, gv_ref, extra_ref):
    core = lax.rem(lax.axis_index("seq"), 2)
    rows, cols = tri(TOK, TOK)
    own_mask, lead_mask = rows <= cols, rows > cols
    for h in range(NH):
        k, v = head(kv_ref, h), head(kv_ref, h, 256)
        x, y, o = head(xb_ref, h), head(yo_ref, h), head(yo_ref, h, 256)
        xl, yl, ol = head(xl_ref, h), head(yol_ref, h), head(yol_ref, h, 256)

        def scores(left, own, lead):
            return jnp.concatenate(
                [jnp.where(own_mask, mm_nt(left, own), 0.0), jnp.where(lead_mask, mm_nt(left, lead), 0.0)], axis=1
            )

        a = scores(k, x, xl).astype(BF16)
        c = (scores(v, o, ol) - scores(k, y, yl)).astype(BF16)
        ys = jnp.concatenate([y, yl], axis=0)
        xs = jnp.concatenate([x, xl], axis=0)
        os = jnp.concatenate([o, ol], axis=0)
        gk_ref[:, h * DH : (h + 1) * DH] = mm(c, xs) - mm(a, ys)
        gv_ref[:, h * DH : (h + 1) * DH] = mm(a, os)
        pair = mm_tn(yl, xl)
        extra_ref[h] = jnp.where(core == 1, t_ref[h], pair + pair.T)
        extra_ref[NH + h] = jnp.where(core == 1, t_ref[NH + h], mm_tn(xl, ol))


def base_terms(kv_ref, part_ref, recv_ref, gk_in, gv_in, gk_ref, gv_ref):
    for h in range(NH):
        k, v = head(kv_ref, h), head(kv_ref, h, 256)
        s_hi, s_lo = split(part_ref[h] + recv_ref[h])
        c_hi, c_lo = split(part_ref[NH + h] + recv_ref[NH + h])
        cols = slice(h * DH, (h + 1) * DH)
        gk_ref[:, cols] = gk_in[:, cols] - mm(k, s_hi) - mm(k, s_lo) + mm_nt(v, c_hi) + mm_nt(v, c_lo)
        gv_ref[:, cols] = gv_in[:, cols] + mm(k, c_hi) + mm(k, c_lo)


def body(key_rows, values, d_layer, out_weight, saved_solutions, ridge_scale):
    n = lax.axis_size("seq")
    lag = n // 4

    def moved(value, source):
        route = [(source(i), i) for i in range(n) if source(i) is not None and 0 <= source(i) < n]
        return lax.ppermute(value, "seq", route)

    def swapped(value):
        return moved(value, lambda i: i ^ 1)

    st = (2 * NH, DH, DH)
    copies = jnp.broadcast_to(d_layer, (8, *d_layer.shape))
    gathered = lax.all_to_all(copies, "head", split_axis=0, concat_axis=0, tiled=True)

    own, kv, xb = call(
        own_states, [(st, F32), ((TOK, 512), BF16), ((TOK, 256), BF16)], key_rows, values, saved_solutions
    )
    kv_lag = moved(kv, lambda i: i - lag)
    x_lead = moved(xb, lambda i: i + lag)
    chip = own + swapped(own)
    p1 = moved(chip, lambda i: i - 2 if i % 2 == 0 else i - 4)
    p2 = moved(chip, lambda i: i - 6 if i % 2 == 0 else None)
    part, send = call(states_to_send, [(st, F32), (st, F32)], own, kv_lag, p1, p2)
    recv, x_lead = lax.optimization_barrier((swapped(send), x_lead))

    y, yo, tl = call(
        adjoints,
        [((TOK, 256), F32), ((TOK, 512), BF16), (st, F32)],
        gathered, out_weight, kv, kv_lag, saved_solutions, part, recv, ridge_scale,
        flops=1 << 32, smem=(7,),
    )

    yo_lead = moved(yo, lambda i: i + lag)
    chip_l = tl + swapped(tl)
    q1 = moved(chip_l, lambda i: i + 2 if i % 2 == 0 else i + 4)
    q2 = moved(chip_l, lambda i: i + 6 if i % 2 == 0 else None)
    gk, gv, extra = call(
        near_terms, [((TOK, 256), F32), ((TOK, 256), F32), (st, F32)], kv, xb, yo, x_lead, yo_lead, tl, flops=1 << 28
    )
    part_l = q1 + q2
    recv_l = swapped(part_l + extra)
    grad_k, grad_v = call(
        base_terms, [((TOK, 256), F32), ((TOK, 256), F32)], kv, part_l, recv_l, gk, gv
    )
    return y, grad_k, grad_v


def solution(mesh):
    return jax.shard_map(
        body,
        mesh=mesh,
        in_specs=(
            P("seq", "head"),
            P("seq", "head"),
            P("seq", "head"),
            P("head", None),
            P("seq", "head"),
            P("head"),
        ),
        out_specs=(P("seq", "head"), P("seq", "head"), P("seq", "head")),
        check_vma=False,
    )
```

time: 142 us -> 72 us (0.51)
  the two profiles are of different devices: /device:TPU:59 before, /device:TPU:13 now
where the time goes in v1:
time: 72 us; the launch traced here: 71.6 us
  starting transfers between devices  33.2 us (46%)
  waiting for transfers between devices  22.2 us (31%)
  Pallas kernels  11.6 us (16%)
  local copies, waits for them, and re-layouts  3.65 us (5%)
  between operations  0.77 us (1%)
    ppermute x11, starting transfers between devices, moved(): return lax.ppermute(value, 'seq', route)  24.9 us
    ppermute x11, waiting for transfers between devices, moved(): return lax.ppermute(value, 'seq', route)  20.8 us
    pallas_call x5, Pallas kernels, call(): pl.pallas_call(kernel, out_shape=[jax.ShapeDtypeStruct(s, d) for s, d in...  11.6 us
    all_to_all x1, starting transfers between devices, body(): lax.all_to_all(copies, 'head', split_axis=0, concat_axis=0, tiled=True)  8.32 us
    broadcast_in_dim x1, local copies, waits for them, and re-layouts, body(): copies = jnp.broadcast_to(d_layer, (8, *d_layer.shape))  1.98 us
    unnamed x14, local copies, waits for them, and re-layouts  1.68 us
  transfers between devices with their start and end apart: 12, of which 7 were waited for; matrix products, arithmetic and copies ran while one was open for 0% of the time, Pallas kernels for 3%

profile of v1, /device:TPU:13, one launch (start us, length us, event | category | flops | bytes accessed | tf_op | source)
XLA Modules:
  0.0 71.6 jit_solution(17038975544823279119)
XLA Ops:
  0.6 2.0 %broadcast_in_dim.3 = bf16[8,256,256]{2,1,0:T(8,128)(2,1)} broadcast(bf16[256,256]{1,0:T(8,128)(2,1)} %param.8), dimensions={1,2} | broadcast | bytes 1179648 | tf_op jit(solution)/shard_map/broadcast_in_dim | solution.py:207
  2.6 8.3 %all-to-all-start = ((bf16[8,256,256]{2,1,0:T(8,128)(2,1)}), bf16[8,256,256]{2,1,0:T(8,128)(2,1)S(1)}, u32[]{:S(2)}, u32[]{:S(2)}) async-start(bf16[8,256,256]{2,1,0:T(8,128)(2,1)} %broadcast_in_dim.3), calls=%async_computation | async-start | bytes 2097152 | tf_op jit(solution)/shard_map/all_to_all | solution.py:208
  11.0 0.3 shard_map.85
  11.2 0.0 copy-start.3
  11.2 1.0 %collective-permute-start.1 = (f32[4,128,128]{2,1,0:T(8,128)S(1)}, f32[4,128,128]{2,1,0:T(8,128)S(1)}, u32[]{:S(2)}, u32[]{:S(2)}) collective-permute-start(f32[4,128,128]{2,1,0:T(8,128)S(1)} %get-tuple-element.19.t_ref), channel_id=1, source_target_pairs={{8,0},{0,8},{24,16},{16,24},{40,32},{32,40},{56,48},{48,56},{72,64... | collective-permute-start | bytes 786440 | tf_op jit(solution)/shard_map/ppermute | solution.py:201
  12.3 2.8 %collective-permute-start = (bf16[256,512]{1,0:T(8,128)(2,1)S(1)}, bf16[256,512]{1,0:T(8,128)(2,1)S(1)}, u32[]{:S(2)}, u32[]{:S(2)}) collective-permute-start(bf16[256,512]{1,0:T(8,128)(2,1)S(1)} %get-tuple-element.18.kv_ref), channel_id=1, source_target_pairs={{0,64},{8,72},{16,80},{24,88},{32,96},{40,104},{48,112},{56,120},{... | collective-permute-start | bytes 786440 | tf_op jit(solution)/shard_map/ppermute | solution.py:201
  15.1 0.0 collective-permute-done.1
  15.2 3.9 %collective-permute-start.2 = (f32[4,128,128]{2,1,0:T(8,128)S(1)}, f32[4,128,128]{2,1,0:T(8,128)S(1)}, u32[]{:S(2)}, u32[]{:S(2)}) collective-permute-start(f32[4,128,128]{2,1,0:T(8,128)S(1)} %add.12), channel_id=1, source_target_pairs={{0,16},{16,32},{8,40},{32,48},{24,56},{48,64},{40,72},{64,80},{56,... | collective-permute-start | bytes 786440 | tf_op jit(solution)/shard_map/ppermute | solution.py:201
  19.1 0.7 collective-permute-start.3
  19.8 2.2 %collective-permute-done.lag_ref = bf16[256,512]{1,0:T(8,128)(2,1)S(1)} collective-permute-done((bf16[256,512]{1,0:T(8,128)(2,1)S(1)}, bf16[256,512]{1,0:T(8,128)(2,1)S(1)}, u32[]{:S(2)}, u32[]{:S(2)}) %collective-permute-start) | collective-permute-done | bytes 262176 | tf_op jit(solution)/shard_map/ppermute | solution.py:201
  21.9 7.7 %collective-permute-done.2.p1_ref = f32[4,128,128]{2,1,0:T(8,128)S(1)} collective-permute-done((f32[4,128,128]{2,1,0:T(8,128)S(1)}, f32[4,128,128]{2,1,0:T(8,128)S(1)}, u32[]{:S(2)}, u32[]{:S(2)}) %collective-permute-start.2) | collective-permute-done | bytes 262176 | tf_op jit(solution)/shard_map/ppermute | solution.py:201
  29.6 0.0 collective-permute-done.3.p2_ref
  29.6 0.3 shard_map.86
  29.9 0.9 %collective-permute-start.4 = (f32[4,128,128]{2,1,0:T(8,128)S(1)}, f32[4,128,128]{2,1,0:T(8,128)S(1)}, u32[]{:S(2)}, u32[]{:S(2)}) collective-permute-start(f32[4,128,128]{2,1,0:T(8,128)S(1)} %get-tuple-element.21), channel_id=1, source_target_pairs={{8,0},{0,8},{24,16},{16,24},{40,32},{32,40},{56,48},{48,56},{72,64... | collective-permute-start | bytes 786440 | tf_op jit(solution)/shard_map/ppermute | solution.py:201
  30.8 2.4 %collective-permute-start.5 = (bf16[256,256]{1,0:T(8,128)(2,1)S(1)}, bf16[256,256]{1,0:T(8,128)(2,1)S(1)}, u32[]{:S(2)}, u32[]{:S(2)}) collective-permute-start(bf16[256,256]{1,0:T(8,128)(2,1)S(1)} %get-tuple-element.22.xb_ref), channel_id=1, source_target_pairs={{64,0},{72,8},{80,16},{88,24},{96,32},{104,40},{112,48},{120,56},{... | collective-permute-start | bytes 393224 | tf_op jit(solution)/shard_map/ppermute | solution.py:201
  33.2 4.8 %collective-permute-done.5.xl_ref = bf16[256,256]{1,0:T(8,128)(2,1)S(1)} collective-permute-done((bf16[256,256]{1,0:T(8,128)(2,1)S(1)}, bf16[256,256]{1,0:T(8,128)(2,1)S(1)}, u32[]{:S(2)}, u32[]{:S(2)}) %collective-permute-start.5) | collective-permute-done | bytes 131104 | tf_op jit(solution)/shard_map/ppermute | solution.py:201
  38.0 0.0 collective-permute-done.4.recv_ref
  38.0 0.7 copy-done.4
  38.7 1.4 %all-to-all-done.d_ref = bf16[8,256,256]{2,1,0:T(8,128)(2,1)S(1)} async-done(((bf16[8,256,256]{2,1,0:T(8,128)(2,1)}), bf16[8,256,256]{2,1,0:T(8,128)(2,1)S(1)}, u32[]{:S(2)}, u32[]{:S(2)}) %all-to-all-start) | async-done | bytes 1048608 | tf_op jit(solution)/shard_map/all_to_all | solution.py:208
  40.1 0.9 %copy-done.5 = f32[4,128,128]{2,1,0:T(8,128)S(1)} copy-done((f32[4,128,128]{2,1,0:T(8,128)S(1)}, f32[4,128,128]{2,1,0:T(8,128)}, u32[]{:S(2)}) %copy-start.5) | copy-done | bytes 262168
  41.1 8.6 %shard_map.87 = (f32[256,256]{1,0:T(8,128)}, bf16[256,512]{1,0:T(8,128)(2,1)S(1)}, f32[4,128,128]{2,1,0:T(8,128)S(1)}) custom-call(bf16[8,256,256]{2,1,0:T(8,128)(2,1)S(1)} %all-to-all-done.d_ref, bf16[256,2048]{1,0:T(8,128)(2,1)S(1)} %copy-done.3, bf16[256,512]{1,0:T(8,128)(2,1)S(1)} %get-tuple-element.18.kv_ref, ...), custom_call_target="tpu_custom_call" | custom-call | flops 4294967296 | bytes 524288 | tf_op jit(solution)/shard_map/pallas_call | solution.py:48
  49.7 0.5 collective-permute-start.6
  50.2 2.1 %collective-permute-start.9 = (bf16[256,512]{1,0:T(8,128)(2,1)S(1)}, bf16[256,512]{1,0:T(8,128)(2,1)S(1)}, u32[]{:S(2)}, u32[]{:S(2)}) collective-permute-start(bf16[256,512]{1,0:T(8,128)(2,1)S(1)} %get-tuple-element.26.yo_ref), channel_id=1, source_target_pairs={{64,0},{72,8},{80,16},{88,24},{96,32},{104,40},{112,48},{120,56},{... | collective-permute-start | bytes 786440 | tf_op jit(solution)/shard_map/ppermute | solution.py:201
  52.4 3.9 %collective-permute-start.7 = (f32[4,128,128]{2,1,0:T(8,128)S(1)}, f32[4,128,128]{2,1,0:T(8,128)S(1)}, u32[]{:S(2)}, u32[]{:S(2)}) collective-permute-start(f32[4,128,128]{2,1,0:T(8,128)S(1)} %add.13), channel_id=1, source_target_pairs={{16,0},{40,8},{32,16},{56,24},{48,32},{72,40},{64,48},{88,56},{80,... | collective-permute-start | bytes 786440 | tf_op jit(solution)/shard_map/ppermute | solution.py:201
  56.3 0.7 collective-permute-start.8
  57.0 3.0 %collective-permute-done.9.yol_ref = bf16[256,512]{1,0:T(8,128)(2,1)S(1)} collective-permute-done((bf16[256,512]{1,0:T(8,128)(2,1)S(1)}, bf16[256,512]{1,0:T(8,128)(2,1)S(1)}, u32[]{:S(2)}, u32[]{:S(2)}) %collective-permute-start.9) | collective-permute-done | bytes 262176 | tf_op jit(solution)/shard_map/ppermute | solution.py:201
  60.0 1.3 %shard_map.88 = (f32[256,256]{1,0:T(8,128)S(1)}, f32[256,256]{1,0:T(8,128)S(1)}, f32[4,128,128]{2,1,0:T(8,128)S(1)}) custom-call(bf16[256,512]{1,0:T(8,128)(2,1)S(1)} %get-tuple-element.18.kv_ref, bf16[256,256]{1,0:T(8,128)(2,1)S(1)} %get-tuple-element.22.xb_ref, bf16[256,512]{1,0:T(8,128)(2,1)S(1)} %get-tuple-element.26.yo_ref, ...), custom_call_target="tpu_custom_call" | custom-call | flops 268435456 | bytes 524288 | tf_op jit(solution)/shard_map/pallas_call | solution.py:48
  61.3 2.0 %collective-permute-done.7 = f32[4,128,128]{2,1,0:T(8,128)S(1)} collective-permute-done((f32[4,128,128]{2,1,0:T(8,128)S(1)}, f32[4,128,128]{2,1,0:T(8,128)S(1)}, u32[]{:S(2)}, u32[]{:S(2)}) %collective-permute-start.7) | collective-permute-done | bytes 262176 | tf_op jit(solution)/shard_map/ppermute | solution.py:201
  63.3 0.0 collective-permute-done.8
  63.3 5.9 %collective-permute-start.10 = (f32[4,128,128]{2,1,0:T(8,128)S(1)}, f32[4,128,128]{2,1,0:T(8,128)S(1)}, u32[]{:S(2)}, u32[]{:S(2)}) collective-permute-start(f32[4,128,128]{2,1,0:T(8,128)S(1)} %get-tuple-element.33), channel_id=1, source_target_pairs={{8,0},{0,8},{24,16},{16,24},{40,32},{32,40},{56,48},{48,56},{72,64... | collective-permute-start | bytes 786440 | tf_op jit(solution)/shard_map/ppermute | solution.py:201
  69.3 1.2 %collective-permute-done.10.recv_ref = f32[4,128,128]{2,1,0:T(8,128)S(1)} collective-permute-done((f32[4,128,128]{2,1,0:T(8,128)S(1)}, f32[4,128,128]{2,1,0:T(8,128)S(1)}, u32[]{:S(2)}, u32[]{:S(2)}) %collective-permute-start.10) | collective-permute-done | bytes 262176 | tf_op jit(solution)/shard_map/ppermute | solution.py:201
  70.4 1.1 %shard_map.89 = (f32[256,256]{1,0:T(8,128)}, f32[256,256]{1,0:T(8,128)}) custom-call(bf16[256,512]{1,0:T(8,128)(2,1)S(1)} %get-tuple-element.18.kv_ref, f32[4,128,128]{2,1,0:T(8,128)S(1)} %get-tuple-element.34.part_ref, f32[4,128,128]{2,1,0:T(8,128)S(1)} %collective-permute-done.10.recv_ref, f32[256,256]{1,0:T(8,128)S(1)} %get-tuple-element.29.gk_in, ...), custom_call_target="tpu_custom_call" | custom-call | bytes 524288 | tf_op jit(solution)/shard_map/pallas_call | solution.py:48
  (15 shorter events, 0.1 us)
Async XLA Ops:
  2.6 8.3 %copy-start = (f32[256,256]{1,0:T(8,128)S(1)}, f32[256,256]{1,0:T(8,128)}, u32[]{:S(2)}) copy-start(f32[256,256]{1,0:T(8,128)} %x_ref.3) | copy-start | bytes 786436
  2.6 8.3 %copy-start.1 = (bf16[256,256]{1,0:T(8,128)(2,1)S(1)}, bf16[256,256]{1,0:T(8,128)(2,1)}, u32[]{:S(2)}) copy-start(bf16[256,256]{1,0:T(8,128)(2,1)} %k_ref.1) | copy-start | bytes 393220
  2.6 8.3 %copy-start.2 = (bf16[256,256]{1,0:T(8,128)(2,1)S(1)}, bf16[256,256]{1,0:T(8,128)(2,1)}, u32[]{:S(2)}) copy-start(bf16[256,256]{1,0:T(8,128)(2,1)} %v_ref.1) | copy-start | bytes 393220
  2.6 37.5 %all-to-all-start = ((bf16[8,256,256]{2,1,0:T(8,128)(2,1)}), bf16[8,256,256]{2,1,0:T(8,128)(2,1)S(1)}, u32[]{:S(2)}, u32[]{:S(2)}) async-start(bf16[8,256,256]{2,1,0:T(8,128)(2,1)} %broadcast_in_dim.3), calls=%async_computation | async-start | bytes 2097152 | tf_op jit(solution)/shard_map/all_to_all | solution.py:208
  11.2 28.9 %copy-start.3 = (bf16[256,2048]{1,0:T(8,128)(2,1)S(1)}, bf16[256,2048]{1,0:T(8,128)(2,1)}, u32[]{:S(2)}) copy-start(bf16[256,2048]{1,0:T(8,128)(2,1)} %w_ref.1) | copy-start | bytes 3145732
  11.2 3.9 %collective-permute-start.1 = (f32[4,128,128]{2,1,0:T(8,128)S(1)}, f32[4,128,128]{2,1,0:T(8,128)S(1)}, u32[]{:S(2)}, u32[]{:S(2)}) collective-permute-start(f32[4,128,128]{2,1,0:T(8,128)S(1)} %get-tuple-element.19.t_ref), channel_id=1, source_target_pairs={{8,0},{0,8},{24,16},{16,24},{40,32},{32,40},{56,48},{48,56},{72,64... | collective-permute-start | bytes 786440 | tf_op jit(solution)/shard_map/ppermute | solution.py:201
  12.3 9.6 %collective-permute-start = (bf16[256,512]{1,0:T(8,128)(2,1)S(1)}, bf16[256,512]{1,0:T(8,128)(2,1)S(1)}, u32[]{:S(2)}, u32[]{:S(2)}) collective-permute-start(bf16[256,512]{1,0:T(8,128)(2,1)S(1)} %get-tuple-element.18.kv_ref), channel_id=1, source_target_pairs={{0,64},{8,72},{16,80},{24,88},{32,96},{40,104},{48,112},{56,120},{... | collective-permute-start | bytes 786440 | tf_op jit(solution)/shard_map/ppermute | solution.py:201
  15.2 14.5 %collective-permute-start.2 = (f32[4,128,128]{2,1,0:T(8,128)S(1)}, f32[4,128,128]{2,1,0:T(8,128)S(1)}, u32[]{:S(2)}, u32[]{:S(2)}) collective-permute-start(f32[4,128,128]{2,1,0:T(8,128)S(1)} %add.12), channel_id=1, source_target_pairs={{0,16},{16,32},{8,40},{32,48},{24,56},{48,64},{40,72},{64,80},{56,... | collective-permute-start | bytes 786440 | tf_op jit(solution)/shard_map/ppermute | solution.py:201
  19.1 10.5 %collective-permute-start.3 = (f32[4,128,128]{2,1,0:T(8,128)S(1)}, f32[4,128,128]{2,1,0:T(8,128)S(1)}, u32[]{:S(2)}, u32[]{:S(2)}) collective-permute-start(f32[4,128,128]{2,1,0:T(8,128)S(1)} %add.12), channel_id=1, source_target_pairs={{0,48},{16,64},{32,80},{48,96},{64,112},{80,128},{96,144},{112,160... | collective-permute-start | bytes 786440 | tf_op jit(solution)/shard_map/ppermute | solution.py:201
  29.9 8.1 %collective-permute-start.4 = (f32[4,128,128]{2,1,0:T(8,128)S(1)}, f32[4,128,128]{2,1,0:T(8,128)S(1)}, u32[]{:S(2)}, u32[]{:S(2)}) collective-permute-start(f32[4,128,128]{2,1,0:T(8,128)S(1)} %get-tuple-element.21), channel_id=1, source_target_pairs={{8,0},{0,8},{24,16},{16,24},{40,32},{32,40},{56,48},{48,56},{72,64... | collective-permute-start | bytes 786440 | tf_op jit(solution)/shard_map/ppermute | solution.py:201
  30.8 9.3 %copy-start.6 = (f32[2]{0:T(128)S(1)}, f32[2]{0:T(128)}, u32[]{:S(2)}) copy-start(f32[2]{0:T(128)} %ridge_ref.1) | copy-start | bytes 28
  30.8 7.3 %collective-permute-start.5 = (bf16[256,256]{1,0:T(8,128)(2,1)S(1)}, bf16[256,256]{1,0:T(8,128)(2,1)S(1)}, u32[]{:S(2)}, u32[]{:S(2)}) collective-permute-start(bf16[256,256]{1,0:T(8,128)(2,1)S(1)} %get-tuple-element.22.xb_ref), channel_id=1, source_target_pairs={{64,0},{72,8},{80,16},{88,24},{96,32},{104,40},{112,48},{120,56},{... | collective-permute-start | bytes 393224 | tf_op jit(solution)/shard_map/ppermute | solution.py:201
  38.0 0.7 copy-start.4
  40.1 1.0 %copy-start.5 = (f32[4,128,128]{2,1,0:T(8,128)S(1)}, f32[4,128,128]{2,1,0:T(8,128)}, u32[]{:S(2)}) copy-start(f32[4,128,128]{2,1,0:T(8,128)} %copy-done.4) | copy-start | bytes 786436
  49.7 2.7 %collective-permute-start.6 = (f32[4,128,128]{2,1,0:T(8,128)S(1)}, f32[4,128,128]{2,1,0:T(8,128)S(1)}, u32[]{:S(2)}, u32[]{:S(2)}) collective-permute-start(f32[4,128,128]{2,1,0:T(8,128)S(1)} %get-tuple-element.25.t_ref), channel_id=1, source_target_pairs={{8,0},{0,8},{24,16},{16,24},{40,32},{32,40},{56,48},{48,56},{72,64... | collective-permute-start | bytes 786440 | tf_op jit(solution)/shard_map/ppermute | solution.py:201
  50.2 9.8 %collective-permute-start.9 = (bf16[256,512]{1,0:T(8,128)(2,1)S(1)}, bf16[256,512]{1,0:T(8,128)(2,1)S(1)}, u32[]{:S(2)}, u32[]{:S(2)}) collective-permute-start(bf16[256,512]{1,0:T(8,128)(2,1)S(1)} %get-tuple-element.26.yo_ref), channel_id=1, source_target_pairs={{64,0},{72,8},{80,16},{88,24},{96,32},{104,40},{112,48},{120,56},{... | collective-permute-start | bytes 786440 | tf_op jit(solution)/shard_map/ppermute | solution.py:201
  52.4 10.9 %collective-permute-start.7 = (f32[4,128,128]{2,1,0:T(8,128)S(1)}, f32[4,128,128]{2,1,0:T(8,128)S(1)}, u32[]{:S(2)}, u32[]{:S(2)}) collective-permute-start(f32[4,128,128]{2,1,0:T(8,128)S(1)} %add.13), channel_id=1, source_target_pairs={{16,0},{40,8},{32,16},{56,24},{48,32},{72,40},{64,48},{88,56},{80,... | collective-permute-start | bytes 786440 | tf_op jit(solution)/shard_map/ppermute | solution.py:201
  56.3 7.0 %collective-permute-start.8 = (f32[4,128,128]{2,1,0:T(8,128)S(1)}, f32[4,128,128]{2,1,0:T(8,128)S(1)}, u32[]{:S(2)}, u32[]{:S(2)}) collective-permute-start(f32[4,128,128]{2,1,0:T(8,128)S(1)} %add.13), channel_id=1, source_target_pairs={{48,0},{64,16},{80,32},{96,48},{112,64},{128,80},{144,96},{160,112... | collective-permute-start | bytes 786440 | tf_op jit(solution)/shard_map/ppermute | solution.py:201
  63.3 7.1 %collective-permute-start.10 = (f32[4,128,128]{2,1,0:T(8,128)S(1)}, f32[4,128,128]{2,1,0:T(8,128)S(1)}, u32[]{:S(2)}, u32[]{:S(2)}) collective-permute-start(f32[4,128,128]{2,1,0:T(8,128)S(1)} %get-tuple-element.33), channel_id=1, source_target_pairs={{8,0},{0,8},{24,16},{16,24},{40,32},{32,40},{56,48},{48,56},{72,64... | collective-permute-start | bytes 786440 | tf_op jit(solution)/shard_map/ppermute | solution.py:201

commit v2 on v1

--- a/solution.py
+++ b/solution.py
@@ -55,14 +55,25 @@
     )(*args)
 
 
-def own_states(k_ref, v_ref, x_ref, t_ref, kv_ref, xb_ref):
+def own_states(k_ref, v_ref, t_ref, kv_ref):
     for h in range(NH):
         k = head(k_ref, h)
         t_ref[h] = mm_tn(k, k)
         t_ref[NH + h] = mm_tn(head(v_ref, h), k)
     kv_ref[:, : NH * DH] = k_ref[...]
     kv_ref[:, NH * DH :] = v_ref[...]
-    xb_ref[...] = x_ref[...].astype(BF16)
+
+
+def to_forward(d_ref, up_ref, down_ref, x_ref, ridge_ref, a_ref, b_ref, c_ref, xb_ref, xlo_ref, rid_ref):
+    core = lax.rem(lax.axis_index("seq"), 2)
+    a_ref[0] = d_ref[...]
+    a_ref[1] = up_ref[...]
+    b_ref[0] = d_ref[...]
+    b_ref[1] = down_ref[...]
+    c_ref[...] = jnp.where(core == 0, up_ref[...], down_ref[...])
+    xb_ref[...], xlo_ref[...] = split(x_ref[...])
+    for h in range(NH):
+        rid_ref[h] = jnp.full((8, DH), ridge_ref[h], F32)
 
 
 def states_to_send(t_ref, lag_ref, p1_ref, p2_ref, part_ref, send_ref):
@@ -77,11 +88,19 @@
             send_ref[at] = part + jnp.where(core == 0, t_ref[at], lag)
 
 
-def adjoints(d_ref, w_ref, kv_ref, lag_ref, x_ref, part_ref, recv_ref, ridge_ref, y_ref, yo_ref, t_ref):
+def adjoints(
+    d_ref, up_ref, down_ref, a_ref, b_ref, c_ref, w_ref, kv_ref, lag_ref, xb_ref, xlo_ref, part_ref, recv_ref, rid_ref,
+    y_ref, yo_ref, t_ref,
+):
     B = 128
-    out = mm_nt(d_ref[0], w_ref[:, :256])
-    for z in range(1, 8):
-        out = out + mm_nt(d_ref[z], w_ref[:, z * 256 : (z + 1) * 256])
+    here = lax.axis_index("head")
+    out = jnp.zeros((TOK, 256), F32)
+    for away, chunk in (
+        (0, d_ref[...]), (2, up_ref[...]), (6, down_ref[...]), (1, a_ref[0]),
+        (3, a_ref[1]), (7, b_ref[0]), (5, b_ref[1]), (4, c_ref[...]),
+    ):
+        start = pl.multiple_of(lax.rem(here + away, 8) * 256, 256)
+        out = out + mm_nt(chunk, w_ref[:, pl.ds(start, 256)])
     out = out.astype(BF16)
     yo_ref[:, 256:] = out
     rows, cols = tri(B, B)
@@ -116,7 +135,7 @@
             p = mm(ob, s_hi) + mm(ob, s_lo)
             p = p + mm(jnp.concatenate([sc_hi, sc_lo], axis=1), keys[-1])
             ps.append(p)
-            ridges.append(ridge_ref[h])
+            ridges.append(rid_ref[h, :1])
 
     n = len(ps)
 
@@ -149,47 +168,51 @@
         y_ref[:, h * DH : (h + 1) * DH] = y
         yo_ref[:, h * DH : (h + 1) * DH] = y.astype(BF16)
         y_hi, y_lo = split(y)
-        x_hi, x_lo = split(head(x_ref, h))
+        x_hi, x_lo = head(xb_ref, h), head(xlo_ref, h)
         o = out[:, h * DH : (h + 1) * DH]
         pair = mm_tn(y_hi, x_hi) + mm_tn(y_lo, x_hi) + mm_tn(y_hi, x_lo)
         t_ref[h] = pair + pair.T
         t_ref[NH + h] = mm_tn(x_hi, o) + mm_tn(x_lo, o)
 
 
-def near_terms(kv_ref, xb_ref, yo_ref, xl_ref, yol_ref, t_ref, gk_ref, gv_ref, extra_ref):
+def pair_terms(k, v, x, y, o, mask):
+    a = jnp.where(mask, mm_nt(k, x), 0.0).astype(BF16)
+    c = jnp.where(mask, mm_nt(v, o) - mm_nt(k, y), 0.0).astype(BF16)
+    return mm(c, x) - mm(a, y), mm(a, o)
+
+
+def own_terms(kv_ref, xb_ref, yo_ref, gk_ref, gv_ref):
+    rows, cols = tri(TOK, TOK)
+    for h in range(NH):
+        gk, gv = pair_terms(
+            head(kv_ref, h), head(kv_ref, h, 256), head(xb_ref, h), head(yo_ref, h), head(yo_ref, h, 256), rows <= cols
+        )
+        gk_ref[:, h * DH : (h + 1) * DH] = gk
+        gv_ref[:, h * DH : (h + 1) * DH] = gv
+
+
+def early_terms(lag_ref, xb_ref, yo_ref, other_ref, early_ref):
     core = lax.rem(lax.axis_index("seq"), 2)
     rows, cols = tri(TOK, TOK)
-    own_mask, lead_mask = rows <= cols, rows > cols
-    for h in range(NH):
-        k, v = head(kv_ref, h), head(kv_ref, h, 256)
-        x, y, o = head(xb_ref, h), head(yo_ref, h), head(yo_ref, h, 256)
-        xl, yl, ol = head(xl_ref, h), head(yol_ref, h), head(yol_ref, h, 256)
-
-        def scores(left, own, lead):
-            return jnp.concatenate(
-                [jnp.where(own_mask, mm_nt(left, own), 0.0), jnp.where(lead_mask, mm_nt(left, lead), 0.0)], axis=1
-            )
-
-        a = scores(k, x, xl).astype(BF16)
-        c = (scores(v, o, ol) - scores(k, y, yl)).astype(BF16)
-        ys = jnp.concatenate([y, yl], axis=0)
-        xs = jnp.concatenate([x, xl], axis=0)
-        os = jnp.concatenate([o, ol], axis=0)
-        gk_ref[:, h * DH : (h + 1) * DH] = mm(c, xs) - mm(a, ys)
-        gv_ref[:, h * DH : (h + 1) * DH] = mm(a, os)
-        pair = mm_tn(yl, xl)
-        extra_ref[h] = jnp.where(core == 1, t_ref[h], pair + pair.T)
-        extra_ref[NH + h] = jnp.where(core == 1, t_ref[NH + h], mm_tn(xl, ol))
-
-
-def base_terms(kv_ref, part_ref, recv_ref, gk_in, gv_in, gk_ref, gv_ref):
+    for h in range(NH):
+        k, v = head(lag_ref, h), head(lag_ref, h, 256)
+        gk, gv = pair_terms(k, v, head(xb_ref, h), head(yo_ref, h), head(yo_ref, h, 256), rows > cols)
+        sym = jnp.where(core == 1, other_ref[h], 0.0).astype(BF16)
+        cross = jnp.where(core == 1, other_ref[NH + h], 0.0).astype(BF16)
+        gk = gk - mm(k, sym) + mm_nt(v, cross)
+        early_ref[:, h * DH : (h + 1) * DH] = gk.astype(BF16)
+        early_ref[:, 256 + h * DH : 256 + (h + 1) * DH] = (gv + mm(k, cross)).astype(BF16)
+
+
+def base_terms(kv_ref, part_ref, recv_ref, early_ref, gk_in, gv_in, gk_ref, gv_ref):
     for h in range(NH):
         k, v = head(kv_ref, h), head(kv_ref, h, 256)
         s_hi, s_lo = split(part_ref[h] + recv_ref[h])
         c_hi, c_lo = split(part_ref[NH + h] + recv_ref[NH + h])
         cols = slice(h * DH, (h + 1) * DH)
-        gk_ref[:, cols] = gk_in[:, cols] - mm(k, s_hi) - mm(k, s_lo) + mm_nt(v, c_hi) + mm_nt(v, c_lo)
-        gv_ref[:, cols] = gv_in[:, cols] + mm(k, c_hi) + mm(k, c_lo)
+        gk = gk_in[:, cols] + head(early_ref, h).astype(F32) - mm(k, s_hi) - mm(k, s_lo)
+        gk_ref[:, cols] = gk + mm_nt(v, c_hi) + mm_nt(v, c_lo)
+        gv_ref[:, cols] = gv_in[:, cols] + head(early_ref, h, 256).astype(F32) + mm(k, c_hi) + mm(k, c_lo)
 
 
 def body(key_rows, values, d_layer, out_weight, saved_solutions, ridge_scale):
@@ -204,38 +227,51 @@
         return moved(value, lambda i: i ^ 1)
 
     st = (2 * NH, DH, DH)
-    copies = jnp.broadcast_to(d_layer, (8, *d_layer.shape))
-    gathered = lax.all_to_all(copies, "head", split_axis=0, concat_axis=0, tiled=True)
-
-    own, kv, xb = call(
-        own_states, [(st, F32), ((TOK, 512), BF16), ((TOK, 256), BF16)], key_rows, values, saved_solutions
-    )
+    def around(value, away):
+        return lax.ppermute(value, "head", [((i + away) % 8, i) for i in range(8)])
+
+    up, down = around(d_layer, 2), around(d_layer, -2)
+    own, kv = call(own_states, [(st, F32), ((TOK, 512), BF16)], key_rows, values)
     kv_lag = moved(kv, lambda i: i - lag)
-    x_lead = moved(xb, lambda i: i + lag)
     chip = own + swapped(own)
+    pair = (2, TOK, 256)
+    flat = ((TOK, 256), BF16)
+    up_two, down_two, across, xb, xlo, rid = call(
+        to_forward, [(pair, BF16), (pair, BF16), flat, flat, flat, ((NH, 8, DH), F32)],
+        d_layer, up, down, saved_solutions, ridge_scale, flops=1 << 34, smem=(4,),
+    )
+    chip, up_two, down_two, across = lax.optimization_barrier((chip, up_two, down_two, across))
+    up_two, down_two = around(up_two, 1), around(down_two, -1)
+    far = [
+        (s * 8 + (z + (2 if s % 2 == 0 else -2)) % 8, s * 8 + z) for s in range(n) for z in range(8)
+    ]
+    across = lax.ppermute(across, ("seq", "head"), far)
     p1 = moved(chip, lambda i: i - 2 if i % 2 == 0 else i - 4)
     p2 = moved(chip, lambda i: i - 6 if i % 2 == 0 else None)
+    p1, p2, across, kv_lag = lax.optimization_barrier((p1, p2, across, kv_lag))
     part, send = call(states_to_send, [(st, F32), (st, F32)], own, kv_lag, p1, p2)
-    recv, x_lead = lax.optimization_barrier((swapped(send), x_lead))
+    recv = swapped(send)
 
     y, yo, tl = call(
         adjoints,
         [((TOK, 256), F32), ((TOK, 512), BF16), (st, F32)],
-        gathered, out_weight, kv, kv_lag, saved_solutions, part, recv, ridge_scale,
-        flops=1 << 32, smem=(7,),
-    )
-
-    yo_lead = moved(yo, lambda i: i + lag)
-    chip_l = tl + swapped(tl)
+        d_layer, up, down, up_two, down_two, across, out_weight, kv, kv_lag, xb, xlo, part, recv, rid,
+        flops=1 << 32,
+    )
+
+    other = swapped(tl)
+    first = lax.rem(lax.axis_index("seq"), 2) == 0
+    chip_l = (tl + other).astype(BF16)
+    (early,) = call(early_terms, [((TOK, 512), BF16)], kv_lag, xb, yo, other, flops=1 << 26)
+    early = moved(early, lambda i: i + lag)
     q1 = moved(chip_l, lambda i: i + 2 if i % 2 == 0 else i + 4)
     q2 = moved(chip_l, lambda i: i + 6 if i % 2 == 0 else None)
-    gk, gv, extra = call(
-        near_terms, [((TOK, 256), F32), ((TOK, 256), F32), (st, F32)], kv, xb, yo, x_lead, yo_lead, tl, flops=1 << 28
-    )
-    part_l = q1 + q2
-    recv_l = swapped(part_l + extra)
+    gk, gv = call(own_terms, [((TOK, 256), F32)] * 2, kv, xb, yo, flops=1 << 26)
+    both = q1.astype(F32) + q2.astype(F32)
+    part_l = both + jnp.where(first, other, 0.0)
+    recv_l = swapped(both)
     grad_k, grad_v = call(
-        base_terms, [((TOK, 256), F32), ((TOK, 256), F32)], kv, part_l, recv_l, gk, gv
+        base_terms, [((TOK, 256), F32)] * 2, kv, part_l, recv_l, early, gk, gv
     )
     return y, grad_k, grad_v
 

time: 72 us -> 64 us (0.89)
  the two profiles are of different devices: /device:TPU:13 before, /device:TPU:2 now
where the time goes in v2:
time: 64 us; the launch traced here: 63.7 us
  starting transfers between devices  30 us (47%)
  waiting for transfers between devices  18.1 us (28%)
  Pallas kernels  12 us (19%)
  local copies, waits for them, and re-layouts  2.73 us (4%)
  between operations  0.81 us (1%)
    ppermute x10, starting transfers between devices, moved(): return lax.ppermute(value, 'seq', route)  20.7 us
    pallas_call x7, Pallas kernels, call(): pl.pallas_call(kernel, out_shape=[jax.ShapeDtypeStruct(s, d) for s, d in...  12 us
    ppermute x4, starting transfers between devices, around(): return lax.ppermute(value, 'head', [((i + away) % 8, i) for i in range(8)])  8.41 us
    ppermute x10, waiting for transfers between devices, moved(): return lax.ppermute(value, 'seq', route)  7.39 us
    ppermute x4, waiting for transfers between devices, around(): return lax.ppermute(value, 'head', [((i + away) % 8, i) for i in range(8)])  6.16 us
    ppermute x1, waiting for transfers between devices, body(): across = lax.ppermute(across, ('seq', 'head'), far)  4.51 us
    unnamed x14, local copies, waits for them, and re-layouts  2.73 us
  transfers between devices with their start and end apart: 15, of which 8 were waited for; matrix products, arithmetic and copies ran while one was open for 0% of the time, Pallas kernels for 4%

profile of v2, /device:TPU:2, one launch (start us, length us, event | category | flops | bytes accessed | tf_op | source)
XLA Modules:
  0.0 63.7 jit_solution(16097835278444660289)
XLA Ops:
  0.6 6.4 %collective-permute-start = (bf16[256,256]{1,0:T(8,128)(2,1)}, bf16[256,256]{1,0:T(8,128)(2,1)S(1)}, u32[]{:S(2)}, u32[]{:S(2)}) collective-permute-start(bf16[256,256]{1,0:T(8,128)(2,1)} %d_ref.3), channel_id=1, source_target_pairs={{2,0},{3,1},{4,2},{5,3},{6,4},{7,5},{0,6},{1,7},{10,8},{11,9},{12,... | collective-permute-start | bytes 393224 | tf_op jit(solution)/shard_map/ppermute | solution.py:231
  7.0 0.9 %copy-done = bf16[256,256]{1,0:T(8,128)(2,1)S(1)} copy-done((bf16[256,256]{1,0:T(8,128)(2,1)S(1)}, bf16[256,256]{1,0:T(8,128)(2,1)}, u32[]{:S(2)}) %copy-start) | copy-done | bytes 131096
  7.9 0.9 %copy-done.1 = bf16[256,256]{1,0:T(8,128)(2,1)S(1)} copy-done((bf16[256,256]{1,0:T(8,128)(2,1)S(1)}, bf16[256,256]{1,0:T(8,128)(2,1)}, u32[]{:S(2)}) %copy-start.1) | copy-done | bytes 131096
  8.8 0.3 shard_map.85
  9.1 0.0 copy-start.6
  9.1 0.1 collective-permute-start.2
  9.2 3.4 %collective-permute-start.8 = (bf16[256,512]{1,0:T(8,128)(2,1)S(1)}, bf16[256,512]{1,0:T(8,128)(2,1)S(1)}, u32[]{:S(2)}, u32[]{:S(2)}) collective-permute-start(bf16[256,512]{1,0:T(8,128)(2,1)S(1)} %get-tuple-element.36.kv_ref), channel_id=1, source_target_pairs={{0,64},{8,72},{16,80},{24,88},{32,96},{40,104},{48,112},{56,120},{... | collective-permute-start | bytes 786440 | tf_op jit(solution)/shard_map/ppermute | solution.py:224
  12.6 0.3 collective-permute-done.up_ref
  12.9 3.7 %collective-permute-done.1.down_ref = bf16[256,256]{1,0:T(8,128)(2,1)S(1)} collective-permute-done((bf16[256,256]{1,0:T(8,128)(2,1)}, bf16[256,256]{1,0:T(8,128)(2,1)S(1)}, u32[]{:S(2)}, u32[]{:S(2)}) %collective-permute-start.1) | collective-permute-done | bytes 131104 | tf_op jit(solution)/shard_map/ppermute | solution.py:231
  16.7 0.9 %copy-done.4 = bf16[256,256]{1,0:T(8,128)(2,1)S(1)} copy-done((bf16[256,256]{1,0:T(8,128)(2,1)S(1)}, bf16[256,256]{1,0:T(8,128)(2,1)}, u32[]{:S(2)}) %copy-start.4) | copy-done | bytes 131096
  17.6 0.6 shard_map.86
  18.3 3.6 %collective-permute-start.5 = (f32[4,128,128]{2,1,0:T(8,128)S(1)}, f32[4,128,128]{2,1,0:T(8,128)S(1)}, u32[]{:S(2)}, u32[]{:S(2)}) collective-permute-start(f32[4,128,128]{2,1,0:T(8,128)S(1)} %add.12), channel_id=1, source_target_pairs={{0,16},{16,32},{8,40},{32,48},{24,56},{48,64},{40,72},{64,80},{56,... | collective-permute-start | bytes 786440 | tf_op jit(solution)/shard_map/ppermute | solution.py:224
  21.9 4.5 %collective-permute-start.6 = (f32[4,128,128]{2,1,0:T(8,128)S(1)}, f32[4,128,128]{2,1,0:T(8,128)S(1)}, u32[]{:S(2)}, u32[]{:S(2)}) collective-permute-start(f32[4,128,128]{2,1,0:T(8,128)S(1)} %add.12), channel_id=1, source_target_pairs={{0,48},{16,64},{32,80},{48,96},{64,112},{80,128},{96,144},{112,160... | collective-permute-start | bytes 786440 | tf_op jit(solution)/shard_map/ppermute | solution.py:224
  26.4 0.8 %collective-permute-start.7 = (bf16[256,256]{1,0:T(8,128)(2,1)S(1)}, bf16[256,256]{1,0:T(8,128)(2,1)S(1)}, u32[]{:S(2)}, u32[]{:S(2)}) collective-permute-start(bf16[256,256]{1,0:T(8,128)(2,1)S(1)} %get-tuple-element.35), channel_id=1, source_target_pairs={{2,0},{3,1},{4,2},{5,3},{6,4},{7,5},{0,6},{1,7},{14,8},{15,9},{8,1... | collective-permute-start | bytes 393224 | tf_op jit(solution)/shard_map/ppermute | solution.py:248
  27.2 1.3 %collective-permute-start.3 = (bf16[2,256,256]{2,1,0:T(8,128)(2,1)S(1)}, bf16[2,256,256]{2,1,0:T(8,128)(2,1)S(1)}, u32[]{:S(2)}, u32[]{:S(2)}) collective-permute-start(bf16[2,256,256]{2,1,0:T(8,128)(2,1)S(1)} %get-tuple-element.32), channel_id=1, source_target_pairs={{1,0},{2,1},{3,2},{4,3},{5,4},{6,5},{7,6},{0,7},{9,8},{10,9},{11,1... | collective-permute-start | bytes 786440 | tf_op jit(solution)/shard_map/ppermute | solution.py:231
  28.5 0.8 %collective-permute-start.4 = (bf16[2,256,256]{2,1,0:T(8,128)(2,1)S(1)}, bf16[2,256,256]{2,1,0:T(8,128)(2,1)S(1)}, u32[]{:S(2)}, u32[]{:S(2)}) collective-permute-start(bf16[2,256,256]{2,1,0:T(8,128)(2,1)S(1)} %get-tuple-element.33), channel_id=1, source_target_pairs={{7,0},{0,1},{1,2},{2,3},{3,4},{4,5},{5,6},{6,7},{15,8},{8,9},{9,10... | collective-permute-start | bytes 786440 | tf_op jit(solution)/shard_map/ppermute | solution.py:231
  29.2 4.5 %collective-permute-done.7.c_ref = bf16[256,256]{1,0:T(8,128)(2,1)S(1)} collective-permute-done((bf16[256,256]{1,0:T(8,128)(2,1)S(1)}, bf16[256,256]{1,0:T(8,128)(2,1)S(1)}, u32[]{:S(2)}, u32[]{:S(2)}) %collective-permute-start.7) | collective-permute-done | bytes 131104 | tf_op jit(solution)/shard_map/ppermute | solution.py:248
  33.8 0.3 shard_map.87
  34.0 0.1 collective-permute-start.9
  34.1 1.5 %collective-permute-done.3.a_ref = bf16[2,256,256]{2,1,0:T(8,128)(2,1)S(1)} collective-permute-done((bf16[2,256,256]{2,1,0:T(8,128)(2,1)S(1)}, bf16[2,256,256]{2,1,0:T(8,128)(2,1)S(1)}, u32[]{:S(2)}, u32[]{:S(2)}) %collective-permute-start.3) | collective-permute-done | bytes 262176 | tf_op jit(solution)/shard_map/ppermute | solution.py:231
  35.7 0.6 collective-permute-done.4.b_ref
  36.3 8.1 %shard_map.88 = (f32[256,256]{1,0:T(8,128)}, bf16[256,512]{1,0:T(8,128)(2,1)S(1)}, f32[4,128,128]{2,1,0:T(8,128)S(1)}) custom-call(bf16[256,256]{1,0:T(8,128)(2,1)S(1)} %copy-done.5, bf16[256,256]{1,0:T(8,128)(2,1)S(1)} %collective-permute-done.up_ref, bf16[256,256]{1,0:T(8,128)(2,1)S(1)} %collective-permute-done.1.down_ref, ...), custom_call_target="tpu_custom_call" | custom-call | flops 4294967296 | bytes 524288 | tf_op jit(solution)/shard_map/pallas_call | solution.py:48
  44.4 1.5 %collective-permute-done.10.other_ref = f32[4,128,128]{2,1,0:T(8,128)S(1)} collective-permute-done((f32[4,128,128]{2,1,0:T(8,128)S(1)}, f32[4,128,128]{2,1,0:T(8,128)S(1)}, u32[]{:S(2)}, u32[]{:S(2)}) %collective-permute-start.10) | collective-permute-done | bytes 262176 | tf_op jit(solution)/shard_map/ppermute | solution.py:224
  46.0 2.6 %collective-permute-start.12 = (bf16[4,128,128]{2,1,0:T(8,128)(2,1)S(1)}, bf16[4,128,128]{2,1,0:T(8,128)(2,1)S(1)}, u32[]{:S(2)}, u32[]{:S(2)}) collective-permute-start(bf16[4,128,128]{2,1,0:T(8,128)(2,1)S(1)} %add_convert_fusion), channel_id=1, source_target_pairs={{48,0},{64,16},{80,32},{96,48},{112,64},{128,80},{144,96},{160,112... | collective-permute-start | bytes 393224 | tf_op jit(solution)/shard_map/ppermute | solution.py:224
  48.6 4.5 %collective-permute-start.11 = (bf16[4,128,128]{2,1,0:T(8,128)(2,1)S(1)}, bf16[4,128,128]{2,1,0:T(8,128)(2,1)S(1)}, u32[]{:S(2)}, u32[]{:S(2)}) collective-permute-start(bf16[4,128,128]{2,1,0:T(8,128)(2,1)S(1)} %add_convert_fusion), channel_id=1, source_target_pairs={{16,0},{40,8},{32,16},{56,24},{48,32},{72,40},{64,48},{88,56},{80,... | collective-permute-start | bytes 393224 | tf_op jit(solution)/shard_map/ppermute | solution.py:224
  53.1 0.8 %shard_map.89 = bf16[256,512]{1,0:T(8,128)(2,1)S(1)} custom-call(bf16[256,512]{1,0:T(8,128)(2,1)S(1)} %collective-permute-done.8.lag_ref, bf16[256,256]{1,0:T(8,128)(2,1)S(1)} %get-tuple-element.39.xb_ref, bf16[256,512]{1,0:T(8,128)(2,1)S(1)} %get-tuple-element.48.yo_ref, f32[4,128,128]{2,1,0:T(8,128)S(1)} %collective-permute-done.10.other_ref), custom_call_target="tpu_custom_call" | custom-call | flops 67108864 | bytes 524288 | tf_op jit(solution)/shard_map/pallas_call | solution.py:48
  53.9 1.9 %collective-permute-start.14 = (bf16[256,512]{1,0:T(8,128)(2,1)S(1)}, bf16[256,512]{1,0:T(8,128)(2,1)S(1)}, u32[]{:S(2)}, u32[]{:S(2)}) collective-permute-start(bf16[256,512]{1,0:T(8,128)(2,1)S(1)} %shard_map.89), channel_id=1, source_target_pairs={{64,0},{72,8},{80,16},{88,24},{96,32},{104,40},{112,48},{120,56},{... | collective-permute-start | bytes 786440 | tf_op jit(solution)/shard_map/ppermute | solution.py:224
  55.8 1.1 %collective-permute-done.11 = bf16[4,128,128]{2,1,0:T(8,128)(2,1)S(1)} collective-permute-done((bf16[4,128,128]{2,1,0:T(8,128)(2,1)S(1)}, bf16[4,128,128]{2,1,0:T(8,128)(2,1)S(1)}, u32[]{:S(2)}, u32[]{:S(2)}) %collective-permute-start.11) | collective-permute-done | bytes 131104 | tf_op jit(solution)/shard_map/ppermute | solution.py:224
  56.9 0.1 collective-permute-start.13
  57.0 0.7 %shard_map.90 = (f32[256,256]{1,0:T(8,128)S(1)}, f32[256,256]{1,0:T(8,128)S(1)}) custom-call(bf16[256,512]{1,0:T(8,128)(2,1)S(1)} %get-tuple-element.36.kv_ref, bf16[256,256]{1,0:T(8,128)(2,1)S(1)} %get-tuple-element.39.xb_ref, bf16[256,512]{1,0:T(8,128)(2,1)S(1)} %get-tuple-element.48.yo_ref), custom_call_target="tpu_custom_call" | custom-call | flops 67108864 | bytes 524288 | tf_op jit(solution)/shard_map/pallas_call | solution.py:48
  57.8 4.7 %collective-permute-done.14.early_ref = bf16[256,512]{1,0:T(8,128)(2,1)S(1)} collective-permute-done((bf16[256,512]{1,0:T(8,128)(2,1)S(1)}, bf16[256,512]{1,0:T(8,128)(2,1)S(1)}, u32[]{:S(2)}, u32[]{:S(2)}) %collective-permute-start.14) | collective-permute-done | bytes 262176 | tf_op jit(solution)/shard_map/ppermute | solution.py:224
  62.5 1.1 %shard_map.91 = (f32[256,256]{1,0:T(8,128)}, f32[256,256]{1,0:T(8,128)}) custom-call(bf16[256,512]{1,0:T(8,128)(2,1)S(1)} %get-tuple-element.36.kv_ref, f32[4,128,128]{2,1,0:T(8,128)S(1)} %get-tuple-element.54.part_ref, f32[4,128,128]{2,1,0:T(8,128)S(1)} %collective-permute-done.13.recv_ref, bf16[256,512]{1,0:T(8,128)(2,1)S(1)} %collective-permute-done.14.early_ref, ...), custom_call_target="tpu_custom_call" | custom-call | bytes 524288 | tf_op jit(solution)/shard_map/pallas_call | solution.py:48
  (22 shorter events, 0.2 us)
Async XLA Ops:
  0.6 12.3 %collective-permute-start = (bf16[256,256]{1,0:T(8,128)(2,1)}, bf16[256,256]{1,0:T(8,128)(2,1)S(1)}, u32[]{:S(2)}, u32[]{:S(2)}) collective-permute-start(bf16[256,256]{1,0:T(8,128)(2,1)} %d_ref.3), channel_id=1, source_target_pairs={{2,0},{3,1},{4,2},{5,3},{6,4},{7,5},{0,6},{1,7},{10,8},{11,9},{12,... | collective-permute-start | bytes 393224 | tf_op jit(solution)/shard_map/ppermute | solution.py:231
  7.0 9.6 %collective-permute-start.1 = (bf16[256,256]{1,0:T(8,128)(2,1)}, bf16[256,256]{1,0:T(8,128)(2,1)S(1)}, u32[]{:S(2)}, u32[]{:S(2)}) collective-permute-start(bf16[256,256]{1,0:T(8,128)(2,1)} %d_ref.3), channel_id=1, source_target_pairs={{6,0},{7,1},{0,2},{1,3},{2,4},{3,5},{4,6},{5,7},{14,8},{15,9},{8,1... | collective-permute-start | bytes 393224 | tf_op jit(solution)/shard_map/ppermute | solution.py:231
  7.0 0.9 %copy-start = (bf16[256,256]{1,0:T(8,128)(2,1)S(1)}, bf16[256,256]{1,0:T(8,128)(2,1)}, u32[]{:S(2)}) copy-start(bf16[256,256]{1,0:T(8,128)(2,1)} %k_ref.1) | copy-start | bytes 393220
  7.9 0.9 %copy-start.1 = (bf16[256,256]{1,0:T(8,128)(2,1)S(1)}, bf16[256,256]{1,0:T(8,128)(2,1)}, u32[]{:S(2)}) copy-start(bf16[256,256]{1,0:T(8,128)(2,1)} %v_ref.1) | copy-start | bytes 393220
  8.8 7.8 %copy-start.3 = (f32[256,256]{1,0:T(8,128)S(1)}, f32[256,256]{1,0:T(8,128)}, u32[]{:S(2)}) copy-start(f32[256,256]{1,0:T(8,128)} %x_ref.1) | copy-start | bytes 786436
  9.1 7.5 %copy-start.6 = (f32[2]{0:T(128)S(1)}, f32[2]{0:T(128)}, u32[]{:S(2)}) copy-start(f32[2]{0:T(128)} %ridge_ref.1) | copy-start | bytes 28
  9.1 9.1 %collective-permute-start.2 = (f32[4,128,128]{2,1,0:T(8,128)S(1)}, f32[4,128,128]{2,1,0:T(8,128)S(1)}, u32[]{:S(2)}, u32[]{:S(2)}) collective-permute-start(f32[4,128,128]{2,1,0:T(8,128)S(1)} %get-tuple-element.28.t_ref), channel_id=1, source_target_pairs={{8,0},{0,8},{24,16},{16,24},{40,32},{32,40},{56,48},{48,56},{72,64... | collective-permute-start | bytes 786440 | tf_op jit(solution)/shard_map/ppermute | solution.py:224
  9.2 19.3 %collective-permute-start.8 = (bf16[256,512]{1,0:T(8,128)(2,1)S(1)}, bf16[256,512]{1,0:T(8,128)(2,1)S(1)}, u32[]{:S(2)}, u32[]{:S(2)}) collective-permute-start(bf16[256,512]{1,0:T(8,128)(2,1)S(1)} %get-tuple-element.36.kv_ref), channel_id=1, source_target_pairs={{0,64},{8,72},{16,80},{24,88},{32,96},{40,104},{48,112},{56,120},{... | collective-permute-start | bytes 786440 | tf_op jit(solution)/shard_map/ppermute | solution.py:224
  16.6 0.9 %copy-start.4 = (bf16[256,256]{1,0:T(8,128)(2,1)S(1)}, bf16[256,256]{1,0:T(8,128)(2,1)}, u32[]{:S(2)}) copy-start(bf16[256,256]{1,0:T(8,128)(2,1)} %d_ref.3) | copy-start | bytes 393220
  18.2 18.1 %copy-start.2 = (bf16[256,2048]{1,0:T(8,128)(2,1)S(1)}, bf16[256,2048]{1,0:T(8,128)(2,1)}, u32[]{:S(2)}) copy-start(bf16[256,2048]{1,0:T(8,128)(2,1)} %w_ref.1) | copy-start | bytes 3145732
  18.3 18.0 %copy-start.5 = (bf16[256,256]{1,0:T(8,128)(2,1)S(1)}, bf16[256,256]{1,0:T(8,128)(2,1)}, u32[]{:S(2)}) copy-start(bf16[256,256]{1,0:T(8,128)(2,1)} %d_ref.3) | copy-start | bytes 393220
  18.3 15.5 %collective-permute-start.5 = (f32[4,128,128]{2,1,0:T(8,128)S(1)}, f32[4,128,128]{2,1,0:T(8,128)S(1)}, u32[]{:S(2)}, u32[]{:S(2)}) collective-permute-start(f32[4,128,128]{2,1,0:T(8,128)S(1)} %add.12), channel_id=1, source_target_pairs={{0,16},{16,32},{8,40},{32,48},{24,56},{48,64},{40,72},{64,80},{56,... | collective-permute-start | bytes 786440 | tf_op jit(solution)/shard_map/ppermute | solution.py:224
  21.9 11.9 %collective-permute-start.6 = (f32[4,128,128]{2,1,0:T(8,128)S(1)}, f32[4,128,128]{2,1,0:T(8,128)S(1)}, u32[]{:S(2)}, u32[]{:S(2)}) collective-permute-start(f32[4,128,128]{2,1,0:T(8,128)S(1)} %add.12), channel_id=1, source_target_pairs={{0,48},{16,64},{32,80},{48,96},{64,112},{80,128},{96,144},{112,160... | collective-permute-start | bytes 786440 | tf_op jit(solution)/shard_map/ppermute | solution.py:224
  26.4 7.4 %collective-permute-start.7 = (bf16[256,256]{1,0:T(8,128)(2,1)S(1)}, bf16[256,256]{1,0:T(8,128)(2,1)S(1)}, u32[]{:S(2)}, u32[]{:S(2)}) collective-permute-start(bf16[256,256]{1,0:T(8,128)(2,1)S(1)} %get-tuple-element.35), channel_id=1, source_target_pairs={{2,0},{3,1},{4,2},{5,3},{6,4},{7,5},{0,6},{1,7},{14,8},{15,9},{8,1... | collective-permute-start | bytes 393224 | tf_op jit(solution)/shard_map/ppermute | solution.py:248
  27.2 8.5 %collective-permute-start.3 = (bf16[2,256,256]{2,1,0:T(8,128)(2,1)S(1)}, bf16[2,256,256]{2,1,0:T(8,128)(2,1)S(1)}, u32[]{:S(2)}, u32[]{:S(2)}) collective-permute-start(bf16[2,256,256]{2,1,0:T(8,128)(2,1)S(1)} %get-tuple-element.32), channel_id=1, source_target_pairs={{1,0},{2,1},{3,2},{4,3},{5,4},{6,5},{7,6},{0,7},{9,8},{10,9},{11,1... | collective-permute-start | bytes 786440 | tf_op jit(solution)/shard_map/ppermute | solution.py:231
  28.5 7.8 %collective-permute-start.4 = (bf16[2,256,256]{2,1,0:T(8,128)(2,1)S(1)}, bf16[2,256,256]{2,1,0:T(8,128)(2,1)S(1)}, u32[]{:S(2)}, u32[]{:S(2)}) collective-permute-start(bf16[2,256,256]{2,1,0:T(8,128)(2,1)S(1)} %get-tuple-element.33), channel_id=1, source_target_pairs={{7,0},{0,1},{1,2},{2,3},{3,4},{4,5},{5,6},{6,7},{15,8},{8,9},{9,10... | collective-permute-start | bytes 786440 | tf_op jit(solution)/shard_map/ppermute | solution.py:231
  34.0 2.2 %collective-permute-start.9 = (f32[4,128,128]{2,1,0:T(8,128)S(1)}, f32[4,128,128]{2,1,0:T(8,128)S(1)}, u32[]{:S(2)}, u32[]{:S(2)}) collective-permute-start(f32[4,128,128]{2,1,0:T(8,128)S(1)} %get-tuple-element.44), channel_id=1, source_target_pairs={{8,0},{0,8},{24,16},{16,24},{40,32},{32,40},{56,48},{48,56},{72,64... | collective-permute-start | bytes 786440 | tf_op jit(solution)/shard_map/ppermute | solution.py:224
  44.4 1.5 %collective-permute-start.10 = (f32[4,128,128]{2,1,0:T(8,128)S(1)}, f32[4,128,128]{2,1,0:T(8,128)S(1)}, u32[]{:S(2)}, u32[]{:S(2)}) collective-permute-start(f32[4,128,128]{2,1,0:T(8,128)S(1)} %get-tuple-element.47), channel_id=1, source_target_pairs={{8,0},{0,8},{24,16},{16,24},{40,32},{32,40},{56,48},{48,56},{72,64... | collective-permute-start | bytes 786440 | tf_op jit(solution)/shard_map/ppermute | solution.py:224
  46.0 9.8 %collective-permute-start.12 = (bf16[4,128,128]{2,1,0:T(8,128)(2,1)S(1)}, bf16[4,128,128]{2,1,0:T(8,128)(2,1)S(1)}, u32[]{:S(2)}, u32[]{:S(2)}) collective-permute-start(bf16[4,128,128]{2,1,0:T(8,128)(2,1)S(1)} %add_convert_fusion), channel_id=1, source_target_pairs={{48,0},{64,16},{80,32},{96,48},{112,64},{128,80},{144,96},{160,112... | collective-permute-start | bytes 393224 | tf_op jit(solution)/shard_map/ppermute | solution.py:224
  48.6 8.3 %collective-permute-start.11 = (bf16[4,128,128]{2,1,0:T(8,128)(2,1)S(1)}, bf16[4,128,128]{2,1,0:T(8,128)(2,1)S(1)}, u32[]{:S(2)}, u32[]{:S(2)}) collective-permute-start(bf16[4,128,128]{2,1,0:T(8,128)(2,1)S(1)} %add_convert_fusion), channel_id=1, source_target_pairs={{16,0},{40,8},{32,16},{56,24},{48,32},{72,40},{64,48},{88,56},{80,... | collective-permute-start | bytes 393224 | tf_op jit(solution)/shard_map/ppermute | solution.py:224
  53.9 8.7 %collective-permute-start.14 = (bf16[256,512]{1,0:T(8,128)(2,1)S(1)}, bf16[256,512]{1,0:T(8,128)(2,1)S(1)}, u32[]{:S(2)}, u32[]{:S(2)}) collective-permute-start(bf16[256,512]{1,0:T(8,128)(2,1)S(1)} %shard_map.89), channel_id=1, source_target_pairs={{64,0},{72,8},{80,16},{88,24},{96,32},{104,40},{112,48},{120,56},{... | collective-permute-start | bytes 786440 | tf_op jit(solution)/shard_map/ppermute | solution.py:224
  56.9 5.6 %collective-permute-start.13 = (f32[4,128,128]{2,1,0:T(8,128)S(1)}, f32[4,128,128]{2,1,0:T(8,128)S(1)}, u32[]{:S(2)}, u32[]{:S(2)}) collective-permute-start(f32[4,128,128]{2,1,0:T(8,128)S(1)} %get-tuple-element.53), channel_id=1, source_target_pairs={{8,0},{0,8},{24,16},{16,24},{40,32},{32,40},{56,48},{48,56},{72,64... | collective-permute-start | bytes 786440 | tf_op jit(solution)/shard_map/ppermute | solution.py:224

commit v3 on v2

--- a/solution.py
+++ b/solution.py
@@ -9,6 +9,7 @@
 TOK = 256
 NH = 2
 ITERS = 8
+FINE = 3
 EPSILON = 1e-06
 F32 = jnp.float32
 BF16 = jnp.bfloat16
@@ -44,24 +45,24 @@
     return r, c
 
 
-def call(kernel, outs, *args, flops=0, smem=()):
+def call(kernel, outs, *args, flops=0, size=1 << 19, smem=()):
     return pl.pallas_call(
         kernel,
         out_shape=[jax.ShapeDtypeStruct(s, d) for s, d in outs],
         in_specs=[SM if i in smem else VM for i in range(len(args))],
         out_specs=[VM] * len(outs),
         compiler_params=PARAMS,
-        cost_estimate=pl.CostEstimate(flops=flops, bytes_accessed=1 << 19, transcendentals=0),
+        cost_estimate=pl.CostEstimate(flops=flops, bytes_accessed=size, transcendentals=0),
     )(*args)
 
 
-def own_states(k_ref, v_ref, t_ref, kv_ref):
-    for h in range(NH):
-        k = head(k_ref, h)
+def own_states(kvd_ref, t_ref, kv_ref, dv_ref):
+    for h in range(NH):
+        k = head(kvd_ref, h)
         t_ref[h] = mm_tn(k, k)
-        t_ref[NH + h] = mm_tn(head(v_ref, h), k)
-    kv_ref[:, : NH * DH] = k_ref[...]
-    kv_ref[:, NH * DH :] = v_ref[...]
+        t_ref[NH + h] = mm_tn(head(kvd_ref, h, 256), k)
+    kv_ref[...] = kvd_ref[:, :512]
+    dv_ref[...] = kvd_ref[:, 512:]
 
 
 def to_forward(d_ref, up_ref, down_ref, x_ref, ridge_ref, a_ref, b_ref, c_ref, xb_ref, xlo_ref, rid_ref):
@@ -76,14 +77,24 @@
         rid_ref[h] = jnp.full((8, DH), ridge_ref[h], F32)
 
 
+def chip_states(own_ref, other_ref, out_ref):
+    for h in range(NH):
+        out_ref[h] = (own_ref[h] + other_ref[h]).astype(BF16)
+        hi, lo = split(own_ref[NH + h] + other_ref[NH + h])
+        out_ref[NH + h] = hi
+        out_ref[2 * NH + h] = lo
+
+
 def states_to_send(t_ref, lag_ref, p1_ref, p2_ref, part_ref, send_ref):
     core = lax.rem(lax.axis_index("seq"), 2)
     for h in range(NH):
         k = head(lag_ref, h)
         lag_g = mm_tn(k, k)
         lag_s = mm_tn(head(lag_ref, h, NH * DH), k)
-        for at, lag in ((h, lag_g), (NH + h, lag_s)):
-            part = p1_ref[at] + p2_ref[at]
+        gram = p1_ref[h].astype(F32) + p2_ref[h].astype(F32)
+        state = p1_ref[NH + h].astype(F32) + p2_ref[NH + h].astype(F32)
+        state = state + p1_ref[2 * NH + h].astype(F32) + p2_ref[2 * NH + h].astype(F32)
+        for at, lag, part in ((h, lag_g, gram), (NH + h, lag_s, state)):
             part_ref[at] = part
             send_ref[at] = part + jnp.where(core == 0, t_ref[at], lag)
 
@@ -139,29 +150,49 @@
 
     n = len(ps)
 
-    def apply_gram(p, i):
-        p_hi, p_lo = split(p)
-        r = mm(jnp.concatenate([p_hi, p_lo], axis=1), rhs[i])
-        sc = jnp.concatenate(
-            [jnp.where(low, r[:, B : 2 * B], 0.0), jnp.where(up, r[:, 2 * B : 3 * B], 0.0)], axis=1
-        )
-        sc_hi, sc_lo = split(sc)
-        t = mm(jnp.concatenate([sc_hi, sc_lo], axis=1), keys[i])
-        return t + r[:, :B] + r[:, 3 * B :] + ridges[i] * p
+    def products(vectors, fine):
+        firsts = []
+        for i in range(n):
+            if fine:
+                hi, lo = split(vectors[i])
+                firsts.append(mm(jnp.concatenate([hi, lo], axis=1), rhs[i]))
+            else:
+                firsts.append(mm(vectors[i].astype(BF16), rhs[i][:DH, : 3 * B]))
+        seconds = []
+        for i in range(n):
+            r = firsts[i]
+            sc = jnp.concatenate(
+                [jnp.where(low, r[:, B : 2 * B], 0.0), jnp.where(up, r[:, 2 * B : 3 * B], 0.0)], axis=1
+            )
+            if fine:
+                sc_hi, sc_lo = split(sc)
+                seconds.append(mm(jnp.concatenate([sc_hi, sc_lo], axis=1), keys[i]))
+            else:
+                seconds.append(mm(sc.astype(BF16), keys[i][: 2 * B]))
+        images = []
+        for i in range(n):
+            base = firsts[i][:, :B] + ridges[i] * vectors[i]
+            if fine:
+                base = base + firsts[i][:, 3 * B :]
+            images.append(seconds[i] + base)
+        return images
 
     ys = [jnp.zeros((B, DH), F32)] * n
     rs = list(ps)
     rrs = [jnp.sum(r * r, axis=-1, keepdims=True) for r in rs]
+    images = products(ps, True)
     for it in range(ITERS):
-        for i in range(n):
-            a = apply_gram(ps[i], i)
-            alpha = rrs[i] / (jnp.sum(ps[i] * a, axis=-1, keepdims=True) + EPSILON)
-            ys[i] = ys[i] + alpha * ps[i]
-            if it < ITERS - 1:
-                rs[i] = rs[i] - alpha * a
-                nr = jnp.sum(rs[i] * rs[i], axis=-1, keepdims=True)
-                ps[i] = rs[i] + nr / (rrs[i] + EPSILON) * ps[i]
-                rrs[i] = nr
+        steps = [jnp.sum(ps[i] * images[i], axis=-1, keepdims=True) for i in range(n)]
+        alphas = [rrs[i] / (steps[i] + EPSILON) for i in range(n)]
+        rs = [rs[i] - alphas[i] * images[i] for i in range(n)]
+        ys = [ys[i] + alphas[i] * ps[i] for i in range(n)]
+        if it < ITERS - 1:
+            fresh = products(rs, it + 1 < FINE)
+            nrs = [jnp.sum(r * r, axis=-1, keepdims=True) for r in rs]
+            betas = [nrs[i] / (rrs[i] + EPSILON) for i in range(n)]
+            ps = [rs[i] + betas[i] * ps[i] for i in range(n)]
+            images = [fresh[i] + betas[i] * images[i] for i in range(n)]
+            rrs = nrs
 
     for h in range(NH):
         y = jnp.concatenate([ys[2 * h], ys[2 * h + 1]], axis=0)
@@ -231,16 +262,16 @@
         return lax.ppermute(value, "head", [((i + away) % 8, i) for i in range(8)])
 
     up, down = around(d_layer, 2), around(d_layer, -2)
-    own, kv = call(own_states, [(st, F32), ((TOK, 512), BF16)], key_rows, values)
+    flat = ((TOK, 256), BF16)
+    kvd = jnp.concatenate([key_rows, values, d_layer], axis=1)
+    own, kv, dv = call(own_states, [(st, F32), ((TOK, 512), BF16), flat], kvd)
     kv_lag = moved(kv, lambda i: i - lag)
-    chip = own + swapped(own)
+    (chip,) = call(chip_states, [((3 * NH, DH, DH), BF16)], own, swapped(own))
     pair = (2, TOK, 256)
-    flat = ((TOK, 256), BF16)
     up_two, down_two, across, xb, xlo, rid = call(
         to_forward, [(pair, BF16), (pair, BF16), flat, flat, flat, ((NH, 8, DH), F32)],
-        d_layer, up, down, saved_solutions, ridge_scale, flops=1 << 34, smem=(4,),
+        dv, up, down, saved_solutions, ridge_scale, flops=1 << 34, smem=(4,),
     )
-    chip, up_two, down_two, across = lax.optimization_barrier((chip, up_two, down_two, across))
     up_two, down_two = around(up_two, 1), around(down_two, -1)
     far = [
         (s * 8 + (z + (2 if s % 2 == 0 else -2)) % 8, s * 8 + z) for s in range(n) for z in range(8)
@@ -248,14 +279,15 @@
     across = lax.ppermute(across, ("seq", "head"), far)
     p1 = moved(chip, lambda i: i - 2 if i % 2 == 0 else i - 4)
     p2 = moved(chip, lambda i: i - 6 if i % 2 == 0 else None)
-    p1, p2, across, kv_lag = lax.optimization_barrier((p1, p2, across, kv_lag))
-    part, send = call(states_to_send, [(st, F32), (st, F32)], own, kv_lag, p1, p2)
+    p1, p2, kv_lag = lax.optimization_barrier((p1, p2, kv_lag))
+    part, send = call(states_to_send, [(st, F32), (st, F32)], own, kv_lag, p1, p2, size=0)
+    send, across = lax.optimization_barrier((send, across))
     recv = swapped(send)
 
     y, yo, tl = call(
         adjoints,
         [((TOK, 256), F32), ((TOK, 512), BF16), (st, F32)],
-        d_layer, up, down, up_two, down_two, across, out_weight, kv, kv_lag, xb, xlo, part, recv, rid,
+        dv, up, down, up_two, down_two, across, out_weight, kv, kv_lag, xb, xlo, part, recv, rid,
         flops=1 << 32,
     )
 

time: 64 us -> 58 us (0.906)
  waiting for transfers between devices: 18.1 us -> 13.1 us
  local copies, waits for them, and re-layouts: 2.73 us -> 0.54 us
  Pallas kernels: 12 us -> 9.84 us
  starting transfers between devices: 30 us -> 32 us
  other arithmetic: 0.13 us -> 1.14 us
    ppermute x1, starting transfers between devices: 0.81 us -> 4.21 us  [body(): across = lax.ppermute(across, ('seq', 'head'), far)]
    ppermute x1, waiting for transfers between devices: 4.51 us -> 1.61 us  [body(): across = lax.ppermute(across, ('seq', 'head'), far)]
    ppermute x4, waiting for transfers between devices: 6.16 us -> 3.67 us  [around(): return lax.ppermute(value, 'head', [((i + away) % 8, i) for i in range(8)])]
    unnamed x14 -> x8, local copies, waits for them, and re-layouts: 2.73 us -> 0.54 us
    pallas_call x7 -> x8, Pallas kernels: 12 us -> 9.84 us  [call(): pl.pallas_call(kernel, out_shape=[jax.ShapeDtypeStruct(s, d) for s, d in...]
    ppermute x10, starting transfers between devices: 20.7 us -> 19.4 us  [moved(): return lax.ppermute(value, 'seq', route)]
    concatenate x0 -> x1, other arithmetic: none -> 1.06 us  [body(): kvd = jnp.concatenate([key_rows, values, d_layer], axis=1)]
  transfers between devices with their start and end apart: 15 -> 15, of which waited for: 8 -> 6; matrix products, arithmetic and copies ran while one was open for 0% -> 0% of each run, Pallas kernels for 4% -> 4%
where the time goes in v3:
time: 58 us; the launch traced here: 57.5 us
  starting transfers between devices  32 us (55%)
  waiting for transfers between devices  13.1 us (23%)
  Pallas kernels  9.84 us (17%)
  other arithmetic  1.14 us (2%)
  between operations  0.83 us (1%)
    ppermute x10, starting transfers between devices, moved(): return lax.ppermute(value, 'seq', route)  19.4 us
    pallas_call x8, Pallas kernels, call(): pl.pallas_call(kernel, out_shape=[jax.ShapeDtypeStruct(s, d) for s, d in...  9.84 us
    ppermute x4, starting transfers between devices, around(): return lax.ppermute(value, 'head', [((i + away) % 8, i) for i in range(8)])  8.33 us
    ppermute x10, waiting for transfers between devices, moved(): return lax.ppermute(value, 'seq', route)  7.87 us
    ppermute x1, starting transfers between devices, body(): across = lax.ppermute(across, ('seq', 'head'), far)  4.21 us
    ppermute x4, waiting for transfers between devices, around(): return lax.ppermute(value, 'head', [((i + away) % 8, i) for i in range(8)])  3.67 us
    ppermute x1, waiting for transfers between devices, body(): across = lax.ppermute(across, ('seq', 'head'), far)  1.61 us
  transfers between devices with their start and end apart: 15, of which 6 were waited for; matrix products, arithmetic and copies ran while one was open for 0% of the time, Pallas kernels for 4%

profile of v3, /device:TPU:2, one launch (start us, length us, event | category | flops | bytes accessed | tf_op | source)
XLA Modules:
  0.0 57.5 jit_solution(9318736412617809419)
XLA Ops:
  0.6 1.1 %pad_maximum_fusion.kvd_ref = bf16[256,768]{1,0:T(8,128)(2,1)S(1)} fusion(bf16[256,256]{1,0:T(8,128)(2,1)} %param.8, bf16[256,256]{1,0:T(8,128)(2,1)} %param.7, bf16[256,256]{1,0:T(8,128)(2,1)} %param.6), kind=kLoop, calls=%fused_computation | loop fusion | flops 1179648 | bytes 786432 | tf_op jit(solution)/shard_map/concatenate | solution.py:266
  1.7 0.0 copy-start.3
  1.7 0.3 shard_map.85
  2.0 0.1 collective-permute-start.4
  2.1 0.5 copy-done.3
  2.6 6.3 %collective-permute-start = (bf16[256,256]{1,0:T(8,128)(2,1)S(1)}, bf16[256,256]{1,0:T(8,128)(2,1)S(1)}, u32[]{:S(2)}, u32[]{:S(2)}) collective-permute-start(bf16[256,256]{1,0:T(8,128)(2,1)S(1)} %copy-done.3), channel_id=1, source_target_pairs={{2,0},{3,1},{4,2},{5,3},{6,4},{7,5},{0,6},{1,7},{10,8},{11,9},{12,... | collective-permute-start | bytes 393224 | tf_op jit(solution)/shard_map/ppermute | solution.py:262
  8.9 3.5 %collective-permute-start.7 = (bf16[256,512]{1,0:T(8,128)(2,1)S(1)}, bf16[256,512]{1,0:T(8,128)(2,1)S(1)}, u32[]{:S(2)}, u32[]{:S(2)}) collective-permute-start(bf16[256,512]{1,0:T(8,128)(2,1)S(1)} %get-tuple-element.30.kv_ref), channel_id=1, source_target_pairs={{0,64},{8,72},{16,80},{24,88},{32,96},{40,104},{48,112},{56,120},{... | collective-permute-start | bytes 786440 | tf_op jit(solution)/shard_map/ppermute | solution.py:255
  12.4 0.0 collective-permute-done.4.other_ref
  12.4 0.1 shard_map.87
  12.5 0.0 copy-start.2
  12.5 3.5 %collective-permute-start.5 = (bf16[6,128,128]{2,1,0:T(8,128)(2,1)S(1)}, bf16[6,128,128]{2,1,0:T(8,128)(2,1)S(1)}, u32[]{:S(2)}, u32[]{:S(2)}) collective-permute-start(bf16[6,128,128]{2,1,0:T(8,128)(2,1)S(1)} %shard_map.87), channel_id=1, source_target_pairs={{0,16},{16,32},{8,40},{32,48},{24,56},{48,64},{40,72},{64,80},{56,... | collective-permute-start | bytes 589832 | tf_op jit(solution)/shard_map/ppermute | solution.py:255
  16.0 4.2 %collective-permute-start.6 = (bf16[6,128,128]{2,1,0:T(8,128)(2,1)S(1)}, bf16[6,128,128]{2,1,0:T(8,128)(2,1)S(1)}, u32[]{:S(2)}, u32[]{:S(2)}) collective-permute-start(bf16[6,128,128]{2,1,0:T(8,128)(2,1)S(1)} %shard_map.87), channel_id=1, source_target_pairs={{0,48},{16,64},{32,80},{48,96},{64,112},{80,128},{96,144},{112,160... | collective-permute-start | bytes 589832 | tf_op jit(solution)/shard_map/ppermute | solution.py:255
  20.3 0.0 copy-start
  20.3 0.6 %shard_map.86 = (bf16[2,256,256]{2,1,0:T(8,128)(2,1)S(1)}, bf16[2,256,256]{2,1,0:T(8,128)(2,1)S(1)}, bf16[256,256]{1,0:T(8,128)(2,1)S(1)}, bf16[256,256]{1,0:T(8...) custom-call(bf16[256,256]{1,0:T(8,128)(2,1)S(1)} %get-tuple-element.26.d_ref, ...), custom_call_target="tpu_custom_call" | custom-call | flops 17179869184 | bytes 524288 | tf_op jit(solution)/shard_map/pallas_call | solution.py:49
  20.9 4.2 %collective-permute-start.8 = (bf16[256,256]{1,0:T(8,128)(2,1)S(1)}, bf16[256,256]{1,0:T(8,128)(2,1)S(1)}, u32[]{:S(2)}, u32[]{:S(2)}) collective-permute-start(bf16[256,256]{1,0:T(8,128)(2,1)S(1)} %get-tuple-element.35), channel_id=1, source_target_pairs={{2,0},{3,1},{4,2},{5,3},{6,4},{7,5},{0,6},{1,7},{14,8},{15,9},{8,1... | collective-permute-start | bytes 393224 | tf_op jit(solution)/shard_map/ppermute | solution.py:279
  25.1 2.0 %collective-permute-start.3 = (bf16[2,256,256]{2,1,0:T(8,128)(2,1)S(1)}, bf16[2,256,256]{2,1,0:T(8,128)(2,1)S(1)}, u32[]{:S(2)}, u32[]{:S(2)}) collective-permute-start(bf16[2,256,256]{2,1,0:T(8,128)(2,1)S(1)} %get-tuple-element.28), channel_id=1, source_target_pairs={{7,0},{0,1},{1,2},{2,3},{3,4},{4,5},{5,6},{6,7},{15,8},{8,9},{9,10... | collective-permute-start | bytes 786440 | tf_op jit(solution)/shard_map/ppermute | solution.py:262
  27.1 0.0 collective-permute-done.5.p1_ref
  27.1 0.3 shard_map.88
  27.4 1.6 %collective-permute-done.8.c_ref = bf16[256,256]{1,0:T(8,128)(2,1)S(1)} collective-permute-done((bf16[256,256]{1,0:T(8,128)(2,1)S(1)}, bf16[256,256]{1,0:T(8,128)(2,1)S(1)}, u32[]{:S(2)}, u32[]{:S(2)}) %collective-permute-start.8) | collective-permute-done | bytes 131104 | tf_op jit(solution)/shard_map/ppermute | solution.py:279
  29.0 3.1 %collective-permute-done.2.a_ref = bf16[2,256,256]{2,1,0:T(8,128)(2,1)S(1)} collective-permute-done((bf16[2,256,256]{2,1,0:T(8,128)(2,1)S(1)}, bf16[2,256,256]{2,1,0:T(8,128)(2,1)S(1)}, u32[]{:S(2)}, u32[]{:S(2)}) %collective-permute-start.2) | collective-permute-done | bytes 262176 | tf_op jit(solution)/shard_map/ppermute | solution.py:262
  32.2 0.5 collective-permute-done.3.b_ref
  32.7 5.9 %shard_map.89 = (f32[256,256]{1,0:T(8,128)}, bf16[256,512]{1,0:T(8,128)(2,1)S(1)}, f32[4,128,128]{2,1,0:T(8,128)S(1)}) custom-call(bf16[256,256]{1,0:T(8,128)(2,1)S(1)} %get-tuple-element.26.d_ref, bf16[256,256]{1,0:T(8,128)(2,1)S(1)} %collective-permute-done.up_ref, bf16[256,256]{1,0:T(8,128)(2,1)S(1)} %collective-permute-done.1.down_ref, ...), custom_call_target="tpu_custom_call" | custom-call | flops 4294967296 | bytes 524288 | tf_op jit(solution)/shard_map/pallas_call | solution.py:49
  38.6 1.5 %collective-permute-done.10.other_ref = f32[4,128,128]{2,1,0:T(8,128)S(1)} collective-permute-done((f32[4,128,128]{2,1,0:T(8,128)S(1)}, f32[4,128,128]{2,1,0:T(8,128)S(1)}, u32[]{:S(2)}, u32[]{:S(2)}) %collective-permute-start.10) | collective-permute-done | bytes 262176 | tf_op jit(solution)/shard_map/ppermute | solution.py:255
  40.2 4.0 %collective-permute-start.11 = (bf16[4,128,128]{2,1,0:T(8,128)(2,1)S(1)}, bf16[4,128,128]{2,1,0:T(8,128)(2,1)S(1)}, u32[]{:S(2)}, u32[]{:S(2)}) collective-permute-start(bf16[4,128,128]{2,1,0:T(8,128)(2,1)S(1)} %add_convert_fusion), channel_id=1, source_target_pairs={{16,0},{40,8},{32,16},{56,24},{48,32},{72,40},{64,48},{88,56},{80,... | collective-permute-start | bytes 393224 | tf_op jit(solution)/shard_map/ppermute | solution.py:255
  44.2 2.1 %collective-permute-start.12 = (bf16[4,128,128]{2,1,0:T(8,128)(2,1)S(1)}, bf16[4,128,128]{2,1,0:T(8,128)(2,1)S(1)}, u32[]{:S(2)}, u32[]{:S(2)}) collective-permute-start(bf16[4,128,128]{2,1,0:T(8,128)(2,1)S(1)} %add_convert_fusion), channel_id=1, source_target_pairs={{48,0},{64,16},{80,32},{96,48},{112,64},{128,80},{144,96},{160,112... | collective-permute-start | bytes 393224 | tf_op jit(solution)/shard_map/ppermute | solution.py:255
  46.3 0.8 %shard_map.90 = bf16[256,512]{1,0:T(8,128)(2,1)S(1)} custom-call(bf16[256,512]{1,0:T(8,128)(2,1)S(1)} %collective-permute-done.7.lag_ref, bf16[256,256]{1,0:T(8,128)(2,1)S(1)} %get-tuple-element.37.xb_ref, bf16[256,512]{1,0:T(8,128)(2,1)S(1)} %get-tuple-element.44.yo_ref, f32[4,128,128]{2,1,0:T(8,128)S(1)} %collective-permute-done.10.other_ref), custom_call_target="tpu_custom_call" | custom-call | flops 67108864 | bytes 524288 | tf_op jit(solution)/shard_map/pallas_call | solution.py:49
  47.1 1.9 %collective-permute-start.14 = (bf16[256,512]{1,0:T(8,128)(2,1)S(1)}, bf16[256,512]{1,0:T(8,128)(2,1)S(1)}, u32[]{:S(2)}, u32[]{:S(2)}) collective-permute-start(bf16[256,512]{1,0:T(8,128)(2,1)S(1)} %shard_map.90), channel_id=1, source_target_pairs={{64,0},{72,8},{80,16},{88,24},{96,32},{104,40},{112,48},{120,56},{... | collective-permute-start | bytes 786440 | tf_op jit(solution)/shard_map/ppermute | solution.py:255
  49.1 3.2 %collective-permute-done.12 = bf16[4,128,128]{2,1,0:T(8,128)(2,1)S(1)} collective-permute-done((bf16[4,128,128]{2,1,0:T(8,128)(2,1)S(1)}, bf16[4,128,128]{2,1,0:T(8,128)(2,1)S(1)}, u32[]{:S(2)}, u32[]{:S(2)}) %collective-permute-start.12) | collective-permute-done | bytes 131104 | tf_op jit(solution)/shard_map/ppermute | solution.py:255
  52.3 0.1 collective-permute-start.13
  52.4 0.7 %shard_map.91 = (f32[256,256]{1,0:T(8,128)S(1)}, f32[256,256]{1,0:T(8,128)S(1)}) custom-call(bf16[256,512]{1,0:T(8,128)(2,1)S(1)} %get-tuple-element.30.kv_ref, bf16[256,256]{1,0:T(8,128)(2,1)S(1)} %get-tuple-element.37.xb_ref, bf16[256,512]{1,0:T(8,128)(2,1)S(1)} %get-tuple-element.44.yo_ref), custom_call_target="tpu_custom_call" | custom-call | flops 67108864 | bytes 524288 | tf_op jit(solution)/shard_map/pallas_call | solution.py:49
  53.2 3.1 %collective-permute-done.14.early_ref = bf16[256,512]{1,0:T(8,128)(2,1)S(1)} collective-permute-done((bf16[256,512]{1,0:T(8,128)(2,1)S(1)}, bf16[256,512]{1,0:T(8,128)(2,1)S(1)}, u32[]{:S(2)}, u32[]{:S(2)}) %collective-permute-start.14) | collective-permute-done | bytes 262176 | tf_op jit(solution)/shard_map/ppermute | solution.py:255
  56.3 1.1 %shard_map.92 = (f32[256,256]{1,0:T(8,128)}, f32[256,256]{1,0:T(8,128)}) custom-call(bf16[256,512]{1,0:T(8,128)(2,1)S(1)} %get-tuple-element.30.kv_ref, f32[4,128,128]{2,1,0:T(8,128)S(1)} %get-tuple-element.50.part_ref, f32[4,128,128]{2,1,0:T(8,128)S(1)} %collective-permute-done.13.recv_ref, bf16[256,512]{1,0:T(8,128)(2,1)S(1)} %collective-permute-done.14.early_ref, ...), custom_call_target="tpu_custom_call" | custom-call | bytes 524288 | tf_op jit(solution)/shard_map/pallas_call | solution.py:49
  (17 shorter events, 0.1 us)
Async XLA Ops:
  1.7 0.9 %copy-start.3 = (bf16[256,256]{1,0:T(8,128)(2,1)S(1)}, bf16[256,256]{1,0:T(8,128)(2,1)}, u32[]{:S(2)}) copy-start(bf16[256,256]{1,0:T(8,128)(2,1)} %param.8) | copy-start | bytes 393220
  2.0 10.5 %collective-permute-start.4 = (f32[4,128,128]{2,1,0:T(8,128)S(1)}, f32[4,128,128]{2,1,0:T(8,128)S(1)}, u32[]{:S(2)}, u32[]{:S(2)}) collective-permute-start(f32[4,128,128]{2,1,0:T(8,128)S(1)} %get-tuple-element.29.own_ref.t_ref), channel_id=1, source_target_pairs={{8,0},{0,8},{24,16},{16,24},{40,32},{32,40},{56,48},{48,56},{72,64... | collective-permute-start | bytes 786440 | tf_op jit(solution)/shard_map/ppermute | solution.py:255
  2.6 17.6 %collective-permute-start = (bf16[256,256]{1,0:T(8,128)(2,1)S(1)}, bf16[256,256]{1,0:T(8,128)(2,1)S(1)}, u32[]{:S(2)}, u32[]{:S(2)}) collective-permute-start(bf16[256,256]{1,0:T(8,128)(2,1)S(1)} %copy-done.3), channel_id=1, source_target_pairs={{2,0},{3,1},{4,2},{5,3},{6,4},{7,5},{0,6},{1,7},{10,8},{11,9},{12,... | collective-permute-start | bytes 393224 | tf_op jit(solution)/shard_map/ppermute | solution.py:262
  8.9 11.3 %collective-permute-start.1 = (bf16[256,256]{1,0:T(8,128)(2,1)S(1)}, bf16[256,256]{1,0:T(8,128)(2,1)S(1)}, u32[]{:S(2)}, u32[]{:S(2)}) collective-permute-start(bf16[256,256]{1,0:T(8,128)(2,1)S(1)} %copy-done.3), channel_id=1, source_target_pairs={{6,0},{7,1},{0,2},{1,3},{2,4},{3,5},{4,6},{5,7},{14,8},{15,9},{8,1... | collective-permute-start | bytes 393224 | tf_op jit(solution)/shard_map/ppermute | solution.py:262
  8.9 11.3 %copy-start.1 = (f32[256,256]{1,0:T(8,128)S(1)}, f32[256,256]{1,0:T(8,128)}, u32[]{:S(2)}) copy-start(f32[256,256]{1,0:T(8,128)} %x_ref.1) | copy-start | bytes 786436
  8.9 16.2 %collective-permute-start.7 = (bf16[256,512]{1,0:T(8,128)(2,1)S(1)}, bf16[256,512]{1,0:T(8,128)(2,1)S(1)}, u32[]{:S(2)}, u32[]{:S(2)}) collective-permute-start(bf16[256,512]{1,0:T(8,128)(2,1)S(1)} %get-tuple-element.30.kv_ref), channel_id=1, source_target_pairs={{0,64},{8,72},{16,80},{24,88},{32,96},{40,104},{48,112},{56,120},{... | collective-permute-start | bytes 786440 | tf_op jit(solution)/shard_map/ppermute | solution.py:255
  12.5 7.7 %copy-start.2 = (f32[2]{0:T(128)S(1)}, f32[2]{0:T(128)}, u32[]{:S(2)}) copy-start(f32[2]{0:T(128)} %ridge_ref.1) | copy-start | bytes 28
  12.5 14.6 %collective-permute-start.5 = (bf16[6,128,128]{2,1,0:T(8,128)(2,1)S(1)}, bf16[6,128,128]{2,1,0:T(8,128)(2,1)S(1)}, u32[]{:S(2)}, u32[]{:S(2)}) collective-permute-start(bf16[6,128,128]{2,1,0:T(8,128)(2,1)S(1)} %shard_map.87), channel_id=1, source_target_pairs={{0,16},{16,32},{8,40},{32,48},{24,56},{48,64},{40,72},{64,80},{56,... | collective-permute-start | bytes 589832 | tf_op jit(solution)/shard_map/ppermute | solution.py:255
  16.0 11.1 %collective-permute-start.6 = (bf16[6,128,128]{2,1,0:T(8,128)(2,1)S(1)}, bf16[6,128,128]{2,1,0:T(8,128)(2,1)S(1)}, u32[]{:S(2)}, u32[]{:S(2)}) collective-permute-start(bf16[6,128,128]{2,1,0:T(8,128)(2,1)S(1)} %shard_map.87), channel_id=1, source_target_pairs={{0,48},{16,64},{32,80},{48,96},{64,112},{80,128},{96,144},{112,160... | collective-permute-start | bytes 589832 | tf_op jit(solution)/shard_map/ppermute | solution.py:255
  20.3 12.5 %copy-start = (bf16[256,2048]{1,0:T(8,128)(2,1)S(1)}, bf16[256,2048]{1,0:T(8,128)(2,1)}, u32[]{:S(2)}) copy-start(bf16[256,2048]{1,0:T(8,128)(2,1)} %w_ref.1) | copy-start | bytes 3145732
  20.9 8.1 %collective-permute-start.8 = (bf16[256,256]{1,0:T(8,128)(2,1)S(1)}, bf16[256,256]{1,0:T(8,128)(2,1)S(1)}, u32[]{:S(2)}, u32[]{:S(2)}) collective-permute-start(bf16[256,256]{1,0:T(8,128)(2,1)S(1)} %get-tuple-element.35), channel_id=1, source_target_pairs={{2,0},{3,1},{4,2},{5,3},{6,4},{7,5},{0,6},{1,7},{14,8},{15,9},{8,1... | collective-permute-start | bytes 393224 | tf_op jit(solution)/shard_map/ppermute | solution.py:279
  25.1 7.1 %collective-permute-start.2 = (bf16[2,256,256]{2,1,0:T(8,128)(2,1)S(1)}, bf16[2,256,256]{2,1,0:T(8,128)(2,1)S(1)}, u32[]{:S(2)}, u32[]{:S(2)}) collective-permute-start(bf16[2,256,256]{2,1,0:T(8,128)(2,1)S(1)} %get-tuple-element.27), channel_id=1, source_target_pairs={{1,0},{2,1},{3,2},{4,3},{5,4},{6,5},{7,6},{0,7},{9,8},{10,9},{11,1... | collective-permute-start | bytes 786440 | tf_op jit(solution)/shard_map/ppermute | solution.py:262
  25.1 7.6 %collective-permute-start.3 = (bf16[2,256,256]{2,1,0:T(8,128)(2,1)S(1)}, bf16[2,256,256]{2,1,0:T(8,128)(2,1)S(1)}, u32[]{:S(2)}, u32[]{:S(2)}) collective-permute-start(bf16[2,256,256]{2,1,0:T(8,128)(2,1)S(1)} %get-tuple-element.28), channel_id=1, source_target_pairs={{7,0},{0,1},{1,2},{2,3},{3,4},{4,5},{5,6},{6,7},{15,8},{8,9},{9,10... | collective-permute-start | bytes 786440 | tf_op jit(solution)/shard_map/ppermute | solution.py:262
  29.0 3.7 %collective-permute-start.9 = (f32[4,128,128]{2,1,0:T(8,128)S(1)}, f32[4,128,128]{2,1,0:T(8,128)S(1)}, u32[]{:S(2)}, u32[]{:S(2)}) collective-permute-start(f32[4,128,128]{2,1,0:T(8,128)S(1)} %get-tuple-element.40), channel_id=1, source_target_pairs={{8,0},{0,8},{24,16},{16,24},{40,32},{32,40},{56,48},{48,56},{72,64... | collective-permute-start | bytes 786440 | tf_op jit(solution)/shard_map/ppermute | solution.py:255
  38.6 1.5 %collective-permute-start.10 = (f32[4,128,128]{2,1,0:T(8,128)S(1)}, f32[4,128,128]{2,1,0:T(8,128)S(1)}, u32[]{:S(2)}, u32[]{:S(2)}) collective-permute-start(f32[4,128,128]{2,1,0:T(8,128)S(1)} %get-tuple-element.43), channel_id=1, source_target_pairs={{8,0},{0,8},{24,16},{16,24},{40,32},{32,40},{56,48},{48,56},{72,64... | collective-permute-start | bytes 786440 | tf_op jit(solution)/shard_map/ppermute | solution.py:255
  40.2 8.9 %collective-permute-start.11 = (bf16[4,128,128]{2,1,0:T(8,128)(2,1)S(1)}, bf16[4,128,128]{2,1,0:T(8,128)(2,1)S(1)}, u32[]{:S(2)}, u32[]{:S(2)}) collective-permute-start(bf16[4,128,128]{2,1,0:T(8,128)(2,1)S(1)} %add_convert_fusion), channel_id=1, source_target_pairs={{16,0},{40,8},{32,16},{56,24},{48,32},{72,40},{64,48},{88,56},{80,... | collective-permute-start | bytes 393224 | tf_op jit(solution)/shard_map/ppermute | solution.py:255
  44.2 8.1 %collective-permute-start.12 = (bf16[4,128,128]{2,1,0:T(8,128)(2,1)S(1)}, bf16[4,128,128]{2,1,0:T(8,128)(2,1)S(1)}, u32[]{:S(2)}, u32[]{:S(2)}) collective-permute-start(bf16[4,128,128]{2,1,0:T(8,128)(2,1)S(1)} %add_convert_fusion), channel_id=1, source_target_pairs={{48,0},{64,16},{80,32},{96,48},{112,64},{128,80},{144,96},{160,112... | collective-permute-start | bytes 393224 | tf_op jit(solution)/shard_map/ppermute | solution.py:255
  47.1 9.2 %collective-permute-start.14 = (bf16[256,512]{1,0:T(8,128)(2,1)S(1)}, bf16[256,512]{1,0:T(8,128)(2,1)S(1)}, u32[]{:S(2)}, u32[]{:S(2)}) collective-permute-start(bf16[256,512]{1,0:T(8,128)(2,1)S(1)} %shard_map.90), channel_id=1, source_target_pairs={{64,0},{72,8},{80,16},{88,24},{96,32},{104,40},{112,48},{120,56},{... | collective-permute-start | bytes 786440 | tf_op jit(solution)/shard_map/ppermute | solution.py:255
  52.3 4.0 %collective-permute-start.13 = (f32[4,128,128]{2,1,0:T(8,128)S(1)}, f32[4,128,128]{2,1,0:T(8,128)S(1)}, u32[]{:S(2)}, u32[]{:S(2)}) collective-permute-start(f32[4,128,128]{2,1,0:T(8,128)S(1)} %get-tuple-element.49), channel_id=1, source_target_pairs={{8,0},{0,8},{24,16},{16,24},{40,32},{32,40},{56,48},{48,56},{72,64... | collective-permute-start | bytes 786440 | tf_op jit(solution)/shard_map/ppermute | solution.py:255

commit v4 on v3

--- a/solution.py
+++ b/solution.py
@@ -65,16 +65,23 @@
     dv_ref[...] = kvd_ref[:, 512:]
 
 
-def to_forward(d_ref, up_ref, down_ref, x_ref, ridge_ref, a_ref, b_ref, c_ref, xb_ref, xlo_ref, rid_ref):
+def to_forward(d_ref, up_ref, down_ref, a_ref, b_ref, c_ref):
     core = lax.rem(lax.axis_index("seq"), 2)
     a_ref[0] = d_ref[...]
     a_ref[1] = up_ref[...]
     b_ref[0] = d_ref[...]
     b_ref[1] = down_ref[...]
     c_ref[...] = jnp.where(core == 0, up_ref[...], down_ref[...])
-    xb_ref[...], xlo_ref[...] = split(x_ref[...])
-    for h in range(NH):
-        rid_ref[h] = jnp.full((8, DH), ridge_ref[h], F32)
+
+
+def weight_part(w_ref, away):
+    start = pl.multiple_of(lax.rem(lax.axis_index("head") + away, 8) * 256, 256)
+    return w_ref[:, pl.ds(start, 256)]
+
+
+def halves(ref, h, base=0):
+    whole = head(ref, h, base)
+    return whole[:DH], whole[DH:]
 
 
 def chip_states(own_ref, other_ref, out_ref):
@@ -85,7 +92,10 @@
         out_ref[2 * NH + h] = lo
 
 
-def states_to_send(t_ref, lag_ref, p1_ref, p2_ref, part_ref, send_ref):
+def states_to_send(
+    t_ref, lag_ref, p1_ref, p2_ref, kv_ref, d_ref, up_ref, down_ref, w_ref, x_ref, ridge_ref,
+    part_ref, send_ref, out_ref, turned_ref, near_ref, xb_ref, xlo_ref, rid_ref,
+):
     core = lax.rem(lax.axis_index("seq"), 2)
     for h in range(NH):
         k = head(lag_ref, h)
@@ -97,21 +107,29 @@
         for at, lag, part in ((h, lag_g, gram), (NH + h, lag_s, state)):
             part_ref[at] = part
             send_ref[at] = part + jnp.where(core == 0, t_ref[at], lag)
+    out = mm_nt(d_ref[...], weight_part(w_ref, 0)) + mm_nt(up_ref[...], weight_part(w_ref, 2))
+    out_ref[...] = out + mm_nt(down_ref[...], weight_part(w_ref, 6))
+    for h in range(NH):
+        keys, lags = halves(kv_ref, h), halves(lag_ref, h)
+        for b in range(2):
+            turned_ref[2 * h + b, :, :DH] = keys[b].astype(F32).T.astype(BF16)
+            turned_ref[2 * h + b, :, DH:] = lags[b].astype(F32).T.astype(BF16)
+        near_ref[4 * h] = mm_tn(lags[1], lags[1])
+        near_ref[4 * h + 1] = mm_tn(keys[0], keys[0])
+        near_ref[4 * h + 2] = mm_tn(halves(lag_ref, h, 256)[1], lags[1])
+        near_ref[4 * h + 3] = mm_tn(halves(kv_ref, h, 256)[0], keys[0])
+        rid_ref[h] = jnp.full((8, DH), ridge_ref[h], F32)
+    xb_ref[...], xlo_ref[...] = split(x_ref[...])
 
 
 def adjoints(
-    d_ref, up_ref, down_ref, a_ref, b_ref, c_ref, w_ref, kv_ref, lag_ref, xb_ref, xlo_ref, part_ref, recv_ref, rid_ref,
-    y_ref, yo_ref, t_ref,
+    a_ref, b_ref, c_ref, w_ref, kv_ref, lag_ref, xb_ref, xlo_ref, part_ref, recv_ref, rid_ref, out_ref, turned_ref,
+    near_ref, y_ref, yo_ref, t_ref,
 ):
     B = 128
-    here = lax.axis_index("head")
-    out = jnp.zeros((TOK, 256), F32)
-    for away, chunk in (
-        (0, d_ref[...]), (2, up_ref[...]), (6, down_ref[...]), (1, a_ref[0]),
-        (3, a_ref[1]), (7, b_ref[0]), (5, b_ref[1]), (4, c_ref[...]),
-    ):
-        start = pl.multiple_of(lax.rem(here + away, 8) * 256, 256)
-        out = out + mm_nt(chunk, w_ref[:, pl.ds(start, 256)])
+    out = out_ref[...]
+    for away, chunk in ((4, c_ref[...]), (1, a_ref[0]), (3, a_ref[1]), (7, b_ref[0]), (5, b_ref[1])):
+        out = out + mm_nt(chunk, weight_part(w_ref, away))
     out = out.astype(BF16)
     yo_ref[:, 256:] = out
     rows, cols = tri(B, B)
@@ -128,13 +146,10 @@
             kb, vb = k[b * B : (b + 1) * B], v[b * B : (b + 1) * B]
             klb, vlb = kl[b * B : (b + 1) * B], vl[b * B : (b + 1) * B]
             ob = o[b * B : (b + 1) * B]
-            kf, vf = (kl[B:], vl[B:]) if b == 0 else (k[:B], v[:B])
-            g = gram + mm_tn(kf, kf)
-            s = state + mm_tn(vf, kf)
+            g = gram + near_ref[4 * h + b]
+            s = state + near_ref[4 * h + 2 + b]
             g_hi, g_lo = split(g)
-            kbt = kb.astype(F32).T.astype(BF16)
-            klbt = klb.astype(F32).T.astype(BF16)
-            half = jnp.concatenate([g_hi, kbt, klbt, g_lo], axis=1)
+            half = jnp.concatenate([g_hi, turned_ref[2 * h + b], g_lo], axis=1)
             rhs.append(jnp.concatenate([half, half], axis=0))
             both = jnp.concatenate([kb, klb], axis=0)
             keys.append(jnp.concatenate([both, both], axis=0))
@@ -268,9 +283,8 @@
     kv_lag = moved(kv, lambda i: i - lag)
     (chip,) = call(chip_states, [((3 * NH, DH, DH), BF16)], own, swapped(own))
     pair = (2, TOK, 256)
-    up_two, down_two, across, xb, xlo, rid = call(
-        to_forward, [(pair, BF16), (pair, BF16), flat, flat, flat, ((NH, 8, DH), F32)],
-        dv, up, down, saved_solutions, ridge_scale, flops=1 << 34, smem=(4,),
+    up_two, down_two, across = call(
+        to_forward, [(pair, BF16), (pair, BF16), flat], dv, up, down, flops=1 << 34
     )
     up_two, down_two = around(up_two, 1), around(down_two, -1)
     far = [
@@ -280,14 +294,21 @@
     p1 = moved(chip, lambda i: i - 2 if i % 2 == 0 else i - 4)
     p2 = moved(chip, lambda i: i - 6 if i % 2 == 0 else None)
     p1, p2, kv_lag = lax.optimization_barrier((p1, p2, kv_lag))
-    part, send = call(states_to_send, [(st, F32), (st, F32)], own, kv_lag, p1, p2, size=0)
+    part, send, begun, turned, near, xb, xlo, rid = call(
+        states_to_send,
+        [
+            (st, F32), (st, F32), ((TOK, 256), F32), ((4, DH, 256), BF16), ((8, DH, DH), F32), flat, flat,
+            ((NH, 8, DH), F32),
+        ],
+        own, kv_lag, p1, p2, kv, dv, up, down, out_weight, saved_solutions, ridge_scale, size=0, smem=(10,),
+    )
     send, across = lax.optimization_barrier((send, across))
     recv = swapped(send)
 
     y, yo, tl = call(
         adjoints,
         [((TOK, 256), F32), ((TOK, 512), BF16), (st, F32)],
-        dv, up, down, up_two, down_two, across, out_weight, kv, kv_lag, xb, xlo, part, recv, rid,
+        up_two, down_two, across, out_weight, kv, kv_lag, xb, xlo, part, recv, rid, begun, turned, near,
         flops=1 << 32,
     )
 

time: 58 us -> 56.9 us (0.981)
  waiting for transfers between devices: 13.1 us -> 12.5 us
    ppermute x1, waiting for transfers between devices: 1.61 us -> 0.81 us  [body(): across = lax.ppermute(across, ('seq', 'head'), far)]
  transfers between devices with their start and end apart: 15 -> 15, of which waited for: 6 -> 6; matrix products, arithmetic and copies ran while one was open for 0% -> 0% of each run, Pallas kernels for 4% -> 5%
where the time goes in v4:
time: 56.9 us; the launch traced here: 56.6 us
  starting transfers between devices  31.8 us (56%)
  waiting for transfers between devices  12.5 us (22%)
  Pallas kernels  9.78 us (17%)
  other arithmetic  1.14 us (2%)
  between operations  0.84 us (1%)
    ppermute x10, starting transfers between devices, moved(): return lax.ppermute(value, 'seq', route)  19.3 us
    pallas_call x8, Pallas kernels, call(): pl.pallas_call(kernel, out_shape=[jax.ShapeDtypeStruct(s, d) for s, d in...  9.78 us
    ppermute x4, starting transfers between devices, around(): return lax.ppermute(value, 'head', [((i + away) % 8, i) for i in range(8)])  8.33 us
    ppermute x10, waiting for transfers between devices, moved(): return lax.ppermute(value, 'seq', route)  7.91 us
    ppermute x1, starting transfers between devices, body(): across = lax.ppermute(across, ('seq', 'head'), far)  4.21 us
    ppermute x4, waiting for transfers between devices, around(): return lax.ppermute(value, 'head', [((i + away) % 8, i) for i in range(8)])  3.75 us
  transfers between devices with their start and end apart: 15, of which 6 were waited for; matrix products, arithmetic and copies ran while one was open for 0% of the time, Pallas kernels for 5%

profile of v4, /device:TPU:2, one launch (start us, length us, event | category | flops | bytes accessed | tf_op | source)
XLA Modules:
  0.0 56.6 jit_solution(3471126267752845560)
XLA Ops:
  0.6 1.1 %pad_maximum_fusion.kvd_ref = bf16[256,768]{1,0:T(8,128)(2,1)S(1)} fusion(bf16[256,256]{1,0:T(8,128)(2,1)} %param.8, bf16[256,256]{1,0:T(8,128)(2,1)} %param.7, bf16[256,256]{1,0:T(8,128)(2,1)} %param.6), kind=kLoop, calls=%fused_computation | loop fusion | flops 1179648 | bytes 786432 | tf_op jit(solution)/shard_map/concatenate | solution.py:281
  1.7 0.0 copy-start.3
  1.7 0.3 shard_map.85
  2.0 0.1 collective-permute-start.4
  2.1 0.5 copy-done.3
  2.6 6.3 %collective-permute-start = (bf16[256,256]{1,0:T(8,128)(2,1)S(1)}, bf16[256,256]{1,0:T(8,128)(2,1)S(1)}, u32[]{:S(2)}, u32[]{:S(2)}) collective-permute-start(bf16[256,256]{1,0:T(8,128)(2,1)S(1)} %copy-done.3), channel_id=1, source_target_pairs={{2,0},{3,1},{4,2},{5,3},{6,4},{7,5},{0,6},{1,7},{10,8},{11,9},{12,... | collective-permute-start | bytes 393224 | tf_op jit(solution)/shard_map/ppermute | solution.py:277
  8.9 3.4 %collective-permute-start.7 = (bf16[256,512]{1,0:T(8,128)(2,1)S(1)}, bf16[256,512]{1,0:T(8,128)(2,1)S(1)}, u32[]{:S(2)}, u32[]{:S(2)}) collective-permute-start(bf16[256,512]{1,0:T(8,128)(2,1)S(1)} %get-tuple-element.33.kv_ref), channel_id=1, source_target_pairs={{0,64},{8,72},{16,80},{24,88},{32,96},{40,104},{48,112},{56,120},{... | collective-permute-start | bytes 786440 | tf_op jit(solution)/shard_map/ppermute | solution.py:270
  12.4 3.5 %collective-permute-start.5 = (bf16[6,128,128]{2,1,0:T(8,128)(2,1)S(1)}, bf16[6,128,128]{2,1,0:T(8,128)(2,1)S(1)}, u32[]{:S(2)}, u32[]{:S(2)}) collective-permute-start(bf16[6,128,128]{2,1,0:T(8,128)(2,1)S(1)} %shard_map.87), channel_id=1, source_target_pairs={{0,16},{16,32},{8,40},{32,48},{24,56},{48,64},{40,72},{64,80},{56,... | collective-permute-start | bytes 589832 | tf_op jit(solution)/shard_map/ppermute | solution.py:270
  15.8 4.2 %collective-permute-start.6 = (bf16[6,128,128]{2,1,0:T(8,128)(2,1)S(1)}, bf16[6,128,128]{2,1,0:T(8,128)(2,1)S(1)}, u32[]{:S(2)}, u32[]{:S(2)}) collective-permute-start(bf16[6,128,128]{2,1,0:T(8,128)(2,1)S(1)} %shard_map.87), channel_id=1, source_target_pairs={{0,48},{16,64},{32,80},{48,96},{64,112},{80,128},{96,144},{112,160... | collective-permute-start | bytes 589832 | tf_op jit(solution)/shard_map/ppermute | solution.py:270
  20.1 0.0 collective-permute-done.up_ref
  20.1 0.0 collective-permute-done.1.down_ref
  20.1 0.0 copy-start
  20.1 0.0 copy-start.1
  20.1 0.1 shard_map.86
  20.2 4.2 %collective-permute-start.8 = (bf16[256,256]{1,0:T(8,128)(2,1)S(1)}, bf16[256,256]{1,0:T(8,128)(2,1)S(1)}, u32[]{:S(2)}, u32[]{:S(2)}) collective-permute-start(bf16[256,256]{1,0:T(8,128)(2,1)S(1)} %get-tuple-element.38), channel_id=1, source_target_pairs={{2,0},{3,1},{4,2},{5,3},{6,4},{7,5},{0,6},{1,7},{14,8},{15,9},{8,1... | collective-permute-start | bytes 393224 | tf_op jit(solution)/shard_map/ppermute | solution.py:293
  24.4 0.0 collective-permute-start.2
  24.4 2.0 %collective-permute-start.3 = (bf16[2,256,256]{2,1,0:T(8,128)(2,1)S(1)}, bf16[2,256,256]{2,1,0:T(8,128)(2,1)S(1)}, u32[]{:S(2)}, u32[]{:S(2)}) collective-permute-start(bf16[2,256,256]{2,1,0:T(8,128)(2,1)S(1)} %get-tuple-element.31), channel_id=1, source_target_pairs={{7,0},{0,1},{1,2},{2,3},{3,4},{4,5},{5,6},{6,7},{15,8},{8,9},{9,10... | collective-permute-start | bytes 786440 | tf_op jit(solution)/shard_map/ppermute | solution.py:277
  26.4 1.0 %shard_map.88 = (f32[4,128,128]{2,1,0:T(8,128)S(1)}, f32[4,128,128]{2,1,0:T(8,128)S(1)}, f32[256,256]{1,0:T(8,128)S(1)}, bf16[4,128,256]{2,1,0:T(8,128)(2,1)S(1)...) custom-call(f32[4,128,128]{2,1,0:T(8,128)S(1)} %get-tuple-element.32, ...), custom_call_target="tpu_custom_call" | custom-call | tf_op jit(solution)/shard_map/pallas_call | solution.py:49
  27.5 0.8 %collective-permute-done.8.c_ref = bf16[256,256]{1,0:T(8,128)(2,1)S(1)} collective-permute-done((bf16[256,256]{1,0:T(8,128)(2,1)S(1)}, bf16[256,256]{1,0:T(8,128)(2,1)S(1)}, u32[]{:S(2)}, u32[]{:S(2)}) %collective-permute-start.8) | collective-permute-done | bytes 131104 | tf_op jit(solution)/shard_map/ppermute | solution.py:293
  28.3 3.1 %collective-permute-done.2.a_ref = bf16[2,256,256]{2,1,0:T(8,128)(2,1)S(1)} collective-permute-done((bf16[2,256,256]{2,1,0:T(8,128)(2,1)S(1)}, bf16[2,256,256]{2,1,0:T(8,128)(2,1)S(1)}, u32[]{:S(2)}, u32[]{:S(2)}) %collective-permute-start.2) | collective-permute-done | bytes 262176 | tf_op jit(solution)/shard_map/ppermute | solution.py:277
  31.4 0.6 %collective-permute-done.3.b_ref = bf16[2,256,256]{2,1,0:T(8,128)(2,1)S(1)} collective-permute-done((bf16[2,256,256]{2,1,0:T(8,128)(2,1)S(1)}, bf16[2,256,256]{2,1,0:T(8,128)(2,1)S(1)}, u32[]{:S(2)}, u32[]{:S(2)}) %collective-permute-start.3) | collective-permute-done | bytes 262176 | tf_op jit(solution)/shard_map/ppermute | solution.py:277
  32.0 5.7 %shard_map.89 = (f32[256,256]{1,0:T(8,128)}, bf16[256,512]{1,0:T(8,128)(2,1)S(1)}, f32[4,128,128]{2,1,0:T(8,128)S(1)}) custom-call(bf16[2,256,256]{2,1,0:T(8,128)(2,1)S(1)} %collective-permute-done.2.a_ref, bf16[2,256,256]{2,1,0:T(8,128)(2,1)S(1)} %collective-permute-done.3.b_ref, bf16[256,256]{1,0:T(8,128)(2,1)S(1)} %collective-permute-done.8.c_ref, ...), custom_call_target="tpu_custom_call" | custom-call | flops 4294967296 | bytes 524288 | tf_op jit(solution)/shard_map/pallas_call | solution.py:49
  37.7 1.5 %collective-permute-done.10.other_ref = f32[4,128,128]{2,1,0:T(8,128)S(1)} collective-permute-done((f32[4,128,128]{2,1,0:T(8,128)S(1)}, f32[4,128,128]{2,1,0:T(8,128)S(1)}, u32[]{:S(2)}, u32[]{:S(2)}) %collective-permute-start.10) | collective-permute-done | bytes 262176 | tf_op jit(solution)/shard_map/ppermute | solution.py:270
  39.3 4.0 %collective-permute-start.11 = (bf16[4,128,128]{2,1,0:T(8,128)(2,1)S(1)}, bf16[4,128,128]{2,1,0:T(8,128)(2,1)S(1)}, u32[]{:S(2)}, u32[]{:S(2)}) collective-permute-start(bf16[4,128,128]{2,1,0:T(8,128)(2,1)S(1)} %add_convert_fusion), channel_id=1, source_target_pairs={{16,0},{40,8},{32,16},{56,24},{48,32},{72,40},{64,48},{88,56},{80,... | collective-permute-start | bytes 393224 | tf_op jit(solution)/shard_map/ppermute | solution.py:270
  43.3 2.1 %collective-permute-start.12 = (bf16[4,128,128]{2,1,0:T(8,128)(2,1)S(1)}, bf16[4,128,128]{2,1,0:T(8,128)(2,1)S(1)}, u32[]{:S(2)}, u32[]{:S(2)}) collective-permute-start(bf16[4,128,128]{2,1,0:T(8,128)(2,1)S(1)} %add_convert_fusion), channel_id=1, source_target_pairs={{48,0},{64,16},{80,32},{96,48},{112,64},{128,80},{144,96},{160,112... | collective-permute-start | bytes 393224 | tf_op jit(solution)/shard_map/ppermute | solution.py:270
  45.4 0.8 %shard_map.90 = bf16[256,512]{1,0:T(8,128)(2,1)S(1)} custom-call(bf16[256,512]{1,0:T(8,128)(2,1)S(1)} %collective-permute-done.7.lag_ref, bf16[256,256]{1,0:T(8,128)(2,1)S(1)} %get-tuple-element.40.xb_ref, bf16[256,512]{1,0:T(8,128)(2,1)S(1)} %get-tuple-element.50.yo_ref, f32[4,128,128]{2,1,0:T(8,128)S(1)} %collective-permute-done.10.other_ref), custom_call_target="tpu_custom_call" | custom-call | flops 67108864 | bytes 524288 | tf_op jit(solution)/shard_map/pallas_call | solution.py:49
  46.2 1.9 %collective-permute-start.14 = (bf16[256,512]{1,0:T(8,128)(2,1)S(1)}, bf16[256,512]{1,0:T(8,128)(2,1)S(1)}, u32[]{:S(2)}, u32[]{:S(2)}) collective-permute-start(bf16[256,512]{1,0:T(8,128)(2,1)S(1)} %shard_map.90), channel_id=1, source_target_pairs={{64,0},{72,8},{80,16},{88,24},{96,32},{104,40},{112,48},{120,56},{... | collective-permute-start | bytes 786440 | tf_op jit(solution)/shard_map/ppermute | solution.py:270
  48.2 3.2 %collective-permute-done.12 = bf16[4,128,128]{2,1,0:T(8,128)(2,1)S(1)} collective-permute-done((bf16[4,128,128]{2,1,0:T(8,128)(2,1)S(1)}, bf16[4,128,128]{2,1,0:T(8,128)(2,1)S(1)}, u32[]{:S(2)}, u32[]{:S(2)}) %collective-permute-start.12) | collective-permute-done | bytes 131104 | tf_op jit(solution)/shard_map/ppermute | solution.py:270
  51.4 0.1 collective-permute-start.13
  51.5 0.7 %shard_map.91 = (f32[256,256]{1,0:T(8,128)S(1)}, f32[256,256]{1,0:T(8,128)S(1)}) custom-call(bf16[256,512]{1,0:T(8,128)(2,1)S(1)} %get-tuple-element.33.kv_ref, bf16[256,256]{1,0:T(8,128)(2,1)S(1)} %get-tuple-element.40.xb_ref, bf16[256,512]{1,0:T(8,128)(2,1)S(1)} %get-tuple-element.50.yo_ref), custom_call_target="tpu_custom_call" | custom-call | flops 67108864 | bytes 524288 | tf_op jit(solution)/shard_map/pallas_call | solution.py:49
  52.3 3.2 %collective-permute-done.14.early_ref = bf16[256,512]{1,0:T(8,128)(2,1)S(1)} collective-permute-done((bf16[256,512]{1,0:T(8,128)(2,1)S(1)}, bf16[256,512]{1,0:T(8,128)(2,1)S(1)}, u32[]{:S(2)}, u32[]{:S(2)}) %collective-permute-start.14) | collective-permute-done | bytes 262176 | tf_op jit(solution)/shard_map/ppermute | solution.py:270
  55.4 1.1 %shard_map.92 = (f32[256,256]{1,0:T(8,128)}, f32[256,256]{1,0:T(8,128)}) custom-call(bf16[256,512]{1,0:T(8,128)(2,1)S(1)} %get-tuple-element.33.kv_ref, f32[4,128,128]{2,1,0:T(8,128)S(1)} %get-tuple-element.56.part_ref, f32[4,128,128]{2,1,0:T(8,128)S(1)} %collective-permute-done.13.recv_ref, bf16[256,512]{1,0:T(8,128)(2,1)S(1)} %collective-permute-done.14.early_ref, ...), custom_call_target="tpu_custom_call" | custom-call | bytes 524288 | tf_op jit(solution)/shard_map/pallas_call | solution.py:49
  (17 shorter events, 0.2 us)
Async XLA Ops:
  1.7 0.9 %copy-start.3 = (bf16[256,256]{1,0:T(8,128)(2,1)S(1)}, bf16[256,256]{1,0:T(8,128)(2,1)}, u32[]{:S(2)}) copy-start(bf16[256,256]{1,0:T(8,128)(2,1)} %param.8) | copy-start | bytes 393220
  2.0 10.3 %collective-permute-start.4 = (f32[4,128,128]{2,1,0:T(8,128)S(1)}, f32[4,128,128]{2,1,0:T(8,128)S(1)}, u32[]{:S(2)}, u32[]{:S(2)}) collective-permute-start(f32[4,128,128]{2,1,0:T(8,128)S(1)} %get-tuple-element.32.own_ref.t_ref), channel_id=1, source_target_pairs={{8,0},{0,8},{24,16},{16,24},{40,32},{32,40},{56,48},{48,56},{72,64... | collective-permute-start | bytes 786440 | tf_op jit(solution)/shard_map/ppermute | solution.py:270
  2.6 17.5 %collective-permute-start = (bf16[256,256]{1,0:T(8,128)(2,1)S(1)}, bf16[256,256]{1,0:T(8,128)(2,1)S(1)}, u32[]{:S(2)}, u32[]{:S(2)}) collective-permute-start(bf16[256,256]{1,0:T(8,128)(2,1)S(1)} %copy-done.3), channel_id=1, source_target_pairs={{2,0},{3,1},{4,2},{5,3},{6,4},{7,5},{0,6},{1,7},{10,8},{11,9},{12,... | collective-permute-start | bytes 393224 | tf_op jit(solution)/shard_map/ppermute | solution.py:277
  8.9 11.2 %collective-permute-start.1 = (bf16[256,256]{1,0:T(8,128)(2,1)S(1)}, bf16[256,256]{1,0:T(8,128)(2,1)S(1)}, u32[]{:S(2)}, u32[]{:S(2)}) collective-permute-start(bf16[256,256]{1,0:T(8,128)(2,1)S(1)} %copy-done.3), channel_id=1, source_target_pairs={{6,0},{7,1},{0,2},{1,3},{2,4},{3,5},{4,6},{5,7},{14,8},{15,9},{8,1... | collective-permute-start | bytes 393224 | tf_op jit(solution)/shard_map/ppermute | solution.py:277
  8.9 15.5 %collective-permute-start.7 = (bf16[256,512]{1,0:T(8,128)(2,1)S(1)}, bf16[256,512]{1,0:T(8,128)(2,1)S(1)}, u32[]{:S(2)}, u32[]{:S(2)}) collective-permute-start(bf16[256,512]{1,0:T(8,128)(2,1)S(1)} %get-tuple-element.33.kv_ref), channel_id=1, source_target_pairs={{0,64},{8,72},{16,80},{24,88},{32,96},{40,104},{48,112},{56,120},{... | collective-permute-start | bytes 786440 | tf_op jit(solution)/shard_map/ppermute | solution.py:270
  12.4 14.0 %collective-permute-start.5 = (bf16[6,128,128]{2,1,0:T(8,128)(2,1)S(1)}, bf16[6,128,128]{2,1,0:T(8,128)(2,1)S(1)}, u32[]{:S(2)}, u32[]{:S(2)}) collective-permute-start(bf16[6,128,128]{2,1,0:T(8,128)(2,1)S(1)} %shard_map.87), channel_id=1, source_target_pairs={{0,16},{16,32},{8,40},{32,48},{24,56},{48,64},{40,72},{64,80},{56,... | collective-permute-start | bytes 589832 | tf_op jit(solution)/shard_map/ppermute | solution.py:270
  15.8 10.6 %collective-permute-start.6 = (bf16[6,128,128]{2,1,0:T(8,128)(2,1)S(1)}, bf16[6,128,128]{2,1,0:T(8,128)(2,1)S(1)}, u32[]{:S(2)}, u32[]{:S(2)}) collective-permute-start(bf16[6,128,128]{2,1,0:T(8,128)(2,1)S(1)} %shard_map.87), channel_id=1, source_target_pairs={{0,48},{16,64},{32,80},{48,96},{64,112},{80,128},{96,144},{112,160... | collective-permute-start | bytes 589832 | tf_op jit(solution)/shard_map/ppermute | solution.py:270
  20.1 6.3 %copy-start = (bf16[256,2048]{1,0:T(8,128)(2,1)S(1)}, bf16[256,2048]{1,0:T(8,128)(2,1)}, u32[]{:S(2)}) copy-start(bf16[256,2048]{1,0:T(8,128)(2,1)} %w_ref.3) | copy-start | bytes 3145732
  20.1 6.3 %copy-start.1 = (f32[256,256]{1,0:T(8,128)S(1)}, f32[256,256]{1,0:T(8,128)}, u32[]{:S(2)}) copy-start(f32[256,256]{1,0:T(8,128)} %x_ref.1) | copy-start | bytes 786436
  20.2 8.1 %collective-permute-start.8 = (bf16[256,256]{1,0:T(8,128)(2,1)S(1)}, bf16[256,256]{1,0:T(8,128)(2,1)S(1)}, u32[]{:S(2)}, u32[]{:S(2)}) collective-permute-start(bf16[256,256]{1,0:T(8,128)(2,1)S(1)} %get-tuple-element.38), channel_id=1, source_target_pairs={{2,0},{3,1},{4,2},{5,3},{6,4},{7,5},{0,6},{1,7},{14,8},{15,9},{8,1... | collective-permute-start | bytes 393224 | tf_op jit(solution)/shard_map/ppermute | solution.py:293
  24.4 2.1 %copy-start.2 = (f32[2]{0:T(128)S(1)}, f32[2]{0:T(128)}, u32[]{:S(2)}) copy-start(f32[2]{0:T(128)} %ridge_ref.1) | copy-start | bytes 28
  24.4 7.0 %collective-permute-start.2 = (bf16[2,256,256]{2,1,0:T(8,128)(2,1)S(1)}, bf16[2,256,256]{2,1,0:T(8,128)(2,1)S(1)}, u32[]{:S(2)}, u32[]{:S(2)}) collective-permute-start(bf16[2,256,256]{2,1,0:T(8,128)(2,1)S(1)} %get-tuple-element.30), channel_id=1, source_target_pairs={{1,0},{2,1},{3,2},{4,3},{5,4},{6,5},{7,6},{0,7},{9,8},{10,9},{11,1... | collective-permute-start | bytes 786440 | tf_op jit(solution)/shard_map/ppermute | solution.py:277
  24.4 7.7 %collective-permute-start.3 = (bf16[2,256,256]{2,1,0:T(8,128)(2,1)S(1)}, bf16[2,256,256]{2,1,0:T(8,128)(2,1)S(1)}, u32[]{:S(2)}, u32[]{:S(2)}) collective-permute-start(bf16[2,256,256]{2,1,0:T(8,128)(2,1)S(1)} %get-tuple-element.31), channel_id=1, source_target_pairs={{7,0},{0,1},{1,2},{2,3},{3,4},{4,5},{5,6},{6,7},{15,8},{8,9},{9,10... | collective-permute-start | bytes 786440 | tf_op jit(solution)/shard_map/ppermute | solution.py:277
  28.3 3.8 %collective-permute-start.9 = (f32[4,128,128]{2,1,0:T(8,128)S(1)}, f32[4,128,128]{2,1,0:T(8,128)S(1)}, u32[]{:S(2)}, u32[]{:S(2)}) collective-permute-start(f32[4,128,128]{2,1,0:T(8,128)S(1)} %get-tuple-element.43), channel_id=1, source_target_pairs={{8,0},{0,8},{24,16},{16,24},{40,32},{32,40},{56,48},{48,56},{72,64... | collective-permute-start | bytes 786440 | tf_op jit(solution)/shard_map/ppermute | solution.py:270
  37.7 1.5 %collective-permute-start.10 = (f32[4,128,128]{2,1,0:T(8,128)S(1)}, f32[4,128,128]{2,1,0:T(8,128)S(1)}, u32[]{:S(2)}, u32[]{:S(2)}) collective-permute-start(f32[4,128,128]{2,1,0:T(8,128)S(1)} %get-tuple-element.49), channel_id=1, source_target_pairs={{8,0},{0,8},{24,16},{16,24},{40,32},{32,40},{56,48},{48,56},{72,64... | collective-permute-start | bytes 786440 | tf_op jit(solution)/shard_map/ppermute | solution.py:270
  39.3 8.9 %collective-permute-start.11 = (bf16[4,128,128]{2,1,0:T(8,128)(2,1)S(1)}, bf16[4,128,128]{2,1,0:T(8,128)(2,1)S(1)}, u32[]{:S(2)}, u32[]{:S(2)}) collective-permute-start(bf16[4,128,128]{2,1,0:T(8,128)(2,1)S(1)} %add_convert_fusion), channel_id=1, source_target_pairs={{16,0},{40,8},{32,16},{56,24},{48,32},{72,40},{64,48},{88,56},{80,... | collective-permute-start | bytes 393224 | tf_op jit(solution)/shard_map/ppermute | solution.py:270
  43.3 8.1 %collective-permute-start.12 = (bf16[4,128,128]{2,1,0:T(8,128)(2,1)S(1)}, bf16[4,128,128]{2,1,0:T(8,128)(2,1)S(1)}, u32[]{:S(2)}, u32[]{:S(2)}) collective-permute-start(bf16[4,128,128]{2,1,0:T(8,128)(2,1)S(1)} %add_convert_fusion), channel_id=1, source_target_pairs={{48,0},{64,16},{80,32},{96,48},{112,64},{128,80},{144,96},{160,112... | collective-permute-start | bytes 393224 | tf_op jit(solution)/shard_map/ppermute | solution.py:270
  46.2 9.2 %collective-permute-start.14 = (bf16[256,512]{1,0:T(8,128)(2,1)S(1)}, bf16[256,512]{1,0:T(8,128)(2,1)S(1)}, u32[]{:S(2)}, u32[]{:S(2)}) collective-permute-start(bf16[256,512]{1,0:T(8,128)(2,1)S(1)} %shard_map.90), channel_id=1, source_target_pairs={{64,0},{72,8},{80,16},{88,24},{96,32},{104,40},{112,48},{120,56},{... | collective-permute-start | bytes 786440 | tf_op jit(solution)/shard_map/ppermute | solution.py:270
  51.4 4.0 %collective-permute-start.13 = (f32[4,128,128]{2,1,0:T(8,128)S(1)}, f32[4,128,128]{2,1,0:T(8,128)S(1)}, u32[]{:S(2)}, u32[]{:S(2)}) collective-permute-start(f32[4,128,128]{2,1,0:T(8,128)S(1)} %get-tuple-element.55), channel_id=1, source_target_pairs={{8,0},{0,8},{24,16},{16,24},{40,32},{32,40},{56,48},{48,56},{72,64... | collective-permute-start | bytes 786440 | tf_op jit(solution)/shard_map/ppermute | solution.py:270

commit v5 on v4

--- a/solution.py
+++ b/solution.py
@@ -124,7 +124,7 @@
 
 def adjoints(
     a_ref, b_ref, c_ref, w_ref, kv_ref, lag_ref, xb_ref, xlo_ref, part_ref, recv_ref, rid_ref, out_ref, turned_ref,
-    near_ref, y_ref, yo_ref, t_ref,
+    near_ref, y_out, yo_ref, t_ref, y_ref, sems,
 ):
     B = 128
     out = out_ref[...]
@@ -162,6 +162,10 @@
             p = p + mm(jnp.concatenate([sc_hi, sc_lo], axis=1), keys[-1])
             ps.append(p)
             ridges.append(rid_ref[h, :1])
+
+    for h in range(NH):
+        o = out[:, h * DH : (h + 1) * DH]
+        t_ref[NH + h] = mm_tn(head(xb_ref, h), o) + mm_tn(head(xlo_ref, h), o)
 
     n = len(ps)
 
@@ -209,16 +213,20 @@
             images = [fresh[i] + betas[i] * images[i] for i in range(n)]
             rrs = nrs
 
+    copies = []
     for h in range(NH):
         y = jnp.concatenate([ys[2 * h], ys[2 * h + 1]], axis=0)
-        y_ref[:, h * DH : (h + 1) * DH] = y
+        cols = slice(h * DH, (h + 1) * DH)
+        y_ref[:, cols] = y
+        copies.append(pltpu.make_async_copy(y_ref.at[:, cols], y_out.at[:, cols], sems.at[h]))
+        copies[-1].start()
         yo_ref[:, h * DH : (h + 1) * DH] = y.astype(BF16)
         y_hi, y_lo = split(y)
         x_hi, x_lo = head(xb_ref, h), head(xlo_ref, h)
-        o = out[:, h * DH : (h + 1) * DH]
         pair = mm_tn(y_hi, x_hi) + mm_tn(y_lo, x_hi) + mm_tn(y_hi, x_lo)
         t_ref[h] = pair + pair.T
-        t_ref[NH + h] = mm_tn(x_hi, o) + mm_tn(x_lo, o)
+    for copy in copies:
+        copy.wait()
 
 
 def pair_terms(k, v, x, y, o, mask):
@@ -237,17 +245,26 @@
         gv_ref[:, h * DH : (h + 1) * DH] = gv
 
 
-def early_terms(lag_ref, xb_ref, yo_ref, other_ref, early_ref):
+def early_pairs(lag_ref, xb_ref, yo_ref, early_ref):
+    rows, cols = tri(TOK, TOK)
+    for h in range(NH):
+        gk, gv = pair_terms(
+            head(lag_ref, h), head(lag_ref, h, 256), head(xb_ref, h), head(yo_ref, h), head(yo_ref, h, 256), rows > cols
+        )
+        early_ref[:, h * DH : (h + 1) * DH] = gk.astype(BF16)
+        early_ref[:, 256 + h * DH : 256 + (h + 1) * DH] = gv.astype(BF16)
+
+
+def early_terms(lag_ref, pairs_ref, other_ref, early_ref):
     core = lax.rem(lax.axis_index("seq"), 2)
-    rows, cols = tri(TOK, TOK)
     for h in range(NH):
         k, v = head(lag_ref, h), head(lag_ref, h, 256)
-        gk, gv = pair_terms(k, v, head(xb_ref, h), head(yo_ref, h), head(yo_ref, h, 256), rows > cols)
         sym = jnp.where(core == 1, other_ref[h], 0.0).astype(BF16)
         cross = jnp.where(core == 1, other_ref[NH + h], 0.0).astype(BF16)
-        gk = gk - mm(k, sym) + mm_nt(v, cross)
+        gk = head(pairs_ref, h).astype(F32) - mm(k, sym) + mm_nt(v, cross)
+        gv = head(pairs_ref, h, 256).astype(F32) + mm(k, cross)
         early_ref[:, h * DH : (h + 1) * DH] = gk.astype(BF16)
-        early_ref[:, 256 + h * DH : 256 + (h + 1) * DH] = (gv + mm(k, cross)).astype(BF16)
+        early_ref[:, 256 + h * DH : 256 + (h + 1) * DH] = gv.astype(BF16)
 
 
 def base_terms(kv_ref, part_ref, recv_ref, early_ref, gk_in, gv_in, gk_ref, gv_ref):
@@ -305,17 +322,25 @@
     send, across = lax.optimization_barrier((send, across))
     recv = swapped(send)
 
-    y, yo, tl = call(
+    y, yo, tl = pl.pallas_call(
         adjoints,
-        [((TOK, 256), F32), ((TOK, 512), BF16), (st, F32)],
-        up_two, down_two, across, out_weight, kv, kv_lag, xb, xlo, part, recv, rid, begun, turned, near,
-        flops=1 << 32,
-    )
-
-    other = swapped(tl)
+        out_shape=[
+            jax.ShapeDtypeStruct((TOK, 256), F32),
+            jax.ShapeDtypeStruct((TOK, 512), BF16),
+            jax.ShapeDtypeStruct(st, F32),
+        ],
+        in_specs=[VM] * 14,
+        out_specs=[pl.BlockSpec(memory_space=pltpu.HBM), VM, VM],
+        scratch_shapes=[pltpu.VMEM((TOK, 256), F32), pltpu.SemaphoreType.DMA((NH,))],
+        compiler_params=PARAMS,
+        cost_estimate=pl.CostEstimate(flops=1 << 32, bytes_accessed=1 << 19, transcendentals=0),
+    )(up_two, down_two, across, out_weight, kv, kv_lag, xb, xlo, part, recv, rid, begun, turned, near)
+
+    (pairs,) = call(early_pairs, [((TOK, 512), BF16)], kv_lag, xb, yo, flops=1 << 26)
+    other, pairs = lax.optimization_barrier((swapped(tl), pairs))
     first = lax.rem(lax.axis_index("seq"), 2) == 0
     chip_l = (tl + other).astype(BF16)
-    (early,) = call(early_terms, [((TOK, 512), BF16)], kv_lag, xb, yo, other, flops=1 << 26)
+    (early,) = call(early_terms, [((TOK, 512), BF16)], kv_lag, pairs, other, flops=1 << 26)
     early = moved(early, lambda i: i + lag)
     q1 = moved(chip_l, lambda i: i + 2 if i % 2 == 0 else i + 4)
     q2 = moved(chip_l, lambda i: i + 6 if i % 2 == 0 else None)

time: 56.9 us -> 56.8 us (level)
    pallas_call x0 -> x1, Pallas kernels: none -> 5.53 us  [body(): pl.pallas_call(adjoints, out_shape=[jax.ShapeDtypeStruct((TOK, 256), F32)...]
    pallas_call x8, Pallas kernels: 9.78 us -> 4.31 us  [call(): pl.pallas_call(kernel, out_shape=[jax.ShapeDtypeStruct(s, d) for s, d in...]
where the time goes in v5:
time: 56.8 us; the launch traced here: 56.5 us
  starting transfers between devices  31.9 us (56%)
  waiting for transfers between devices  12.2 us (21%)
  Pallas kernels  9.84 us (17%)
  other arithmetic  1.14 us (2%)
  between operations  0.86 us (2%)
    ppermute x10, starting transfers between devices, moved(): return lax.ppermute(value, 'seq', route)  19.4 us
    ppermute x4, starting transfers between devices, around(): return lax.ppermute(value, 'head', [((i + away) % 8, i) for i in range(8)])  8.33 us
    ppermute x10, waiting for transfers between devices, moved(): return lax.ppermute(value, 'seq', route)  7.68 us
    pallas_call x1, Pallas kernels, body(): pl.pallas_call(adjoints, out_shape=[jax.ShapeDtypeStruct((TOK, 256), F32)...  5.53 us
    pallas_call x8, Pallas kernels, call(): pl.pallas_call(kernel, out_shape=[jax.ShapeDtypeStruct(s, d) for s, d in...  4.31 us
    ppermute x1, starting transfers between devices, body(): across = lax.ppermute(across, ('seq', 'head'), far)  4.21 us
    ppermute x4, waiting for transfers between devices, around(): return lax.ppermute(value, 'head', [((i + away) % 8, i) for i in range(8)])  3.75 us
  transfers between devices with their start and end apart: 15, of which 6 were waited for; matrix products, arithmetic and copies ran while one was open for 0% of the time, Pallas kernels for 5%

profile of v5, /device:TPU:2, one launch (start us, length us, event | category | flops | bytes accessed | tf_op | source)
XLA Modules:
  0.0 56.5 jit_solution(5740880232850048546)
XLA Ops:
  0.6 1.1 %pad_maximum_fusion.kvd_ref = bf16[256,768]{1,0:T(8,128)(2,1)S(1)} fusion(bf16[256,256]{1,0:T(8,128)(2,1)} %param.8, bf16[256,256]{1,0:T(8,128)(2,1)} %param.7, bf16[256,256]{1,0:T(8,128)(2,1)} %param.6), kind=kLoop, calls=%fused_computation | loop fusion | flops 1179648 | bytes 786432 | tf_op jit(solution)/shard_map/concatenate | solution.py:298
  1.7 0.0 copy-start.3
  1.7 0.3 shard_map.85
  2.0 0.1 collective-permute-start.4
  2.1 0.5 copy-done.3
  2.6 6.3 %collective-permute-start = (bf16[256,256]{1,0:T(8,128)(2,1)S(1)}, bf16[256,256]{1,0:T(8,128)(2,1)S(1)}, u32[]{:S(2)}, u32[]{:S(2)}) collective-permute-start(bf16[256,256]{1,0:T(8,128)(2,1)S(1)} %copy-done.3), channel_id=1, source_target_pairs={{2,0},{3,1},{4,2},{5,3},{6,4},{7,5},{0,6},{1,7},{10,8},{11,9},{12,... | collective-permute-start | bytes 393224 | tf_op jit(solution)/shard_map/ppermute | solution.py:294
  8.9 0.0 collective-permute-start.1
  8.9 3.4 %collective-permute-start.7 = (bf16[256,512]{1,0:T(8,128)(2,1)S(1)}, bf16[256,512]{1,0:T(8,128)(2,1)S(1)}, u32[]{:S(2)}, u32[]{:S(2)}) collective-permute-start(bf16[256,512]{1,0:T(8,128)(2,1)S(1)} %get-tuple-element.35.kv_ref), channel_id=1, source_target_pairs={{0,64},{8,72},{16,80},{24,88},{32,96},{40,104},{48,112},{56,120},{... | collective-permute-start | bytes 786440 | tf_op jit(solution)/shard_map/ppermute | solution.py:287
  12.4 3.5 %collective-permute-start.5 = (bf16[6,128,128]{2,1,0:T(8,128)(2,1)S(1)}, bf16[6,128,128]{2,1,0:T(8,128)(2,1)S(1)}, u32[]{:S(2)}, u32[]{:S(2)}) collective-permute-start(bf16[6,128,128]{2,1,0:T(8,128)(2,1)S(1)} %shard_map.87), channel_id=1, source_target_pairs={{0,16},{16,32},{8,40},{32,48},{24,56},{48,64},{40,72},{64,80},{56,... | collective-permute-start | bytes 589832 | tf_op jit(solution)/shard_map/ppermute | solution.py:287
  15.8 4.2 %collective-permute-start.6 = (bf16[6,128,128]{2,1,0:T(8,128)(2,1)S(1)}, bf16[6,128,128]{2,1,0:T(8,128)(2,1)S(1)}, u32[]{:S(2)}, u32[]{:S(2)}) collective-permute-start(bf16[6,128,128]{2,1,0:T(8,128)(2,1)S(1)} %shard_map.87), channel_id=1, source_target_pairs={{0,48},{16,64},{32,80},{48,96},{64,112},{80,128},{96,144},{112,160... | collective-permute-start | bytes 589832 | tf_op jit(solution)/shard_map/ppermute | solution.py:287
  20.1 0.0 copy-start
  20.1 0.0 copy-start.1
  20.1 0.1 shard_map.86
  20.2 4.2 %collective-permute-start.8 = (bf16[256,256]{1,0:T(8,128)(2,1)S(1)}, bf16[256,256]{1,0:T(8,128)(2,1)S(1)}, u32[]{:S(2)}, u32[]{:S(2)}) collective-permute-start(bf16[256,256]{1,0:T(8,128)(2,1)S(1)} %get-tuple-element.40), channel_id=1, source_target_pairs={{2,0},{3,1},{4,2},{5,3},{6,4},{7,5},{0,6},{1,7},{14,8},{15,9},{8,1... | collective-permute-start | bytes 393224 | tf_op jit(solution)/shard_map/ppermute | solution.py:310
  24.4 2.0 %collective-permute-start.3 = (bf16[2,256,256]{2,1,0:T(8,128)(2,1)S(1)}, bf16[2,256,256]{2,1,0:T(8,128)(2,1)S(1)}, u32[]{:S(2)}, u32[]{:S(2)}) collective-permute-start(bf16[2,256,256]{2,1,0:T(8,128)(2,1)S(1)} %get-tuple-element.33), channel_id=1, source_target_pairs={{7,0},{0,1},{1,2},{2,3},{3,4},{4,5},{5,6},{6,7},{15,8},{8,9},{9,10... | collective-permute-start | bytes 786440 | tf_op jit(solution)/shard_map/ppermute | solution.py:294
  26.4 1.0 %shard_map.88 = (f32[4,128,128]{2,1,0:T(8,128)S(1)}, f32[4,128,128]{2,1,0:T(8,128)S(1)}, f32[256,256]{1,0:T(8,128)S(1)}, bf16[4,128,256]{2,1,0:T(8,128)(2,1)S(1)...) custom-call(f32[4,128,128]{2,1,0:T(8,128)S(1)} %get-tuple-element.34, ...), custom_call_target="tpu_custom_call" | custom-call | tf_op jit(solution)/shard_map/pallas_call | solution.py:49
  27.5 0.8 %collective-permute-done.8.c_ref = bf16[256,256]{1,0:T(8,128)(2,1)S(1)} collective-permute-done((bf16[256,256]{1,0:T(8,128)(2,1)S(1)}, bf16[256,256]{1,0:T(8,128)(2,1)S(1)}, u32[]{:S(2)}, u32[]{:S(2)}) %collective-permute-start.8) | collective-permute-done | bytes 131104 | tf_op jit(solution)/shard_map/ppermute | solution.py:310
  28.3 3.1 %collective-permute-done.2.a_ref = bf16[2,256,256]{2,1,0:T(8,128)(2,1)S(1)} collective-permute-done((bf16[2,256,256]{2,1,0:T(8,128)(2,1)S(1)}, bf16[2,256,256]{2,1,0:T(8,128)(2,1)S(1)}, u32[]{:S(2)}, u32[]{:S(2)}) %collective-permute-start.2) | collective-permute-done | bytes 262176 | tf_op jit(solution)/shard_map/ppermute | solution.py:294
  31.4 0.6 %collective-permute-done.3.b_ref = bf16[2,256,256]{2,1,0:T(8,128)(2,1)S(1)} collective-permute-done((bf16[2,256,256]{2,1,0:T(8,128)(2,1)S(1)}, bf16[2,256,256]{2,1,0:T(8,128)(2,1)S(1)}, u32[]{:S(2)}, u32[]{:S(2)}) %collective-permute-start.3) | collective-permute-done | bytes 262176 | tf_op jit(solution)/shard_map/ppermute | solution.py:294
  32.0 5.5 %shard_map.89 = (f32[256,256]{1,0:T(8,128)}, bf16[256,512]{1,0:T(8,128)(2,1)S(1)}, f32[4,128,128]{2,1,0:T(8,128)S(1)}) custom-call(bf16[2,256,256]{2,1,0:T(8,128)(2,1)S(1)} %collective-permute-done.2.a_ref, bf16[2,256,256]{2,1,0:T(8,128)(2,1)S(1)} %collective-permute-done.3.b_ref, bf16[256,256]{1,0:T(8,128)(2,1)S(1)} %collective-permute-done.8.c_ref, ...), custom_call_target="tpu_custom_call" | custom-call | flops 4294967296 | bytes 524288 | tf_op jit(solution)/shard_map/pallas_call | solution.py:325
  37.6 0.1 collective-permute-start.10
  37.7 0.8 %shard_map.90.pairs_ref = bf16[256,512]{1,0:T(8,128)(2,1)S(1)} custom-call(bf16[256,512]{1,0:T(8,128)(2,1)S(1)} %collective-permute-done.7.lag_ref, bf16[256,256]{1,0:T(8,128)(2,1)S(1)} %get-tuple-element.42.xb_ref, bf16[256,512]{1,0:T(8,128)(2,1)S(1)} %get-tuple-element.52.yo_ref), custom_call_target="tpu_custom_call" | custom-call | flops 67108864 | bytes 524288 | tf_op jit(solution)/shard_map/pallas_call | solution.py:49
  38.4 0.8 %collective-permute-done.10.other_ref = f32[4,128,128]{2,1,0:T(8,128)S(1)} collective-permute-done((f32[4,128,128]{2,1,0:T(8,128)S(1)}, f32[4,128,128]{2,1,0:T(8,128)S(1)}, u32[]{:S(2)}, u32[]{:S(2)}) %collective-permute-start.10) | collective-permute-done | bytes 262176 | tf_op jit(solution)/shard_map/ppermute | solution.py:287
  39.2 4.0 %collective-permute-start.11 = (bf16[4,128,128]{2,1,0:T(8,128)(2,1)S(1)}, bf16[4,128,128]{2,1,0:T(8,128)(2,1)S(1)}, u32[]{:S(2)}, u32[]{:S(2)}) collective-permute-start(bf16[4,128,128]{2,1,0:T(8,128)(2,1)S(1)} %add_convert_fusion), channel_id=1, source_target_pairs={{16,0},{40,8},{32,16},{56,24},{48,32},{72,40},{64,48},{88,56},{80,... | collective-permute-start | bytes 393224 | tf_op jit(solution)/shard_map/ppermute | solution.py:287
  43.2 2.1 %collective-permute-start.12 = (bf16[4,128,128]{2,1,0:T(8,128)(2,1)S(1)}, bf16[4,128,128]{2,1,0:T(8,128)(2,1)S(1)}, u32[]{:S(2)}, u32[]{:S(2)}) collective-permute-start(bf16[4,128,128]{2,1,0:T(8,128)(2,1)S(1)} %add_convert_fusion), channel_id=1, source_target_pairs={{48,0},{64,16},{80,32},{96,48},{112,64},{128,80},{144,96},{160,112... | collective-permute-start | bytes 393224 | tf_op jit(solution)/shard_map/ppermute | solution.py:287
  45.4 0.3 shard_map.91
  45.6 1.9 %collective-permute-start.14 = (bf16[256,512]{1,0:T(8,128)(2,1)S(1)}, bf16[256,512]{1,0:T(8,128)(2,1)S(1)}, u32[]{:S(2)}, u32[]{:S(2)}) collective-permute-start(bf16[256,512]{1,0:T(8,128)(2,1)S(1)} %shard_map.91), channel_id=1, source_target_pairs={{64,0},{72,8},{80,16},{88,24},{96,32},{104,40},{112,48},{120,56},{... | collective-permute-start | bytes 786440 | tf_op jit(solution)/shard_map/ppermute | solution.py:287
  47.6 3.7 %collective-permute-done.12 = bf16[4,128,128]{2,1,0:T(8,128)(2,1)S(1)} collective-permute-done((bf16[4,128,128]{2,1,0:T(8,128)(2,1)S(1)}, bf16[4,128,128]{2,1,0:T(8,128)(2,1)S(1)}, u32[]{:S(2)}, u32[]{:S(2)}) %collective-permute-start.12) | collective-permute-done | bytes 131104 | tf_op jit(solution)/shard_map/ppermute | solution.py:287
  51.3 0.1 collective-permute-start.13
  51.4 0.7 %shard_map.92 = (f32[256,256]{1,0:T(8,128)S(1)}, f32[256,256]{1,0:T(8,128)S(1)}) custom-call(bf16[256,512]{1,0:T(8,128)(2,1)S(1)} %get-tuple-element.35.kv_ref, bf16[256,256]{1,0:T(8,128)(2,1)S(1)} %get-tuple-element.42.xb_ref, bf16[256,512]{1,0:T(8,128)(2,1)S(1)} %get-tuple-element.52.yo_ref), custom_call_target="tpu_custom_call" | custom-call | flops 67108864 | bytes 524288 | tf_op jit(solution)/shard_map/pallas_call | solution.py:49
  52.2 3.2 %collective-permute-done.14.early_ref = bf16[256,512]{1,0:T(8,128)(2,1)S(1)} collective-permute-done((bf16[256,512]{1,0:T(8,128)(2,1)S(1)}, bf16[256,512]{1,0:T(8,128)(2,1)S(1)}, u32[]{:S(2)}, u32[]{:S(2)}) %collective-permute-start.14) | collective-permute-done | bytes 262176 | tf_op jit(solution)/shard_map/ppermute | solution.py:287
  55.4 1.1 %shard_map.93 = (f32[256,256]{1,0:T(8,128)}, f32[256,256]{1,0:T(8,128)}) custom-call(bf16[256,512]{1,0:T(8,128)(2,1)S(1)} %get-tuple-element.35.kv_ref, f32[4,128,128]{2,1,0:T(8,128)S(1)} %get-tuple-element.60.part_ref, f32[4,128,128]{2,1,0:T(8,128)S(1)} %collective-permute-done.13.recv_ref, bf16[256,512]{1,0:T(8,128)(2,1)S(1)} %collective-permute-done.14.early_ref, ...), custom_call_target="tpu_custom_call" | custom-call | bytes 524288 | tf_op jit(solution)/shard_map/pallas_call | solution.py:49
  (18 shorter events, 0.2 us)
Async XLA Ops:
  1.7 0.9 %copy-start.3 = (bf16[256,256]{1,0:T(8,128)(2,1)S(1)}, bf16[256,256]{1,0:T(8,128)(2,1)}, u32[]{:S(2)}) copy-start(bf16[256,256]{1,0:T(8,128)(2,1)} %param.8) | copy-start | bytes 393220
  2.0 10.3 %collective-permute-start.4 = (f32[4,128,128]{2,1,0:T(8,128)S(1)}, f32[4,128,128]{2,1,0:T(8,128)S(1)}, u32[]{:S(2)}, u32[]{:S(2)}) collective-permute-start(f32[4,128,128]{2,1,0:T(8,128)S(1)} %get-tuple-element.34.own_ref.t_ref), channel_id=1, source_target_pairs={{8,0},{0,8},{24,16},{16,24},{40,32},{32,40},{56,48},{48,56},{72,64... | collective-permute-start | bytes 786440 | tf_op jit(solution)/shard_map/ppermute | solution.py:287
  2.6 17.5 %collective-permute-start = (bf16[256,256]{1,0:T(8,128)(2,1)S(1)}, bf16[256,256]{1,0:T(8,128)(2,1)S(1)}, u32[]{:S(2)}, u32[]{:S(2)}) collective-permute-start(bf16[256,256]{1,0:T(8,128)(2,1)S(1)} %copy-done.3), channel_id=1, source_target_pairs={{2,0},{3,1},{4,2},{5,3},{6,4},{7,5},{0,6},{1,7},{10,8},{11,9},{12,... | collective-permute-start | bytes 393224 | tf_op jit(solution)/shard_map/ppermute | solution.py:294
  8.9 11.2 %collective-permute-start.1 = (bf16[256,256]{1,0:T(8,128)(2,1)S(1)}, bf16[256,256]{1,0:T(8,128)(2,1)S(1)}, u32[]{:S(2)}, u32[]{:S(2)}) collective-permute-start(bf16[256,256]{1,0:T(8,128)(2,1)S(1)} %copy-done.3), channel_id=1, source_target_pairs={{6,0},{7,1},{0,2},{1,3},{2,4},{3,5},{4,6},{5,7},{14,8},{15,9},{8,1... | collective-permute-start | bytes 393224 | tf_op jit(solution)/shard_map/ppermute | solution.py:294
  8.9 15.5 %collective-permute-start.7 = (bf16[256,512]{1,0:T(8,128)(2,1)S(1)}, bf16[256,512]{1,0:T(8,128)(2,1)S(1)}, u32[]{:S(2)}, u32[]{:S(2)}) collective-permute-start(bf16[256,512]{1,0:T(8,128)(2,1)S(1)} %get-tuple-element.35.kv_ref), channel_id=1, source_target_pairs={{0,64},{8,72},{16,80},{24,88},{32,96},{40,104},{48,112},{56,120},{... | collective-permute-start | bytes 786440 | tf_op jit(solution)/shard_map/ppermute | solution.py:287
  12.4 14.0 %collective-permute-start.5 = (bf16[6,128,128]{2,1,0:T(8,128)(2,1)S(1)}, bf16[6,128,128]{2,1,0:T(8,128)(2,1)S(1)}, u32[]{:S(2)}, u32[]{:S(2)}) collective-permute-start(bf16[6,128,128]{2,1,0:T(8,128)(2,1)S(1)} %shard_map.87), channel_id=1, source_target_pairs={{0,16},{16,32},{8,40},{32,48},{24,56},{48,64},{40,72},{64,80},{56,... | collective-permute-start | bytes 589832 | tf_op jit(solution)/shard_map/ppermute | solution.py:287
  15.8 10.6 %collective-permute-start.6 = (bf16[6,128,128]{2,1,0:T(8,128)(2,1)S(1)}, bf16[6,128,128]{2,1,0:T(8,128)(2,1)S(1)}, u32[]{:S(2)}, u32[]{:S(2)}) collective-permute-start(bf16[6,128,128]{2,1,0:T(8,128)(2,1)S(1)} %shard_map.87), channel_id=1, source_target_pairs={{0,48},{16,64},{32,80},{48,96},{64,112},{80,128},{96,144},{112,160... | collective-permute-start | bytes 589832 | tf_op jit(solution)/shard_map/ppermute | solution.py:287
  20.1 6.3 %copy-start = (bf16[256,2048]{1,0:T(8,128)(2,1)S(1)}, bf16[256,2048]{1,0:T(8,128)(2,1)}, u32[]{:S(2)}) copy-start(bf16[256,2048]{1,0:T(8,128)(2,1)} %w_ref.3) | copy-start | bytes 3145732
  20.1 6.3 %copy-start.1 = (f32[256,256]{1,0:T(8,128)S(1)}, f32[256,256]{1,0:T(8,128)}, u32[]{:S(2)}) copy-start(f32[256,256]{1,0:T(8,128)} %x_ref.1) | copy-start | bytes 786436
  20.2 8.1 %collective-permute-start.8 = (bf16[256,256]{1,0:T(8,128)(2,1)S(1)}, bf16[256,256]{1,0:T(8,128)(2,1)S(1)}, u32[]{:S(2)}, u32[]{:S(2)}) collective-permute-start(bf16[256,256]{1,0:T(8,128)(2,1)S(1)} %get-tuple-element.40), channel_id=1, source_target_pairs={{2,0},{3,1},{4,2},{5,3},{6,4},{7,5},{0,6},{1,7},{14,8},{15,9},{8,1... | collective-permute-start | bytes 393224 | tf_op jit(solution)/shard_map/ppermute | solution.py:310
  24.4 2.1 %copy-start.2 = (f32[2]{0:T(128)S(1)}, f32[2]{0:T(128)}, u32[]{:S(2)}) copy-start(f32[2]{0:T(128)} %ridge_ref.1) | copy-start | bytes 28
  24.4 7.0 %collective-permute-start.2 = (bf16[2,256,256]{2,1,0:T(8,128)(2,1)S(1)}, bf16[2,256,256]{2,1,0:T(8,128)(2,1)S(1)}, u32[]{:S(2)}, u32[]{:S(2)}) collective-permute-start(bf16[2,256,256]{2,1,0:T(8,128)(2,1)S(1)} %get-tuple-element.32), channel_id=1, source_target_pairs={{1,0},{2,1},{3,2},{4,3},{5,4},{6,5},{7,6},{0,7},{9,8},{10,9},{11,1... | collective-permute-start | bytes 786440 | tf_op jit(solution)/shard_map/ppermute | solution.py:294
  24.4 7.7 %collective-permute-start.3 = (bf16[2,256,256]{2,1,0:T(8,128)(2,1)S(1)}, bf16[2,256,256]{2,1,0:T(8,128)(2,1)S(1)}, u32[]{:S(2)}, u32[]{:S(2)}) collective-permute-start(bf16[2,256,256]{2,1,0:T(8,128)(2,1)S(1)} %get-tuple-element.33), channel_id=1, source_target_pairs={{7,0},{0,1},{1,2},{2,3},{3,4},{4,5},{5,6},{6,7},{15,8},{8,9},{9,10... | collective-permute-start | bytes 786440 | tf_op jit(solution)/shard_map/ppermute | solution.py:294
  28.3 3.8 %collective-permute-start.9 = (f32[4,128,128]{2,1,0:T(8,128)S(1)}, f32[4,128,128]{2,1,0:T(8,128)S(1)}, u32[]{:S(2)}, u32[]{:S(2)}) collective-permute-start(f32[4,128,128]{2,1,0:T(8,128)S(1)} %get-tuple-element.45), channel_id=1, source_target_pairs={{8,0},{0,8},{24,16},{16,24},{40,32},{32,40},{56,48},{48,56},{72,64... | collective-permute-start | bytes 786440 | tf_op jit(solution)/shard_map/ppermute | solution.py:287
  37.6 1.6 %collective-permute-start.10 = (f32[4,128,128]{2,1,0:T(8,128)S(1)}, f32[4,128,128]{2,1,0:T(8,128)S(1)}, u32[]{:S(2)}, u32[]{:S(2)}) collective-permute-start(f32[4,128,128]{2,1,0:T(8,128)S(1)} %get-tuple-element.51), channel_id=1, source_target_pairs={{8,0},{0,8},{24,16},{16,24},{40,32},{32,40},{56,48},{48,56},{72,64... | collective-permute-start | bytes 786440 | tf_op jit(solution)/shard_map/ppermute | solution.py:287
  39.2 8.3 %collective-permute-start.11 = (bf16[4,128,128]{2,1,0:T(8,128)(2,1)S(1)}, bf16[4,128,128]{2,1,0:T(8,128)(2,1)S(1)}, u32[]{:S(2)}, u32[]{:S(2)}) collective-permute-start(bf16[4,128,128]{2,1,0:T(8,128)(2,1)S(1)} %add_convert_fusion), channel_id=1, source_target_pairs={{16,0},{40,8},{32,16},{56,24},{48,32},{72,40},{64,48},{88,56},{80,... | collective-permute-start | bytes 393224 | tf_op jit(solution)/shard_map/ppermute | solution.py:287
  43.2 8.1 %collective-permute-start.12 = (bf16[4,128,128]{2,1,0:T(8,128)(2,1)S(1)}, bf16[4,128,128]{2,1,0:T(8,128)(2,1)S(1)}, u32[]{:S(2)}, u32[]{:S(2)}) collective-permute-start(bf16[4,128,128]{2,1,0:T(8,128)(2,1)S(1)} %add_convert_fusion), channel_id=1, source_target_pairs={{48,0},{64,16},{80,32},{96,48},{112,64},{128,80},{144,96},{160,112... | collective-permute-start | bytes 393224 | tf_op jit(solution)/shard_map/ppermute | solution.py:287
  45.6 9.7 %collective-permute-start.14 = (bf16[256,512]{1,0:T(8,128)(2,1)S(1)}, bf16[256,512]{1,0:T(8,128)(2,1)S(1)}, u32[]{:S(2)}, u32[]{:S(2)}) collective-permute-start(bf16[256,512]{1,0:T(8,128)(2,1)S(1)} %shard_map.91), channel_id=1, source_target_pairs={{64,0},{72,8},{80,16},{88,24},{96,32},{104,40},{112,48},{120,56},{... | collective-permute-start | bytes 786440 | tf_op jit(solution)/shard_map/ppermute | solution.py:287
  51.3 4.0 %collective-permute-start.13 = (f32[4,128,128]{2,1,0:T(8,128)S(1)}, f32[4,128,128]{2,1,0:T(8,128)S(1)}, u32[]{:S(2)}, u32[]{:S(2)}) collective-permute-start(f32[4,128,128]{2,1,0:T(8,128)S(1)} %get-tuple-element.59), channel_id=1, source_target_pairs={{8,0},{0,8},{24,16},{16,24},{40,32},{32,40},{56,48},{48,56},{72,64... | collective-permute-start | bytes 786440 | tf_op jit(solution)/shard_map/ppermute | solution.py:287

commit v6 on v5

--- a/solution.py
+++ b/solution.py
@@ -243,6 +243,35 @@
         )
         gk_ref[:, h * DH : (h + 1) * DH] = gk
         gv_ref[:, h * DH : (h + 1) * DH] = gv
+
+
+def square():
+    r, c = tri(DH, DH)
+    return r > c, r == c
+
+
+def chip_sums(own_ref, other_ref, out_ref):
+    below, level = square()
+    first, second = own_ref[0] + other_ref[0], own_ref[1] + other_ref[1]
+    out_ref[:DH] = jnp.where(below | level, first, second).astype(BF16)
+    diagonal = jnp.sum(jnp.where(level, second, 0.0), axis=0, keepdims=True)
+    out_ref[DH : DH + 16] = jnp.broadcast_to(diagonal, (16, DH)).astype(BF16)
+    for h in range(NH):
+        rows = slice(DH + 16 + h * DH, DH + 16 + (h + 1) * DH)
+        out_ref[rows] = (own_ref[NH + h] + other_ref[NH + h]).astype(BF16)
+
+
+def sums_to_send(other_ref, q1_ref, q2_ref, part_ref, both_ref):
+    core = lax.rem(lax.axis_index("seq"), 2)
+    below, level = square()
+    total = q1_ref[...].astype(F32) + q2_ref[...].astype(F32)
+    mixed, turned, diagonal = total[:DH], total[:DH].T, total[DH : DH + 1]
+    first = jnp.where(below | level, mixed, turned)
+    second = jnp.where(level, diagonal, jnp.where(below, turned, mixed))
+    crosses = [total[DH + 16 + h * DH : DH + 16 + (h + 1) * DH] for h in range(NH)]
+    for at, both in enumerate([first, second] + crosses):
+        both_ref[at] = both
+        part_ref[at] = both + jnp.where(core == 0, other_ref[at], 0.0)
 
 
 def early_pairs(lag_ref, xb_ref, yo_ref, early_ref):
@@ -338,15 +367,13 @@
 
     (pairs,) = call(early_pairs, [((TOK, 512), BF16)], kv_lag, xb, yo, flops=1 << 26)
     other, pairs = lax.optimization_barrier((swapped(tl), pairs))
-    first = lax.rem(lax.axis_index("seq"), 2) == 0
-    chip_l = (tl + other).astype(BF16)
+    (chip_l,) = call(chip_sums, [((3 * DH + 16, DH), BF16)], tl, other, size=0)
     (early,) = call(early_terms, [((TOK, 512), BF16)], kv_lag, pairs, other, flops=1 << 26)
     early = moved(early, lambda i: i + lag)
     q1 = moved(chip_l, lambda i: i + 2 if i % 2 == 0 else i + 4)
     q2 = moved(chip_l, lambda i: i + 6 if i % 2 == 0 else None)
     gk, gv = call(own_terms, [((TOK, 256), F32)] * 2, kv, xb, yo, flops=1 << 26)
-    both = q1.astype(F32) + q2.astype(F32)
-    part_l = both + jnp.where(first, other, 0.0)
+    part_l, both = call(sums_to_send, [(st, F32), (st, F32)], other, q1, q2, size=0)
     recv_l = swapped(both)
     grad_k, grad_v = call(
         base_terms, [((TOK, 256), F32)] * 2, kv, part_l, recv_l, early, gk, gv

time: 56.8 us -> 56.5 us (level)
  waiting for transfers between devices: 12.2 us -> 11.6 us
    ppermute x10, waiting for transfers between devices: 7.68 us -> 7.01 us  [moved(): return lax.ppermute(value, 'seq', route)]
    pallas_call x8 -> x10, Pallas kernels: 4.31 us -> 4.47 us  [call(): pl.pallas_call(kernel, out_shape=[jax.ShapeDtypeStruct(s, d) for s, d in...]
where the time goes in v6:
time: 56.5 us; the launch traced here: 56 us
  starting transfers between devices  31.9 us (56%)
  waiting for transfers between devices  11.6 us (21%)
  Pallas kernels  10.1 us (18%)
  other arithmetic  1.06 us (2%)
  between operations  0.86 us (2%)
    ppermute x10, starting transfers between devices, moved(): return lax.ppermute(value, 'seq', route)  19.4 us
    ppermute x4, starting transfers between devices, around(): return lax.ppermute(value, 'head', [((i + away) % 8, i) for i in range(8)])  8.33 us
    ppermute x10, waiting for transfers between devices, moved(): return lax.ppermute(value, 'seq', route)  7.01 us
    pallas_call x1, Pallas kernels, body(): pl.pallas_call(adjoints, out_shape=[jax.ShapeDtypeStruct((TOK, 256), F32)...  5.62 us
    pallas_call x10, Pallas kernels, call(): pl.pallas_call(kernel, out_shape=[jax.ShapeDtypeStruct(s, d) for s, d in...  4.47 us
    ppermute x1, starting transfers between devices, body(): across = lax.ppermute(across, ('seq', 'head'), far)  4.21 us
    ppermute x4, waiting for transfers between devices, around(): return lax.ppermute(value, 'head', [((i + away) % 8, i) for i in range(8)])  3.75 us
  transfers between devices with their start and end apart: 15, of which 6 were waited for; matrix products, arithmetic and copies ran while one was open for 0% of the time, Pallas kernels for 5%

profile of v6, /device:TPU:2, one launch (start us, length us, event | category | flops | bytes accessed | tf_op | source)
XLA Modules:
  0.0 56.0 jit_solution(8166051919181871928)
XLA Ops:
  0.6 1.1 %pad_maximum_fusion.kvd_ref = bf16[256,768]{1,0:T(8,128)(2,1)S(1)} fusion(bf16[256,256]{1,0:T(8,128)(2,1)} %param.8, bf16[256,256]{1,0:T(8,128)(2,1)} %param.7, bf16[256,256]{1,0:T(8,128)(2,1)} %param.6), kind=kLoop, calls=%fused_computation | loop fusion | flops 1179648 | bytes 786432 | tf_op jit(solution)/shard_map/concatenate | solution.py:327
  1.7 0.0 copy-start.3
  1.7 0.3 shard_map.85
  2.0 0.1 collective-permute-start.4
  2.1 0.5 copy-done.3
  2.6 6.3 %collective-permute-start = (bf16[256,256]{1,0:T(8,128)(2,1)S(1)}, bf16[256,256]{1,0:T(8,128)(2,1)S(1)}, u32[]{:S(2)}, u32[]{:S(2)}) collective-permute-start(bf16[256,256]{1,0:T(8,128)(2,1)S(1)} %copy-done.3), channel_id=1, source_target_pairs={{2,0},{3,1},{4,2},{5,3},{6,4},{7,5},{0,6},{1,7},{10,8},{11,9},{12,... | collective-permute-start | bytes 393224 | tf_op jit(solution)/shard_map/ppermute | solution.py:323
  8.9 3.4 %collective-permute-start.7 = (bf16[256,512]{1,0:T(8,128)(2,1)S(1)}, bf16[256,512]{1,0:T(8,128)(2,1)S(1)}, u32[]{:S(2)}, u32[]{:S(2)}) collective-permute-start(bf16[256,512]{1,0:T(8,128)(2,1)S(1)} %get-tuple-element.37.kv_ref), channel_id=1, source_target_pairs={{0,64},{8,72},{16,80},{24,88},{32,96},{40,104},{48,112},{56,120},{... | collective-permute-start | bytes 786440 | tf_op jit(solution)/shard_map/ppermute | solution.py:316
  12.4 3.5 %collective-permute-start.5 = (bf16[6,128,128]{2,1,0:T(8,128)(2,1)S(1)}, bf16[6,128,128]{2,1,0:T(8,128)(2,1)S(1)}, u32[]{:S(2)}, u32[]{:S(2)}) collective-permute-start(bf16[6,128,128]{2,1,0:T(8,128)(2,1)S(1)} %shard_map.87), channel_id=1, source_target_pairs={{0,16},{16,32},{8,40},{32,48},{24,56},{48,64},{40,72},{64,80},{56,... | collective-permute-start | bytes 589832 | tf_op jit(solution)/shard_map/ppermute | solution.py:316
  15.8 4.2 %collective-permute-start.6 = (bf16[6,128,128]{2,1,0:T(8,128)(2,1)S(1)}, bf16[6,128,128]{2,1,0:T(8,128)(2,1)S(1)}, u32[]{:S(2)}, u32[]{:S(2)}) collective-permute-start(bf16[6,128,128]{2,1,0:T(8,128)(2,1)S(1)} %shard_map.87), channel_id=1, source_target_pairs={{0,48},{16,64},{32,80},{48,96},{64,112},{80,128},{96,144},{112,160... | collective-permute-start | bytes 589832 | tf_op jit(solution)/shard_map/ppermute | solution.py:316
  20.1 0.0 copy-start
  20.1 0.0 copy-start.1
  20.1 0.1 shard_map.86
  20.2 4.2 %collective-permute-start.8 = (bf16[256,256]{1,0:T(8,128)(2,1)S(1)}, bf16[256,256]{1,0:T(8,128)(2,1)S(1)}, u32[]{:S(2)}, u32[]{:S(2)}) collective-permute-start(bf16[256,256]{1,0:T(8,128)(2,1)S(1)} %get-tuple-element.42), channel_id=1, source_target_pairs={{2,0},{3,1},{4,2},{5,3},{6,4},{7,5},{0,6},{1,7},{14,8},{15,9},{8,1... | collective-permute-start | bytes 393224 | tf_op jit(solution)/shard_map/ppermute | solution.py:339
  24.4 2.0 %collective-permute-start.3 = (bf16[2,256,256]{2,1,0:T(8,128)(2,1)S(1)}, bf16[2,256,256]{2,1,0:T(8,128)(2,1)S(1)}, u32[]{:S(2)}, u32[]{:S(2)}) collective-permute-start(bf16[2,256,256]{2,1,0:T(8,128)(2,1)S(1)} %get-tuple-element.35), channel_id=1, source_target_pairs={{7,0},{0,1},{1,2},{2,3},{3,4},{4,5},{5,6},{6,7},{15,8},{8,9},{9,10... | collective-permute-start | bytes 786440 | tf_op jit(solution)/shard_map/ppermute | solution.py:323
  26.4 1.0 %shard_map.88 = (f32[4,128,128]{2,1,0:T(8,128)S(1)}, f32[4,128,128]{2,1,0:T(8,128)S(1)}, f32[256,256]{1,0:T(8,128)S(1)}, bf16[4,128,256]{2,1,0:T(8,128)(2,1)S(1)...) custom-call(f32[4,128,128]{2,1,0:T(8,128)S(1)} %get-tuple-element.36, ...), custom_call_target="tpu_custom_call" | custom-call | tf_op jit(solution)/shard_map/pallas_call | solution.py:49
  27.5 0.8 %collective-permute-done.8.c_ref = bf16[256,256]{1,0:T(8,128)(2,1)S(1)} collective-permute-done((bf16[256,256]{1,0:T(8,128)(2,1)S(1)}, bf16[256,256]{1,0:T(8,128)(2,1)S(1)}, u32[]{:S(2)}, u32[]{:S(2)}) %collective-permute-start.8) | collective-permute-done | bytes 131104 | tf_op jit(solution)/shard_map/ppermute | solution.py:339
  28.3 3.1 %collective-permute-done.2.a_ref = bf16[2,256,256]{2,1,0:T(8,128)(2,1)S(1)} collective-permute-done((bf16[2,256,256]{2,1,0:T(8,128)(2,1)S(1)}, bf16[2,256,256]{2,1,0:T(8,128)(2,1)S(1)}, u32[]{:S(2)}, u32[]{:S(2)}) %collective-permute-start.2) | collective-permute-done | bytes 262176 | tf_op jit(solution)/shard_map/ppermute | solution.py:323
  31.4 0.6 %collective-permute-done.3.b_ref = bf16[2,256,256]{2,1,0:T(8,128)(2,1)S(1)} collective-permute-done((bf16[2,256,256]{2,1,0:T(8,128)(2,1)S(1)}, bf16[2,256,256]{2,1,0:T(8,128)(2,1)S(1)}, u32[]{:S(2)}, u32[]{:S(2)}) %collective-permute-start.3) | collective-permute-done | bytes 262176 | tf_op jit(solution)/shard_map/ppermute | solution.py:323
  32.0 5.6 %shard_map.89 = (f32[256,256]{1,0:T(8,128)}, bf16[256,512]{1,0:T(8,128)(2,1)S(1)}, f32[4,128,128]{2,1,0:T(8,128)S(1)}) custom-call(bf16[2,256,256]{2,1,0:T(8,128)(2,1)S(1)} %collective-permute-done.2.a_ref, bf16[2,256,256]{2,1,0:T(8,128)(2,1)S(1)} %collective-permute-done.3.b_ref, bf16[256,256]{1,0:T(8,128)(2,1)S(1)} %collective-permute-done.8.c_ref, ...), custom_call_target="tpu_custom_call" | custom-call | flops 4294967296 | bytes 524288 | tf_op jit(solution)/shard_map/pallas_call | solution.py:354
  37.7 0.1 collective-permute-start.10
  37.8 0.8 %shard_map.90.pairs_ref = bf16[256,512]{1,0:T(8,128)(2,1)S(1)} custom-call(bf16[256,512]{1,0:T(8,128)(2,1)S(1)} %collective-permute-done.7.lag_ref, bf16[256,256]{1,0:T(8,128)(2,1)S(1)} %get-tuple-element.44.xb_ref, bf16[256,512]{1,0:T(8,128)(2,1)S(1)} %get-tuple-element.54.yo_ref), custom_call_target="tpu_custom_call" | custom-call | flops 67108864 | bytes 524288 | tf_op jit(solution)/shard_map/pallas_call | solution.py:49
  38.5 0.8 %collective-permute-done.10.other_ref = f32[4,128,128]{2,1,0:T(8,128)S(1)} collective-permute-done((f32[4,128,128]{2,1,0:T(8,128)S(1)}, f32[4,128,128]{2,1,0:T(8,128)S(1)}, u32[]{:S(2)}, u32[]{:S(2)}) %collective-permute-start.10) | collective-permute-done | bytes 262176 | tf_op jit(solution)/shard_map/ppermute | solution.py:316
  39.3 4.0 %collective-permute-start.11 = (bf16[400,128]{1,0:T(8,128)(2,1)S(1)}, bf16[400,128]{1,0:T(8,128)(2,1)S(1)}, u32[]{:S(2)}, u32[]{:S(2)}) collective-permute-start(bf16[400,128]{1,0:T(8,128)(2,1)S(1)} %shard_map.91), channel_id=1, source_target_pairs={{16,0},{40,8},{32,16},{56,24},{48,32},{72,40},{64,48},{88,56},{80,... | collective-permute-start | bytes 307208 | tf_op jit(solution)/shard_map/ppermute | solution.py:316
  43.3 2.1 %collective-permute-start.12 = (bf16[400,128]{1,0:T(8,128)(2,1)S(1)}, bf16[400,128]{1,0:T(8,128)(2,1)S(1)}, u32[]{:S(2)}, u32[]{:S(2)}) collective-permute-start(bf16[400,128]{1,0:T(8,128)(2,1)S(1)} %shard_map.91), channel_id=1, source_target_pairs={{48,0},{64,16},{80,32},{96,48},{112,64},{128,80},{144,96},{160,112... | collective-permute-start | bytes 307208 | tf_op jit(solution)/shard_map/ppermute | solution.py:316
  45.4 0.3 shard_map.93
  45.7 1.9 %collective-permute-start.14 = (bf16[256,512]{1,0:T(8,128)(2,1)S(1)}, bf16[256,512]{1,0:T(8,128)(2,1)S(1)}, u32[]{:S(2)}, u32[]{:S(2)}) collective-permute-start(bf16[256,512]{1,0:T(8,128)(2,1)S(1)} %shard_map.93), channel_id=1, source_target_pairs={{64,0},{72,8},{80,16},{88,24},{96,32},{104,40},{112,48},{120,56},{... | collective-permute-start | bytes 786440 | tf_op jit(solution)/shard_map/ppermute | solution.py:316
  47.7 3.4 %collective-permute-done.12.q2_ref = bf16[400,128]{1,0:T(8,128)(2,1)S(1)} collective-permute-done((bf16[400,128]{1,0:T(8,128)(2,1)S(1)}, bf16[400,128]{1,0:T(8,128)(2,1)S(1)}, u32[]{:S(2)}, u32[]{:S(2)}) %collective-permute-start.12) | collective-permute-done | bytes 102432 | tf_op jit(solution)/shard_map/ppermute | solution.py:316
  51.1 0.1 shard_map.92
  51.2 0.1 collective-permute-start.13
  51.3 0.8 %shard_map.94 = (f32[256,256]{1,0:T(8,128)S(1)}, f32[256,256]{1,0:T(8,128)S(1)}) custom-call(bf16[256,512]{1,0:T(8,128)(2,1)S(1)} %get-tuple-element.37.kv_ref, bf16[256,256]{1,0:T(8,128)(2,1)S(1)} %get-tuple-element.44.xb_ref, bf16[256,512]{1,0:T(8,128)(2,1)S(1)} %get-tuple-element.54.yo_ref), custom_call_target="tpu_custom_call" | custom-call | flops 67108864 | bytes 524288 | tf_op jit(solution)/shard_map/pallas_call | solution.py:49
  52.1 2.8 %collective-permute-done.14.early_ref = bf16[256,512]{1,0:T(8,128)(2,1)S(1)} collective-permute-done((bf16[256,512]{1,0:T(8,128)(2,1)S(1)}, bf16[256,512]{1,0:T(8,128)(2,1)S(1)}, u32[]{:S(2)}, u32[]{:S(2)}) %collective-permute-start.14) | collective-permute-done | bytes 262176 | tf_op jit(solution)/shard_map/ppermute | solution.py:316
  54.9 1.2 %shard_map.95 = (f32[256,256]{1,0:T(8,128)}, f32[256,256]{1,0:T(8,128)}) custom-call(bf16[256,512]{1,0:T(8,128)(2,1)S(1)} %get-tuple-element.37.kv_ref, f32[4,128,128]{2,1,0:T(8,128)S(1)} %get-tuple-element.56.part_ref, f32[4,128,128]{2,1,0:T(8,128)S(1)} %collective-permute-done.13.recv_ref, bf16[256,512]{1,0:T(8,128)(2,1)S(1)} %collective-permute-done.14.early_ref, ...), custom_call_target="tpu_custom_call" | custom-call | bytes 524288 | tf_op jit(solution)/shard_map/pallas_call | solution.py:49
  (18 shorter events, 0.1 us)
Async XLA Ops:
  1.7 0.9 %copy-start.3 = (bf16[256,256]{1,0:T(8,128)(2,1)S(1)}, bf16[256,256]{1,0:T(8,128)(2,1)}, u32[]{:S(2)}) copy-start(bf16[256,256]{1,0:T(8,128)(2,1)} %param.8) | copy-start | bytes 393220
  2.0 10.3 %collective-permute-start.4 = (f32[4,128,128]{2,1,0:T(8,128)S(1)}, f32[4,128,128]{2,1,0:T(8,128)S(1)}, u32[]{:S(2)}, u32[]{:S(2)}) collective-permute-start(f32[4,128,128]{2,1,0:T(8,128)S(1)} %get-tuple-element.36.own_ref.t_ref), channel_id=1, source_target_pairs={{8,0},{0,8},{24,16},{16,24},{40,32},{32,40},{56,48},{48,56},{72,64... | collective-permute-start | bytes 786440 | tf_op jit(solution)/shard_map/ppermute | solution.py:316
  2.6 17.5 %collective-permute-start = (bf16[256,256]{1,0:T(8,128)(2,1)S(1)}, bf16[256,256]{1,0:T(8,128)(2,1)S(1)}, u32[]{:S(2)}, u32[]{:S(2)}) collective-permute-start(bf16[256,256]{1,0:T(8,128)(2,1)S(1)} %copy-done.3), channel_id=1, source_target_pairs={{2,0},{3,1},{4,2},{5,3},{6,4},{7,5},{0,6},{1,7},{10,8},{11,9},{12,... | collective-permute-start | bytes 393224 | tf_op jit(solution)/shard_map/ppermute | solution.py:323
  8.9 11.2 %collective-permute-start.1 = (bf16[256,256]{1,0:T(8,128)(2,1)S(1)}, bf16[256,256]{1,0:T(8,128)(2,1)S(1)}, u32[]{:S(2)}, u32[]{:S(2)}) collective-permute-start(bf16[256,256]{1,0:T(8,128)(2,1)S(1)} %copy-done.3), channel_id=1, source_target_pairs={{6,0},{7,1},{0,2},{1,3},{2,4},{3,5},{4,6},{5,7},{14,8},{15,9},{8,1... | collective-permute-start | bytes 393224 | tf_op jit(solution)/shard_map/ppermute | solution.py:323
  8.9 15.5 %collective-permute-start.7 = (bf16[256,512]{1,0:T(8,128)(2,1)S(1)}, bf16[256,512]{1,0:T(8,128)(2,1)S(1)}, u32[]{:S(2)}, u32[]{:S(2)}) collective-permute-start(bf16[256,512]{1,0:T(8,128)(2,1)S(1)} %get-tuple-element.37.kv_ref), channel_id=1, source_target_pairs={{0,64},{8,72},{16,80},{24,88},{32,96},{40,104},{48,112},{56,120},{... | collective-permute-start | bytes 786440 | tf_op jit(solution)/shard_map/ppermute | solution.py:316
  12.4 14.0 %collective-permute-start.5 = (bf16[6,128,128]{2,1,0:T(8,128)(2,1)S(1)}, bf16[6,128,128]{2,1,0:T(8,128)(2,1)S(1)}, u32[]{:S(2)}, u32[]{:S(2)}) collective-permute-start(bf16[6,128,128]{2,1,0:T(8,128)(2,1)S(1)} %shard_map.87), channel_id=1, source_target_pairs={{0,16},{16,32},{8,40},{32,48},{24,56},{48,64},{40,72},{64,80},{56,... | collective-permute-start | bytes 589832 | tf_op jit(solution)/shard_map/ppermute | solution.py:316
  15.8 10.6 %collective-permute-start.6 = (bf16[6,128,128]{2,1,0:T(8,128)(2,1)S(1)}, bf16[6,128,128]{2,1,0:T(8,128)(2,1)S(1)}, u32[]{:S(2)}, u32[]{:S(2)}) collective-permute-start(bf16[6,128,128]{2,1,0:T(8,128)(2,1)S(1)} %shard_map.87), channel_id=1, source_target_pairs={{0,48},{16,64},{32,80},{48,96},{64,112},{80,128},{96,144},{112,160... | collective-permute-start | bytes 589832 | tf_op jit(solution)/shard_map/ppermute | solution.py:316
  20.1 6.3 %copy-start = (bf16[256,2048]{1,0:T(8,128)(2,1)S(1)}, bf16[256,2048]{1,0:T(8,128)(2,1)}, u32[]{:S(2)}) copy-start(bf16[256,2048]{1,0:T(8,128)(2,1)} %w_ref.3) | copy-start | bytes 3145732
  20.1 6.3 %copy-start.1 = (f32[256,256]{1,0:T(8,128)S(1)}, f32[256,256]{1,0:T(8,128)}, u32[]{:S(2)}) copy-start(f32[256,256]{1,0:T(8,128)} %x_ref.1) | copy-start | bytes 786436
  20.2 8.1 %collective-permute-start.8 = (bf16[256,256]{1,0:T(8,128)(2,1)S(1)}, bf16[256,256]{1,0:T(8,128)(2,1)S(1)}, u32[]{:S(2)}, u32[]{:S(2)}) collective-permute-start(bf16[256,256]{1,0:T(8,128)(2,1)S(1)} %get-tuple-element.42), channel_id=1, source_target_pairs={{2,0},{3,1},{4,2},{5,3},{6,4},{7,5},{0,6},{1,7},{14,8},{15,9},{8,1... | collective-permute-start | bytes 393224 | tf_op jit(solution)/shard_map/ppermute | solution.py:339
  24.4 2.1 %copy-start.2 = (f32[2]{0:T(128)S(1)}, f32[2]{0:T(128)}, u32[]{:S(2)}) copy-start(f32[2]{0:T(128)} %ridge_ref.1) | copy-start | bytes 28
  24.4 7.0 %collective-permute-start.2 = (bf16[2,256,256]{2,1,0:T(8,128)(2,1)S(1)}, bf16[2,256,256]{2,1,0:T(8,128)(2,1)S(1)}, u32[]{:S(2)}, u32[]{:S(2)}) collective-permute-start(bf16[2,256,256]{2,1,0:T(8,128)(2,1)S(1)} %get-tuple-element.34), channel_id=1, source_target_pairs={{1,0},{2,1},{3,2},{4,3},{5,4},{6,5},{7,6},{0,7},{9,8},{10,9},{11,1... | collective-permute-start | bytes 786440 | tf_op jit(solution)/shard_map/ppermute | solution.py:323
  24.4 7.7 %collective-permute-start.3 = (bf16[2,256,256]{2,1,0:T(8,128)(2,1)S(1)}, bf16[2,256,256]{2,1,0:T(8,128)(2,1)S(1)}, u32[]{:S(2)}, u32[]{:S(2)}) collective-permute-start(bf16[2,256,256]{2,1,0:T(8,128)(2,1)S(1)} %get-tuple-element.35), channel_id=1, source_target_pairs={{7,0},{0,1},{1,2},{2,3},{3,4},{4,5},{5,6},{6,7},{15,8},{8,9},{9,10... | collective-permute-start | bytes 786440 | tf_op jit(solution)/shard_map/ppermute | solution.py:323
  28.3 3.8 %collective-permute-start.9 = (f32[4,128,128]{2,1,0:T(8,128)S(1)}, f32[4,128,128]{2,1,0:T(8,128)S(1)}, u32[]{:S(2)}, u32[]{:S(2)}) collective-permute-start(f32[4,128,128]{2,1,0:T(8,128)S(1)} %get-tuple-element.47), channel_id=1, source_target_pairs={{8,0},{0,8},{24,16},{16,24},{40,32},{32,40},{56,48},{48,56},{72,64... | collective-permute-start | bytes 786440 | tf_op jit(solution)/shard_map/ppermute | solution.py:316
  37.7 1.6 %collective-permute-start.10 = (f32[4,128,128]{2,1,0:T(8,128)S(1)}, f32[4,128,128]{2,1,0:T(8,128)S(1)}, u32[]{:S(2)}, u32[]{:S(2)}) collective-permute-start(f32[4,128,128]{2,1,0:T(8,128)S(1)} %get-tuple-element.53.own_ref), channel_id=1, source_target_pairs={{8,0},{0,8},{24,16},{16,24},{40,32},{32,40},{56,48},{48,56},{72,64... | collective-permute-start | bytes 786440 | tf_op jit(solution)/shard_map/ppermute | solution.py:316
  39.3 8.3 %collective-permute-start.11 = (bf16[400,128]{1,0:T(8,128)(2,1)S(1)}, bf16[400,128]{1,0:T(8,128)(2,1)S(1)}, u32[]{:S(2)}, u32[]{:S(2)}) collective-permute-start(bf16[400,128]{1,0:T(8,128)(2,1)S(1)} %shard_map.91), channel_id=1, source_target_pairs={{16,0},{40,8},{32,16},{56,24},{48,32},{72,40},{64,48},{88,56},{80,... | collective-permute-start | bytes 307208 | tf_op jit(solution)/shard_map/ppermute | solution.py:316
  43.3 7.8 %collective-permute-start.12 = (bf16[400,128]{1,0:T(8,128)(2,1)S(1)}, bf16[400,128]{1,0:T(8,128)(2,1)S(1)}, u32[]{:S(2)}, u32[]{:S(2)}) collective-permute-start(bf16[400,128]{1,0:T(8,128)(2,1)S(1)} %shard_map.91), channel_id=1, source_target_pairs={{48,0},{64,16},{80,32},{96,48},{112,64},{128,80},{144,96},{160,112... | collective-permute-start | bytes 307208 | tf_op jit(solution)/shard_map/ppermute | solution.py:316
  45.7 9.2 %collective-permute-start.14 = (bf16[256,512]{1,0:T(8,128)(2,1)S(1)}, bf16[256,512]{1,0:T(8,128)(2,1)S(1)}, u32[]{:S(2)}, u32[]{:S(2)}) collective-permute-start(bf16[256,512]{1,0:T(8,128)(2,1)S(1)} %shard_map.93), channel_id=1, source_target_pairs={{64,0},{72,8},{80,16},{88,24},{96,32},{104,40},{112,48},{120,56},{... | collective-permute-start | bytes 786440 | tf_op jit(solution)/shard_map/ppermute | solution.py:316
  51.2 3.7 %collective-permute-start.13 = (f32[4,128,128]{2,1,0:T(8,128)S(1)}, f32[4,128,128]{2,1,0:T(8,128)S(1)}, u32[]{:S(2)}, u32[]{:S(2)}) collective-permute-start(f32[4,128,128]{2,1,0:T(8,128)S(1)} %get-tuple-element.57), channel_id=1, source_target_pairs={{8,0},{0,8},{24,16},{16,24},{40,32},{32,40},{56,48},{48,56},{72,64... | collective-permute-start | bytes 786440 | tf_op jit(solution)/shard_map/ppermute | solution.py:316

commit v7 on v6

--- a/solution.py
+++ b/solution.py
@@ -84,26 +84,43 @@
     return whole[:DH], whole[DH:]
 
 
+def square():
+    r, c = tri(DH, DH)
+    return r > c, r == c
+
+
 def chip_states(own_ref, other_ref, out_ref):
-    for h in range(NH):
-        out_ref[h] = (own_ref[h] + other_ref[h]).astype(BF16)
+    below, level = square()
+    first, second = own_ref[0] + other_ref[0], own_ref[1] + other_ref[1]
+    out_ref[:DH] = jnp.where(below | level, first, second).astype(BF16)
+    diagonal = jnp.sum(jnp.where(level, second, 0.0), axis=0, keepdims=True)
+    out_ref[DH : DH + 16] = jnp.broadcast_to(diagonal, (16, DH)).astype(BF16)
+    for h in range(NH):
         hi, lo = split(own_ref[NH + h] + other_ref[NH + h])
-        out_ref[NH + h] = hi
-        out_ref[2 * NH + h] = lo
+        at = DH + 16 + 2 * h * DH
+        out_ref[at : at + DH] = hi
+        out_ref[at + DH : at + 2 * DH] = lo
 
 
 def states_to_send(
     t_ref, lag_ref, p1_ref, p2_ref, kv_ref, d_ref, up_ref, down_ref, w_ref, x_ref, ridge_ref,
     part_ref, send_ref, out_ref, turned_ref, near_ref, xb_ref, xlo_ref, rid_ref,
 ):
+    below, level = square()
+    total = p1_ref[...].astype(F32) + p2_ref[...].astype(F32)
+    mixed, turned = total[:DH], total[:DH].T
+    grams = (
+        jnp.where(below | level, mixed, turned),
+        jnp.where(level, total[DH : DH + 1], jnp.where(below, turned, mixed)),
+    )
     core = lax.rem(lax.axis_index("seq"), 2)
     for h in range(NH):
         k = head(lag_ref, h)
         lag_g = mm_tn(k, k)
         lag_s = mm_tn(head(lag_ref, h, NH * DH), k)
-        gram = p1_ref[h].astype(F32) + p2_ref[h].astype(F32)
-        state = p1_ref[NH + h].astype(F32) + p2_ref[NH + h].astype(F32)
-        state = state + p1_ref[2 * NH + h].astype(F32) + p2_ref[2 * NH + h].astype(F32)
+        gram = grams[h]
+        at = DH + 16 + 2 * h * DH
+        state = total[at : at + DH] + total[at + DH : at + 2 * DH]
         for at, lag, part in ((h, lag_g, gram), (NH + h, lag_s, state)):
             part_ref[at] = part
             send_ref[at] = part + jnp.where(core == 0, t_ref[at], lag)
@@ -245,11 +262,6 @@
         gv_ref[:, h * DH : (h + 1) * DH] = gv
 
 
-def square():
-    r, c = tri(DH, DH)
-    return r > c, r == c
-
-
 def chip_sums(own_ref, other_ref, out_ref):
     below, level = square()
     first, second = own_ref[0] + other_ref[0], own_ref[1] + other_ref[1]
@@ -327,7 +339,7 @@
     kvd = jnp.concatenate([key_rows, values, d_layer], axis=1)
     own, kv, dv = call(own_states, [(st, F32), ((TOK, 512), BF16), flat], kvd)
     kv_lag = moved(kv, lambda i: i - lag)
-    (chip,) = call(chip_states, [((3 * NH, DH, DH), BF16)], own, swapped(own))
+    (chip,) = call(chip_states, [((5 * DH + 16, DH), BF16)], own, swapped(own))
     pair = (2, TOK, 256)
     up_two, down_two, across = call(
         to_forward, [(pair, BF16), (pair, BF16), flat], dv, up, down, flops=1 << 34

time: 56.5 us -> 56.6 us (level)
  no operation moved by 1% of the time
where the time goes in v7:
time: 56.6 us; the launch traced here: 56 us
  starting transfers between devices  31.9 us (56%)
  waiting for transfers between devices  11.5 us (20%)
  Pallas kernels  10.1 us (18%)
  other arithmetic  1.06 us (2%)
  between operations  0.85 us (2%)
    ppermute x10, starting transfers between devices, moved(): return lax.ppermute(value, 'seq', route)  19.4 us
    ppermute x4, starting transfers between devices, around(): return lax.ppermute(value, 'head', [((i + away) % 8, i) for i in range(8)])  8.33 us
    ppermute x10, waiting for transfers between devices, moved(): return lax.ppermute(value, 'seq', route)  6.99 us
    pallas_call x1, Pallas kernels, body(): pl.pallas_call(adjoints, out_shape=[jax.ShapeDtypeStruct((TOK, 256), F32)...  5.61 us
    pallas_call x10, Pallas kernels, call(): pl.pallas_call(kernel, out_shape=[jax.ShapeDtypeStruct(s, d) for s, d in...  4.5 us
    ppermute x1, starting transfers between devices, body(): across = lax.ppermute(across, ('seq', 'head'), far)  4.21 us
    ppermute x4, waiting for transfers between devices, around(): return lax.ppermute(value, 'head', [((i + away) % 8, i) for i in range(8)])  3.75 us
  transfers between devices with their start and end apart: 15, of which 6 were waited for; matrix products, arithmetic and copies ran while one was open for 0% of the time, Pallas kernels for 5%

profile of v7, /device:TPU:2, one launch (start us, length us, event | category | flops | bytes accessed | tf_op | source)
XLA Modules:
  0.0 56.0 jit_solution(13786245159885138768)
XLA Ops:
  0.6 1.1 %pad_maximum_fusion.kvd_ref = bf16[256,768]{1,0:T(8,128)(2,1)S(1)} fusion(bf16[256,256]{1,0:T(8,128)(2,1)} %param.8, bf16[256,256]{1,0:T(8,128)(2,1)} %param.7, bf16[256,256]{1,0:T(8,128)(2,1)} %param.6), kind=kLoop, calls=%fused_computation | loop fusion | flops 1179648 | bytes 786432 | tf_op jit(solution)/shard_map/concatenate | solution.py:339
  1.7 0.0 copy-start.3
  1.7 0.3 shard_map.85
  2.0 0.1 collective-permute-start.4
  2.1 0.5 copy-done.3
  2.6 6.3 %collective-permute-start = (bf16[256,256]{1,0:T(8,128)(2,1)S(1)}, bf16[256,256]{1,0:T(8,128)(2,1)S(1)}, u32[]{:S(2)}, u32[]{:S(2)}) collective-permute-start(bf16[256,256]{1,0:T(8,128)(2,1)S(1)} %copy-done.3), channel_id=1, source_target_pairs={{2,0},{3,1},{4,2},{5,3},{6,4},{7,5},{0,6},{1,7},{10,8},{11,9},{12,... | collective-permute-start | bytes 393224 | tf_op jit(solution)/shard_map/ppermute | solution.py:335
  8.9 3.4 %collective-permute-start.7 = (bf16[256,512]{1,0:T(8,128)(2,1)S(1)}, bf16[256,512]{1,0:T(8,128)(2,1)S(1)}, u32[]{:S(2)}, u32[]{:S(2)}) collective-permute-start(bf16[256,512]{1,0:T(8,128)(2,1)S(1)} %get-tuple-element.37.kv_ref), channel_id=1, source_target_pairs={{0,64},{8,72},{16,80},{24,88},{32,96},{40,104},{48,112},{56,120},{... | collective-permute-start | bytes 786440 | tf_op jit(solution)/shard_map/ppermute | solution.py:328
  12.3 0.1 shard_map.87
  12.4 3.5 %collective-permute-start.5 = (bf16[656,128]{1,0:T(8,128)(2,1)S(1)}, bf16[656,128]{1,0:T(8,128)(2,1)S(1)}, u32[]{:S(2)}, u32[]{:S(2)}) collective-permute-start(bf16[656,128]{1,0:T(8,128)(2,1)S(1)} %shard_map.87), channel_id=1, source_target_pairs={{0,16},{16,32},{8,40},{32,48},{24,56},{48,64},{40,72},{64,80},{56,... | collective-permute-start | bytes 503816 | tf_op jit(solution)/shard_map/ppermute | solution.py:328
  15.9 4.2 %collective-permute-start.6 = (bf16[656,128]{1,0:T(8,128)(2,1)S(1)}, bf16[656,128]{1,0:T(8,128)(2,1)S(1)}, u32[]{:S(2)}, u32[]{:S(2)}) collective-permute-start(bf16[656,128]{1,0:T(8,128)(2,1)S(1)} %shard_map.87), channel_id=1, source_target_pairs={{0,48},{16,64},{32,80},{48,96},{64,112},{80,128},{96,144},{112,160... | collective-permute-start | bytes 503816 | tf_op jit(solution)/shard_map/ppermute | solution.py:328
  20.1 0.0 copy-start
  20.1 0.1 shard_map.86
  20.2 4.2 %collective-permute-start.8 = (bf16[256,256]{1,0:T(8,128)(2,1)S(1)}, bf16[256,256]{1,0:T(8,128)(2,1)S(1)}, u32[]{:S(2)}, u32[]{:S(2)}) collective-permute-start(bf16[256,256]{1,0:T(8,128)(2,1)S(1)} %get-tuple-element.42), channel_id=1, source_target_pairs={{2,0},{3,1},{4,2},{5,3},{6,4},{7,5},{0,6},{1,7},{14,8},{15,9},{8,1... | collective-permute-start | bytes 393224 | tf_op jit(solution)/shard_map/ppermute | solution.py:351
  24.4 2.0 %collective-permute-start.3 = (bf16[2,256,256]{2,1,0:T(8,128)(2,1)S(1)}, bf16[2,256,256]{2,1,0:T(8,128)(2,1)S(1)}, u32[]{:S(2)}, u32[]{:S(2)}) collective-permute-start(bf16[2,256,256]{2,1,0:T(8,128)(2,1)S(1)} %get-tuple-element.35), channel_id=1, source_target_pairs={{7,0},{0,1},{1,2},{2,3},{3,4},{4,5},{5,6},{6,7},{15,8},{8,9},{9,10... | collective-permute-start | bytes 786440 | tf_op jit(solution)/shard_map/ppermute | solution.py:335
  26.4 1.1 %shard_map.88 = (f32[4,128,128]{2,1,0:T(8,128)S(1)}, f32[4,128,128]{2,1,0:T(8,128)S(1)}, f32[256,256]{1,0:T(8,128)S(1)}, bf16[4,128,256]{2,1,0:T(8,128)(2,1)S(1)...) custom-call(f32[4,128,128]{2,1,0:T(8,128)S(1)} %get-tuple-element.36, ...), custom_call_target="tpu_custom_call" | custom-call | tf_op jit(solution)/shard_map/pallas_call | solution.py:49
  27.5 0.8 %collective-permute-done.8.c_ref = bf16[256,256]{1,0:T(8,128)(2,1)S(1)} collective-permute-done((bf16[256,256]{1,0:T(8,128)(2,1)S(1)}, bf16[256,256]{1,0:T(8,128)(2,1)S(1)}, u32[]{:S(2)}, u32[]{:S(2)}) %collective-permute-start.8) | collective-permute-done | bytes 131104 | tf_op jit(solution)/shard_map/ppermute | solution.py:351
  28.3 3.1 %collective-permute-done.2.a_ref = bf16[2,256,256]{2,1,0:T(8,128)(2,1)S(1)} collective-permute-done((bf16[2,256,256]{2,1,0:T(8,128)(2,1)S(1)}, bf16[2,256,256]{2,1,0:T(8,128)(2,1)S(1)}, u32[]{:S(2)}, u32[]{:S(2)}) %collective-permute-start.2) | collective-permute-done | bytes 262176 | tf_op jit(solution)/shard_map/ppermute | solution.py:335
  31.5 0.6 %collective-permute-done.3.b_ref = bf16[2,256,256]{2,1,0:T(8,128)(2,1)S(1)} collective-permute-done((bf16[2,256,256]{2,1,0:T(8,128)(2,1)S(1)}, bf16[2,256,256]{2,1,0:T(8,128)(2,1)S(1)}, u32[]{:S(2)}, u32[]{:S(2)}) %collective-permute-start.3) | collective-permute-done | bytes 262176 | tf_op jit(solution)/shard_map/ppermute | solution.py:335
  32.1 5.6 %shard_map.89 = (f32[256,256]{1,0:T(8,128)}, bf16[256,512]{1,0:T(8,128)(2,1)S(1)}, f32[4,128,128]{2,1,0:T(8,128)S(1)}) custom-call(bf16[2,256,256]{2,1,0:T(8,128)(2,1)S(1)} %collective-permute-done.2.a_ref, bf16[2,256,256]{2,1,0:T(8,128)(2,1)S(1)} %collective-permute-done.3.b_ref, bf16[256,256]{1,0:T(8,128)(2,1)S(1)} %collective-permute-done.8.c_ref, ...), custom_call_target="tpu_custom_call" | custom-call | flops 4294967296 | bytes 524288 | tf_op jit(solution)/shard_map/pallas_call | solution.py:366
  37.7 0.1 collective-permute-start.10
  37.8 0.8 %shard_map.90.pairs_ref = bf16[256,512]{1,0:T(8,128)(2,1)S(1)} custom-call(bf16[256,512]{1,0:T(8,128)(2,1)S(1)} %collective-permute-done.7.lag_ref, bf16[256,256]{1,0:T(8,128)(2,1)S(1)} %get-tuple-element.44.xb_ref, bf16[256,512]{1,0:T(8,128)(2,1)S(1)} %get-tuple-element.54.yo_ref), custom_call_target="tpu_custom_call" | custom-call | flops 67108864 | bytes 524288 | tf_op jit(solution)/shard_map/pallas_call | solution.py:49
  38.5 0.8 %collective-permute-done.10.other_ref = f32[4,128,128]{2,1,0:T(8,128)S(1)} collective-permute-done((f32[4,128,128]{2,1,0:T(8,128)S(1)}, f32[4,128,128]{2,1,0:T(8,128)S(1)}, u32[]{:S(2)}, u32[]{:S(2)}) %collective-permute-start.10) | collective-permute-done | bytes 262176 | tf_op jit(solution)/shard_map/ppermute | solution.py:328
  39.3 4.0 %collective-permute-start.11 = (bf16[400,128]{1,0:T(8,128)(2,1)S(1)}, bf16[400,128]{1,0:T(8,128)(2,1)S(1)}, u32[]{:S(2)}, u32[]{:S(2)}) collective-permute-start(bf16[400,128]{1,0:T(8,128)(2,1)S(1)} %shard_map.91), channel_id=1, source_target_pairs={{16,0},{40,8},{32,16},{56,24},{48,32},{72,40},{64,48},{88,56},{80,... | collective-permute-start | bytes 307208 | tf_op jit(solution)/shard_map/ppermute | solution.py:328
  43.3 2.1 %collective-permute-start.12 = (bf16[400,128]{1,0:T(8,128)(2,1)S(1)}, bf16[400,128]{1,0:T(8,128)(2,1)S(1)}, u32[]{:S(2)}, u32[]{:S(2)}) collective-permute-start(bf16[400,128]{1,0:T(8,128)(2,1)S(1)} %shard_map.91), channel_id=1, source_target_pairs={{48,0},{64,16},{80,32},{96,48},{112,64},{128,80},{144,96},{160,112... | collective-permute-start | bytes 307208 | tf_op jit(solution)/shard_map/ppermute | solution.py:328
  45.5 0.3 shard_map.93
  45.7 1.9 %collective-permute-start.14 = (bf16[256,512]{1,0:T(8,128)(2,1)S(1)}, bf16[256,512]{1,0:T(8,128)(2,1)S(1)}, u32[]{:S(2)}, u32[]{:S(2)}) collective-permute-start(bf16[256,512]{1,0:T(8,128)(2,1)S(1)} %shard_map.93), channel_id=1, source_target_pairs={{64,0},{72,8},{80,16},{88,24},{96,32},{104,40},{112,48},{120,56},{... | collective-permute-start | bytes 786440 | tf_op jit(solution)/shard_map/ppermute | solution.py:328
  47.7 3.4 %collective-permute-done.12.q2_ref = bf16[400,128]{1,0:T(8,128)(2,1)S(1)} collective-permute-done((bf16[400,128]{1,0:T(8,128)(2,1)S(1)}, bf16[400,128]{1,0:T(8,128)(2,1)S(1)}, u32[]{:S(2)}, u32[]{:S(2)}) %collective-permute-start.12) | collective-permute-done | bytes 102432 | tf_op jit(solution)/shard_map/ppermute | solution.py:328
  51.1 0.1 shard_map.92
  51.2 0.1 collective-permute-start.13
  51.3 0.8 %shard_map.94 = (f32[256,256]{1,0:T(8,128)S(1)}, f32[256,256]{1,0:T(8,128)S(1)}) custom-call(bf16[256,512]{1,0:T(8,128)(2,1)S(1)} %get-tuple-element.37.kv_ref, bf16[256,256]{1,0:T(8,128)(2,1)S(1)} %get-tuple-element.44.xb_ref, bf16[256,512]{1,0:T(8,128)(2,1)S(1)} %get-tuple-element.54.yo_ref), custom_call_target="tpu_custom_call" | custom-call | flops 67108864 | bytes 524288 | tf_op jit(solution)/shard_map/pallas_call | solution.py:49
  52.1 2.8 %collective-permute-done.14.early_ref = bf16[256,512]{1,0:T(8,128)(2,1)S(1)} collective-permute-done((bf16[256,512]{1,0:T(8,128)(2,1)S(1)}, bf16[256,512]{1,0:T(8,128)(2,1)S(1)}, u32[]{:S(2)}, u32[]{:S(2)}) %collective-permute-start.14) | collective-permute-done | bytes 262176 | tf_op jit(solution)/shard_map/ppermute | solution.py:328
  54.9 1.2 %shard_map.95 = (f32[256,256]{1,0:T(8,128)}, f32[256,256]{1,0:T(8,128)}) custom-call(bf16[256,512]{1,0:T(8,128)(2,1)S(1)} %get-tuple-element.37.kv_ref, f32[4,128,128]{2,1,0:T(8,128)S(1)} %get-tuple-element.56.part_ref, f32[4,128,128]{2,1,0:T(8,128)S(1)} %collective-permute-done.13.recv_ref, bf16[256,512]{1,0:T(8,128)(2,1)S(1)} %collective-permute-done.14.early_ref, ...), custom_call_target="tpu_custom_call" | custom-call | bytes 524288 | tf_op jit(solution)/shard_map/pallas_call | solution.py:49
  (18 shorter events, 0.1 us)
Async XLA Ops:
  1.7 0.9 %copy-start.3 = (bf16[256,256]{1,0:T(8,128)(2,1)S(1)}, bf16[256,256]{1,0:T(8,128)(2,1)}, u32[]{:S(2)}) copy-start(bf16[256,256]{1,0:T(8,128)(2,1)} %param.8) | copy-start | bytes 393220
  2.0 10.3 %collective-permute-start.4 = (f32[4,128,128]{2,1,0:T(8,128)S(1)}, f32[4,128,128]{2,1,0:T(8,128)S(1)}, u32[]{:S(2)}, u32[]{:S(2)}) collective-permute-start(f32[4,128,128]{2,1,0:T(8,128)S(1)} %get-tuple-element.36.own_ref.t_ref), channel_id=1, source_target_pairs={{8,0},{0,8},{24,16},{16,24},{40,32},{32,40},{56,48},{48,56},{72,64... | collective-permute-start | bytes 786440 | tf_op jit(solution)/shard_map/ppermute | solution.py:328
  2.6 17.5 %collective-permute-start = (bf16[256,256]{1,0:T(8,128)(2,1)S(1)}, bf16[256,256]{1,0:T(8,128)(2,1)S(1)}, u32[]{:S(2)}, u32[]{:S(2)}) collective-permute-start(bf16[256,256]{1,0:T(8,128)(2,1)S(1)} %copy-done.3), channel_id=1, source_target_pairs={{2,0},{3,1},{4,2},{5,3},{6,4},{7,5},{0,6},{1,7},{10,8},{11,9},{12,... | collective-permute-start | bytes 393224 | tf_op jit(solution)/shard_map/ppermute | solution.py:335
  8.9 11.2 %collective-permute-start.1 = (bf16[256,256]{1,0:T(8,128)(2,1)S(1)}, bf16[256,256]{1,0:T(8,128)(2,1)S(1)}, u32[]{:S(2)}, u32[]{:S(2)}) collective-permute-start(bf16[256,256]{1,0:T(8,128)(2,1)S(1)} %copy-done.3), channel_id=1, source_target_pairs={{6,0},{7,1},{0,2},{1,3},{2,4},{3,5},{4,6},{5,7},{14,8},{15,9},{8,1... | collective-permute-start | bytes 393224 | tf_op jit(solution)/shard_map/ppermute | solution.py:335
  8.9 15.5 %collective-permute-start.7 = (bf16[256,512]{1,0:T(8,128)(2,1)S(1)}, bf16[256,512]{1,0:T(8,128)(2,1)S(1)}, u32[]{:S(2)}, u32[]{:S(2)}) collective-permute-start(bf16[256,512]{1,0:T(8,128)(2,1)S(1)} %get-tuple-element.37.kv_ref), channel_id=1, source_target_pairs={{0,64},{8,72},{16,80},{24,88},{32,96},{40,104},{48,112},{56,120},{... | collective-permute-start | bytes 786440 | tf_op jit(solution)/shard_map/ppermute | solution.py:328
  12.4 14.0 %collective-permute-start.5 = (bf16[656,128]{1,0:T(8,128)(2,1)S(1)}, bf16[656,128]{1,0:T(8,128)(2,1)S(1)}, u32[]{:S(2)}, u32[]{:S(2)}) collective-permute-start(bf16[656,128]{1,0:T(8,128)(2,1)S(1)} %shard_map.87), channel_id=1, source_target_pairs={{0,16},{16,32},{8,40},{32,48},{24,56},{48,64},{40,72},{64,80},{56,... | collective-permute-start | bytes 503816 | tf_op jit(solution)/shard_map/ppermute | solution.py:328
  15.9 10.6 %collective-permute-start.6 = (bf16[656,128]{1,0:T(8,128)(2,1)S(1)}, bf16[656,128]{1,0:T(8,128)(2,1)S(1)}, u32[]{:S(2)}, u32[]{:S(2)}) collective-permute-start(bf16[656,128]{1,0:T(8,128)(2,1)S(1)} %shard_map.87), channel_id=1, source_target_pairs={{0,48},{16,64},{32,80},{48,96},{64,112},{80,128},{96,144},{112,160... | collective-permute-start | bytes 503816 | tf_op jit(solution)/shard_map/ppermute | solution.py:328
  20.1 6.3 %copy-start = (bf16[256,2048]{1,0:T(8,128)(2,1)S(1)}, bf16[256,2048]{1,0:T(8,128)(2,1)}, u32[]{:S(2)}) copy-start(bf16[256,2048]{1,0:T(8,128)(2,1)} %w_ref.3) | copy-start | bytes 3145732
  20.1 6.3 %copy-start.1 = (f32[256,256]{1,0:T(8,128)S(1)}, f32[256,256]{1,0:T(8,128)}, u32[]{:S(2)}) copy-start(f32[256,256]{1,0:T(8,128)} %x_ref.1) | copy-start | bytes 786436
  20.2 8.1 %collective-permute-start.8 = (bf16[256,256]{1,0:T(8,128)(2,1)S(1)}, bf16[256,256]{1,0:T(8,128)(2,1)S(1)}, u32[]{:S(2)}, u32[]{:S(2)}) collective-permute-start(bf16[256,256]{1,0:T(8,128)(2,1)S(1)} %get-tuple-element.42), channel_id=1, source_target_pairs={{2,0},{3,1},{4,2},{5,3},{6,4},{7,5},{0,6},{1,7},{14,8},{15,9},{8,1... | collective-permute-start | bytes 393224 | tf_op jit(solution)/shard_map/ppermute | solution.py:351
  24.4 2.1 %copy-start.2 = (f32[2]{0:T(128)S(1)}, f32[2]{0:T(128)}, u32[]{:S(2)}) copy-start(f32[2]{0:T(128)} %ridge_ref.1) | copy-start | bytes 28
  24.4 7.1 %collective-permute-start.2 = (bf16[2,256,256]{2,1,0:T(8,128)(2,1)S(1)}, bf16[2,256,256]{2,1,0:T(8,128)(2,1)S(1)}, u32[]{:S(2)}, u32[]{:S(2)}) collective-permute-start(bf16[2,256,256]{2,1,0:T(8,128)(2,1)S(1)} %get-tuple-element.34), channel_id=1, source_target_pairs={{1,0},{2,1},{3,2},{4,3},{5,4},{6,5},{7,6},{0,7},{9,8},{10,9},{11,1... | collective-permute-start | bytes 786440 | tf_op jit(solution)/shard_map/ppermute | solution.py:335
  24.4 7.7 %collective-permute-start.3 = (bf16[2,256,256]{2,1,0:T(8,128)(2,1)S(1)}, bf16[2,256,256]{2,1,0:T(8,128)(2,1)S(1)}, u32[]{:S(2)}, u32[]{:S(2)}) collective-permute-start(bf16[2,256,256]{2,1,0:T(8,128)(2,1)S(1)} %get-tuple-element.35), channel_id=1, source_target_pairs={{7,0},{0,1},{1,2},{2,3},{3,4},{4,5},{5,6},{6,7},{15,8},{8,9},{9,10... | collective-permute-start | bytes 786440 | tf_op jit(solution)/shard_map/ppermute | solution.py:335
  28.3 3.8 %collective-permute-start.9 = (f32[4,128,128]{2,1,0:T(8,128)S(1)}, f32[4,128,128]{2,1,0:T(8,128)S(1)}, u32[]{:S(2)}, u32[]{:S(2)}) collective-permute-start(f32[4,128,128]{2,1,0:T(8,128)S(1)} %get-tuple-element.47), channel_id=1, source_target_pairs={{8,0},{0,8},{24,16},{16,24},{40,32},{32,40},{56,48},{48,56},{72,64... | collective-permute-start | bytes 786440 | tf_op jit(solution)/shard_map/ppermute | solution.py:328
  37.7 1.6 %collective-permute-start.10 = (f32[4,128,128]{2,1,0:T(8,128)S(1)}, f32[4,128,128]{2,1,0:T(8,128)S(1)}, u32[]{:S(2)}, u32[]{:S(2)}) collective-permute-start(f32[4,128,128]{2,1,0:T(8,128)S(1)} %get-tuple-element.53.own_ref), channel_id=1, source_target_pairs={{8,0},{0,8},{24,16},{16,24},{40,32},{32,40},{56,48},{48,56},{72,64... | collective-permute-start | bytes 786440 | tf_op jit(solution)/shard_map/ppermute | solution.py:328
  39.3 8.3 %collective-permute-start.11 = (bf16[400,128]{1,0:T(8,128)(2,1)S(1)}, bf16[400,128]{1,0:T(8,128)(2,1)S(1)}, u32[]{:S(2)}, u32[]{:S(2)}) collective-permute-start(bf16[400,128]{1,0:T(8,128)(2,1)S(1)} %shard_map.91), channel_id=1, source_target_pairs={{16,0},{40,8},{32,16},{56,24},{48,32},{72,40},{64,48},{88,56},{80,... | collective-permute-start | bytes 307208 | tf_op jit(solution)/shard_map/ppermute | solution.py:328
  43.3 7.8 %collective-permute-start.12 = (bf16[400,128]{1,0:T(8,128)(2,1)S(1)}, bf16[400,128]{1,0:T(8,128)(2,1)S(1)}, u32[]{:S(2)}, u32[]{:S(2)}) collective-permute-start(bf16[400,128]{1,0:T(8,128)(2,1)S(1)} %shard_map.91), channel_id=1, source_target_pairs={{48,0},{64,16},{80,32},{96,48},{112,64},{128,80},{144,96},{160,112... | collective-permute-start | bytes 307208 | tf_op jit(solution)/shard_map/ppermute | solution.py:328
  45.7 9.1 %collective-permute-start.14 = (bf16[256,512]{1,0:T(8,128)(2,1)S(1)}, bf16[256,512]{1,0:T(8,128)(2,1)S(1)}, u32[]{:S(2)}, u32[]{:S(2)}) collective-permute-start(bf16[256,512]{1,0:T(8,128)(2,1)S(1)} %shard_map.93), channel_id=1, source_target_pairs={{64,0},{72,8},{80,16},{88,24},{96,32},{104,40},{112,48},{120,56},{... | collective-permute-start | bytes 786440 | tf_op jit(solution)/shard_map/ppermute | solution.py:328
  51.2 3.7 %collective-permute-start.13 = (f32[4,128,128]{2,1,0:T(8,128)S(1)}, f32[4,128,128]{2,1,0:T(8,128)S(1)}, u32[]{:S(2)}, u32[]{:S(2)}) collective-permute-start(f32[4,128,128]{2,1,0:T(8,128)S(1)} %get-tuple-element.57), channel_id=1, source_target_pairs={{8,0},{0,8},{24,16},{16,24},{40,32},{32,40},{56,48},{48,56},{72,64... | collective-permute-start | bytes 786440 | tf_op jit(solution)/shard_map/ppermute | solution.py:328
